TPU v7x, 256 devices: a whole 4x4x8 slice. The times are simulated.
256 devices in a mesh: row: 8 (over y, core), col: 32 (over z, x).
Axes of the slice: x: 4, y: 4, z: 8, core: 2. Of those that a mesh axis runs over, the one named last changes fastest.
Arguments:
- diag_inverse: float32 [2, 2048, 2048], P(None, 'row', 'col'), may hold values from -0.09375 to 0.09375
- panel_rhs: float32 [2, 2048, 128], P(None, 'col'), may hold values from -6 to 6
- factor_slab: bfloat16 [2, 131072, 2048], P(None, ('row', 'col')), may hold values from -0.09375 to 0.09375
- pending_rhs: float32 [2, 131072, 128], P(None, ('row', 'col')), may hold values from -6 to 6
- solved_prev: bfloat16 [2, 65536, 128], P(None, ('row', 'col')), may hold values from -6 to 6
- modes_prev: bfloat16 [65536, 128], P(('row', 'col')), may hold values from -0.0234375 to 0.0234375
- modes_panel: bfloat16 [2048, 128], P(('row', 'col')), may hold values from -0.0234375 to 0.0234375
Outputs:
- panel_solution: float32 [2, 2048, 128], P(None, ('row', 'col'))
- updated_rhs: float32 [2, 131072, 128], P(None, ('row', 'col'))
- modal_forces: float32 [2, 128, 128], replicated
All inputs are finite; a program needn't handle non-finite values.
Results may differ from a plain program's by a relative error of at most 0.002.
Values may be sent and summed in bfloat16 or wider, within the bound.
No kernel may reach another device: no remote copies, remote signals or barrier semaphores. Data moves between devices by JAX's collectives and lax.ppermute only.
A program may use at most 64 MiB of HBM per device.

v0:
```python
import jax
import jax.numpy as jnp
from jax import lax
from jax.sharding import PartitionSpec as P


def on_device(
    diag_inverse, panel_rhs, factor_slab, pending_rhs, solved_prev, modes_prev, modes_panel
):
    highest = lax.Precision.HIGHEST
    width = panel_rhs.shape[2]
    own_count = modes_panel.shape[0]
    straight = jnp.concatenate([panel_rhs[0], panel_rhs[1]], axis=1)
    crossed = jnp.concatenate([-panel_rhs[1], panel_rhs[0]], axis=1)
    earlier = jnp.einsum("sk,csm->ckm", modes_prev, solved_prev, preferred_element_type=jnp.float32)
    real_rows = diag_inverse[0]
    imag_rows = diag_inverse[1]
    block_sum = lax.psum(
        jnp.dot(real_rows, straight, precision=highest, preferred_element_type=jnp.float32)
        + jnp.dot(imag_rows, crossed, precision=highest, preferred_element_type=jnp.float32),
        "col",
    )
    offset = lax.axis_index("col") * own_count
    own_rows = lax.dynamic_slice_in_dim(block_sum, offset, own_count, 0)
    rounded_block = block_sum.astype(jnp.bfloat16)
    rounded_own = lax.dynamic_slice_in_dim(rounded_block, offset, own_count, 0)
    piece = lax.all_gather(rounded_block, "row", axis=0, tiled=True)
    real_cols = factor_slab[0]
    imag_cols = factor_slab[1]
    real_acc = jnp.dot(real_cols, piece, preferred_element_type=jnp.float32)
    imag_acc = jnp.dot(imag_cols, piece, preferred_element_type=jnp.float32)
    panel_solution = jnp.stack([own_rows[:, :width], own_rows[:, width:]])
    update_real = real_acc[:, :width] - imag_acc[:, width:]
    update_imag = real_acc[:, width:] + imag_acc[:, :width]
    updated_rhs = jnp.stack([pending_rhs[0] - update_real, pending_rhs[1] - update_imag])
    rounded_pair = jnp.stack([rounded_own[:, :width], rounded_own[:, width:]])
    latest = jnp.einsum(
        "sk,csm->ckm", modes_panel, rounded_pair, preferred_element_type=jnp.float32
    )
    modal_forces = lax.psum(earlier + latest, ("row", "col"))
    return (panel_solution, updated_rhs, modal_forces)


def solution(mesh):
    placed = (
        P(None, "row", "col"),
        P(None, "col", None),
        P(None, ("row", "col"), None),
        P(None, ("row", "col"), None),
        P(None, ("row", "col"), None),
        P(("row", "col"), None),
        P(("row", "col"), None),
    )
    return jax.shard_map(
        on_device,
        mesh=mesh,
        in_specs=placed,
        out_specs=(P(None, ("row", "col"), None), P(None, ("row", "col"), None), P()),
        check_vma=False,
    )
```

profile of v0, /device:TPU:1, one launch (start us, length us, event | category | flops | bytes accessed | tf_op | source)
XLA Modules:
  0.0 443.2 jit_solution(8867394615563559806)
XLA Ops:
  7.2 0.0 copy-start
  7.2 0.0 all-reduce.3.cloned.1.call-start
  7.2 0.8 fusion.38
  8.0 0.8 slice_bitcast_fusion.1
  8.8 1.3 fusion.18
  10.1 2.0 fusion.12
  12.0 0.0 all-reduce.3.cloned.1.call-update
  12.1 0.0 all-reduce.5.cloned.1.call-start
  12.1 0.0 copy-done
  12.1 1.1 fusion.25
  13.2 142.4 %all-reduce.3.cloned.1.call-done = f32[256,256]{0,1:T(8,128)} async-done(((f32[256,256]{0,1:T(8,128)}), f32[256,256]{0,1:T(8,128)}) %all-reduce.3.cloned.1.call-update) | async-done | bytes 262160 | tf_op jit(solution)/shard_map/psum | solution.py:18
  155.6 1.0 convert_element_type.3
  156.5 0.0 copy-start.1
  156.5 0.1 dynamic-slice_bitcast_fusion.3
  156.6 0.1 copy.22
  156.7 0.1 copy.23
  156.8 1.6 fusion.13
  158.4 0.0 all-reduce.5.cloned.1.call-update
  158.4 0.0 all-gather.2.cloned.1.call-start
  158.4 0.0 copy-done.1
  158.5 0.7 all-gather.2.cloned.1.call-update
  159.1 1.1 fusion.39
  160.2 0.1 copy.27
  160.3 0.1 copy.28
  160.5 1.0 dynamic-slice_bitcast_fusion.1
  161.5 0.1 copy.18
  161.6 0.6 pad_maximum_fusion.1
  162.2 241.6 %all-reduce.5.cloned.1.call-done = f32[2,128,128]{1,2,0:T(8,128)} async-done(((f32[2,128,128]{1,2,0:T(8,128)}), f32[2,128,128]{1,2,0:T(8,128)}) %all-reduce.5.cloned.1.call-update) | async-done | bytes 131088 | tf_op jit(solution)/shard_map/psum | solution.py:40
  403.8 1.7 copy.25
  405.5 24.7 %all-gather.2.cloned.1.call-done = bf16[2048,256]{0,1:T(8,128)(2,1)} async-done(((bf16[256,256]{0,1:T(8,128)(2,1)}), bf16[2048,256]{0,1:T(8,128)(2,1)}) %all-gather.2.cloned.1.call-update) | async-done | bytes 1048592 | tf_op jit(solution)/shard_map/all_gather | solution.py:27
  430.2 0.0 copy-start.2
  430.2 2.8 fusion.9
  433.0 0.3 copy-done.2
  433.4 2.1 fusion.6
  435.5 0.2 fusion.17
  435.7 1.0 copy.24
  (2 shorter events, 0.1 us)
Async XLA Ops:
  7.2 4.9 %copy-start = (bf16[2,256,128]{2,1,0:T(8,128)(2,1)S(1)}, bf16[2,256,128]{2,1,0:T(8,128)(2,1)}, u32[]{:S(2)}) copy-start(bf16[2,256,128]{2,1,0:T(8,128)(2,1)} %param.11) | copy-start | bytes 393220
  7.2 148.4 %all-reduce.3.cloned.1.call-start = ((), (), s32[]{:S(2)}) async-start(), calls=%async_computation | async-start | bytes 524288 | tf_op jit(solution)/shard_map/psum | solution.py:18
  12.1 391.8 %all-reduce.5.cloned.1.call-start = ((), (), s32[]{:S(2)}) async-start(), calls=%async_computation.2 | async-start | bytes 262144 | tf_op jit(solution)/shard_map/psum | solution.py:40
  156.5 1.9 copy-start.1
  158.4 271.8 %all-gather.2.cloned.1.call-start = ((), (), s32[]{:S(2)}) async-start(), calls=%async_computation.1 | async-start | bytes 1179648 | tf_op jit(solution)/shard_map/all_gather | solution.py:27
  430.2 3.1 copy-start.2
Sparse Core Ops, SparseCore 0:
  12.2 143.3 all-reduce.2
  161.6 242.1 all-reduce.4
  406.3 23.9 all-gather.1
where the time goes:
time: 444 us; the launch traced here: 443 us
  waiting for transfers between devices  409 us (92%)
  between operations  13.9 us (3%)
  matrix products  10.8 us (2%)
  local copies, waits for them, and re-layouts  6.43 us (1%)
    psum x1, waiting for transfers between devices, on_device(): modal_forces = lax.psum(earlier + latest, ('row', 'col'))  242 us
    psum x1, waiting for transfers between devices, on_device(): lax.psum(jnp.dot(real_rows, straight, precision=highest, preferred_elemen...  142 us
    all_gather x1, waiting for transfers between devices, on_device(): piece = lax.all_gather(rounded_block, 'row', axis=0, tiled=True)  24.7 us
  transfers between devices with their start and end apart: 3, of which 3 were waited for; matrix products, arithmetic and copies ran while one was open for 1% of the time, Pallas kernels for 0%

commit v1 on v0

v1 whole, which is shorter than its diff:
```python
import jax
import jax.numpy as jnp
from jax import lax
from jax.sharding import Mesh, PartitionSpec as P

F32 = jnp.float32
BF16 = jnp.bfloat16
COL = ("z", "x")
SWAP = [(0, 1), (1, 0)]


def flipped(value, bits):
    return lax.ppermute(value, "y", [(i, i ^ bits) for i in range(4)])


def on_device(
    diag_inverse, panel_rhs, factor_slab, pending_rhs, solved_prev, modes_prev, modes_panel
):
    width = panel_rhs.shape[2]
    own = modes_panel.shape[0]
    peers = diag_inverse.shape[1] // own
    core = lax.axis_index("core")
    y = lax.axis_index("y")
    left = jnp.concatenate([diag_inverse[0], diag_inverse[1]], axis=1)
    right = jnp.concatenate(
        [
            jnp.concatenate([panel_rhs[0], panel_rhs[1]], axis=1),
            jnp.concatenate([-panel_rhs[1], panel_rhs[0]], axis=1),
        ],
        axis=0,
    )
    partial = jnp.dot(left, right, precision=lax.Precision.HIGHEST, preferred_element_type=F32)
    earlier = jnp.einsum("sk,csm->ckm", modes_prev, solved_prev, preferred_element_type=F32)
    outgoing = jnp.concatenate(
        [
            partial[:, :width].reshape(peers, own, width),
            partial[:, width:].reshape(peers, own, width),
            earlier.reshape(peers, own, width),
        ],
        axis=1,
    )
    summed = jnp.sum(lax.all_to_all(outgoing, COL, 0, 0, tiled=True), axis=0)
    panel_solution = summed[: 2 * own].reshape(2, own, width)
    share = summed[2 * own :]
    high = lax.reduce_precision(share, 8, 7)
    low = share - high
    packed = jnp.concatenate(
        [summed[: 2 * own].astype(BF16), modes_panel, high.astype(BF16), low.astype(BF16)], axis=0
    )
    rows = packed.shape[0]
    gathered = lax.all_to_all(
        jnp.broadcast_to(packed[None], (peers, rows, width)), COL, 0, 0, tiled=True
    )
    block = (
        gathered[:, : 3 * own]
        .reshape(peers, 3, own, width)
        .transpose(1, 0, 2, 3)
        .reshape(3, peers * own, width)
    )
    share = gathered[:, 3 * own : 4 * own].astype(F32) + gathered[:, 4 * own :].astype(F32)
    share = share.reshape(2, width, width)
    mine = lax.dynamic_index_in_dim(share, core, 0, keepdims=False)
    other = lax.dynamic_index_in_dim(share, 1 - core, 0, keepdims=False)
    half = mine + lax.ppermute(other, "core", SWAP)
    blocks = jnp.stack([block] + [flipped(block, k) for k in (1, 2, 3)])
    half = (half + flipped(half, 2)) + (flipped(half, 1) + flipped(half, 3))
    ordered = jnp.stack(
        [lax.dynamic_index_in_dim(blocks, y ^ k, 0, keepdims=False) for k in range(4)]
    )
    solved = jnp.concatenate([ordered[:, 0], ordered[:, 1]], axis=2)
    theirs = lax.ppermute(solved, "core", SWAP)
    first = jnp.where(core == 0, solved, theirs)
    second = jnp.where(core == 0, theirs, solved)
    piece = jnp.stack([first, second], axis=1).reshape(-1, 2 * width)
    turned = jnp.concatenate([-piece[:, width:], piece[:, :width]], axis=1)
    update = jnp.dot(factor_slab[0], piece, preferred_element_type=F32) + jnp.dot(
        factor_slab[1], turned, preferred_element_type=F32
    )
    updated_rhs = jnp.stack(
        [pending_rhs[0] - update[:, :width], pending_rhs[1] - update[:, width:]]
    )
    latest = jnp.einsum(
        "ysk,cysm->ckm",
        ordered[:, 2],
        jnp.stack([ordered[:, 0], ordered[:, 1]]),
        preferred_element_type=F32,
    )
    both = jnp.stack([jnp.where(core == 0, half, 0.0), jnp.where(core == 1, half, 0.0)]) + latest
    modal_forces = both + lax.ppermute(both, "core", SWAP)
    return (panel_solution, updated_rhs, modal_forces)


def solution(mesh):
    fine = Mesh(mesh.devices.reshape(4, 2, 8, 4), ("y", "core", "z", "x"))
    row = ("y", "core")
    every = ("y", "core", "z", "x")
    placed = (
        P(None, row, COL),
        P(None, COL, None),
        P(None, every, None),
        P(None, every, None),
        P(None, every, None),
        P(every, None),
        P(every, None),
    )
    return jax.shard_map(
        on_device,
        mesh=fine,
        in_specs=placed,
        out_specs=(P(None, every, None), P(None, every, None), P()),
        check_vma=False,
    )
```

time: 444 us -> 81.3 us (0.18)
  waiting for transfers between devices: 409 us -> 23.1 us
  blocking collectives: 0 us -> 25.5 us
  starting transfers between devices: 0.12 us -> 18.6 us
  between operations: 13.9 us -> 0.97 us
  matrix products: 10.8 us -> 3.37 us
    psum x2 -> x0, waiting for transfers between devices: 384 us -> none  [the longest x1 242 us: on_device(): modal_forces = lax.psum(earlier + latest, ('row', 'col'))]
    all_to_all x0 -> x1, blocking collectives: none -> 25.5 us  [on_device(): summed = jnp.sum(lax.all_to_all(outgoing, COL, 0, 0, tiled=True), axis=0)]
    all_gather x1 -> x0, waiting for transfers between devices: 24.7 us -> none  [on_device(): piece = lax.all_gather(rounded_block, 'row', axis=0, tiled=True)]
    ppermute x0 -> x9, starting transfers between devices: none -> 13.6 us  [the longest x6 7.72 us: flipped(): return lax.ppermute(value, 'y', [(i, i ^ bits) for i in range(4)])]
    ppermute x0 -> x9, waiting for transfers between devices: none -> 11.9 us  [the longest x6 10.7 us: flipped(): return lax.ppermute(value, 'y', [(i, i ^ bits) for i in range(4)])]
    all_to_all x0 -> x1, waiting for transfers between devices: none -> 11.2 us  [on_device(): lax.all_to_all(jnp.broadcast_to(packed[None], (peers, rows, width)), COL,...]
    dot_general x5 -> x4, matrix products: 9.72 us -> 2.26 us  [the longest x1 0.76 us: on_device(): jnp.dot(factor_slab[1], turned, preferred_element_type=F32)]
    all_to_all x0 -> x1, starting transfers between devices: none -> 5 us  [on_device(): lax.all_to_all(jnp.broadcast_to(packed[None], (peers, rows, width)), COL,...]
  transfers between devices with their start and end apart: 3 -> 10, of which waited for: 3 -> 6; matrix products, arithmetic and copies ran while one was open for 1% -> 3% of each run, Pallas kernels for 0% -> 0%
where the time goes in v1:
time: 81.3 us; the launch traced here: 80.9 us
  blocking collectives  25.5 us (31%)
  waiting for transfers between devices  23.1 us (28%)
  starting transfers between devices  18.6 us (23%)
  local copies, waits for them, and re-layouts  7.7 us (9%)
  matrix products  3.37 us (4%)
  other arithmetic  1.73 us (2%)
  between operations  0.97 us (1%)
    all_to_all x1, blocking collectives, on_device(): summed = jnp.sum(lax.all_to_all(outgoing, COL, 0, 0, tiled=True), axis=0)  25.5 us
    all_to_all x1, waiting for transfers between devices, on_device(): lax.all_to_all(jnp.broadcast_to(packed[None], (peers, rows, width)), COL,...  11.2 us
    ppermute x6, waiting for transfers between devices, flipped(): return lax.ppermute(value, 'y', [(i, i ^ bits) for i in range(4)])  10.7 us
    ppermute x6, starting transfers between devices, flipped(): return lax.ppermute(value, 'y', [(i, i ^ bits) for i in range(4)])  7.72 us
    all_to_all x1, starting transfers between devices, on_device(): lax.all_to_all(jnp.broadcast_to(packed[None], (peers, rows, width)), COL,...  5 us
    ppermute x1, starting transfers between devices, on_device(): half = mine + lax.ppermute(other, 'core', SWAP)  4.1 us
    unnamed x12, local copies, waits for them, and re-layouts  4 us
    ppermute x1, starting transfers between devices, on_device(): theirs = lax.ppermute(solved, 'core', SWAP)  1.66 us
  transfers between devices with their start and end apart: 10, of which 6 were waited for; matrix products, arithmetic and copies ran while one was open for 3% of the time, Pallas kernels for 0%

profile of v1, /device:TPU:1, one launch (start us, length us, event | category | flops | bytes accessed | tf_op | source)
XLA Modules:
  0.0 80.9 jit_solution(10666666722660870026)
XLA Ops:
  0.6 0.0 copy-start
  0.6 0.0 copy-start.2
  0.7 0.8 %slice_bitcast_fusion.11 = (f32[64,128]{1,0:T(8,128)S(1)}, f32[64,128]{1,0:T(8,128)S(1)}) fusion(f32[2,64,128]{2,1,0:T(8,128)} %param.8), kind=kLoop, calls=%fused_computation.59 | loop fusion | bytes 131072 | tf_op jit(solution)/shard_map/squeeze | solution.py:27
  1.5 0.8 fusion.38
  2.2 0.9 %slice_bitcast_fusion.10 = (f32[256,64]{0,1:T(8,128)S(1)}, f32[256,64]{0,1:T(8,128)S(1)}) fusion(f32[2,256,64]{1,2,0:T(8,128)} %param.7), kind=kLoop, calls=%fused_computation.58 | loop fusion | bytes 262144 | tf_op jit(solution)/shard_map/squeeze | solution.py:24
  3.1 0.4 fusion.21
  3.6 0.0 copy-done
  3.6 0.0 copy-start.1
  3.6 1.1 %fusion.32 = f32[2,128,128]{1,2,0:T(8,128)S(1)} fusion(bf16[2,256,128]{2,1,0:T(8,128)(2,1)S(1)} %copy-done, bf16[256,128]{1,0:T(8,128)(2,1)} %param.12), kind=kOutput, calls=%fused_computation.52 | convolution fusion | flops 16777216 | bytes 327680 | tf_op jit(solution)/shard_map/sk,csm->ckm/dot_general | solution.py:33
  4.7 25.5 %all_to_all.10 = f32[32,24,128]{2,1,0:T(8,128)S(1)} all-to-all(f32[32,24,128]{2,1,0:T(8,128)S(1)} %pad_maximum_fusion.5), channel_id=1, replica_groups=mesh['y'=4,'core'=2,'z'=8,'x'=4] {'z','x'}, dimensions={0} | all-to-all | bytes 786432 | tf_op jit(solution)/shard_map/all_to_all | solution.py:42
  30.3 0.0 copy-done.2
  30.3 0.8 broadcast_in_dim.11
  31.1 5.0 %all-to-all-start.1 = ((bf16[32,40,128]{2,1,0:T(8,128)(2,1)}), bf16[32,40,128]{2,1,0:T(8,128)(2,1)S(1)}, u32[]{:S(2)}, u32[]{:S(2)}) async-start(bf16[32,40,128]{2,1,0:T(8,128)(2,1)} %broadcast_in_dim.11), calls=%async_computation.1 | async-start | bytes 655360 | tf_op jit(solution)/shard_map/all_to_all | solution.py:51
  36.1 11.2 %all-to-all-done.1 = bf16[32,40,128]{2,1,0:T(8,128)(2,1)S(1)} async-done(((bf16[32,40,128]{2,1,0:T(8,128)(2,1)}), bf16[32,40,128]{2,1,0:T(8,128)(2,1)S(1)}, u32[]{:S(2)}, u32[]{:S(2)}) %all-to-all-start.1) | async-done | bytes 327712 | tf_op jit(solution)/shard_map/all_to_all | solution.py:51
  47.4 0.1 copy.27
  47.5 4.1 %collective-permute-start.4 = (f32[128,128]{0,1:T(8,128)S(1)}, f32[128,128]{0,1:T(8,128)S(1)}, u32[]{:S(2)}, u32[]{:S(2)}) collective-permute-start(f32[128,128]{0,1:T(8,128)S(1)} %bitcast.99), channel_id=1, source_target_pairs={{0,32},{32,0},{1,33},{33,1},{2,34},{34,2},{3,35},{35,3},{4,36},{36... | collective-permute-start | bytes 196616 | tf_op jit(solution)/shard_map/ppermute | solution.py:64
  51.6 0.0 copy-done.1
  51.6 0.1 copy.35
  51.8 0.1 copy.36
  51.9 0.1 copy.26
  52.0 0.5 collective-permute-done.4
  52.5 3.0 %collective-permute-start.5 = (f32[128,128]{0,1:T(8,128)S(1)}, f32[128,128]{0,1:T(8,128)S(1)}, u32[]{:S(2)}, u32[]{:S(2)}) collective-permute-start(f32[128,128]{0,1:T(8,128)S(1)} %bitcast_add_fusion), channel_id=1, source_target_pairs={{0,128},{64,192},{128,0},{192,64},{1,129},{65,193},{129,1},{193,65... | collective-permute-start | bytes 196616 | tf_op jit(solution)/shard_map/ppermute | solution.py:13
  55.5 0.4 collective-permute-start.6
  55.9 0.4 collective-permute-start.7
  56.2 0.1 copy_bitcast_fusion.1
  56.3 0.9 %collective-permute-start = (bf16[3,256,128]{2,1,0:T(8,128)(2,1)S(1)}, bf16[3,256,128]{2,1,0:T(8,128)(2,1)S(1)}, u32[]{:S(2)}, u32[]{:S(2)}) collective-permute-start(bf16[3,256,128]{2,1,0:T(8,128)(2,1)S(1)} %get-tuple-element.30), channel_id=1, source_target_pairs={{0,64},{64,0},{128,192},{192,128},{1,65},{65,1},{129,193},{193,129... | collective-permute-start | bytes 589832 | tf_op jit(solution)/shard_map/ppermute | solution.py:13
  57.2 2.6 %collective-permute-start.1 = (bf16[3,256,128]{2,1,0:T(8,128)(2,1)S(1)}, bf16[3,256,128]{2,1,0:T(8,128)(2,1)S(1)}, u32[]{:S(2)}, u32[]{:S(2)}) collective-permute-start(bf16[3,256,128]{2,1,0:T(8,128)(2,1)S(1)} %get-tuple-element.30), channel_id=1, source_target_pairs={{0,128},{64,192},{128,0},{192,64},{1,129},{65,193},{129,1},{193,65... | collective-permute-start | bytes 589832 | tf_op jit(solution)/shard_map/ppermute | solution.py:13
  59.9 0.0 collective-permute-done.5
  59.9 0.4 collective-permute-start.2
  60.3 0.0 collective-permute-done.6
  60.3 0.0 collective-permute-done.7
  60.3 3.3 %collective-permute-done = bf16[3,256,128]{2,1,0:T(8,128)(2,1)S(1)} collective-permute-done((bf16[3,256,128]{2,1,0:T(8,128)(2,1)S(1)}, bf16[3,256,128]{2,1,0:T(8,128)(2,1)S(1)}, u32[]{:S(2)}, u32[]{:S(2)}) %collective-permute-start) | collective-permute-done | bytes 196640 | tf_op jit(solution)/shard_map/ppermute | solution.py:13
  63.6 4.2 %collective-permute-done.1 = bf16[3,256,128]{2,1,0:T(8,128)(2,1)S(1)} collective-permute-done((bf16[3,256,128]{2,1,0:T(8,128)(2,1)S(1)}, bf16[3,256,128]{2,1,0:T(8,128)(2,1)S(1)}, u32[]{:S(2)}, u32[]{:S(2)}) %collective-permute-start.1) | collective-permute-done | bytes 196640 | tf_op jit(solution)/shard_map/ppermute | solution.py:13
  67.8 3.1 %collective-permute-done.2 = bf16[3,256,128]{2,1,0:T(8,128)(2,1)S(1)} collective-permute-done((bf16[3,256,128]{2,1,0:T(8,128)(2,1)S(1)}, bf16[3,256,128]{2,1,0:T(8,128)(2,1)S(1)}, u32[]{:S(2)}, u32[]{:S(2)}) %collective-permute-start.2) | collective-permute-done | bytes 196640 | tf_op jit(solution)/shard_map/ppermute | solution.py:13
  70.9 0.1 pad_maximum_fusion.1
  71.1 0.1 constant_dynamic-slice_fusion.5
  71.1 0.1 pad_maximum_fusion.2
  71.2 0.2 slice_bitcast_fusion.4
  71.4 0.1 pad_maximum_fusion.3
  71.5 1.7 %collective-permute-start.3 = (bf16[4,256,256]{2,1,0:T(8,128)(2,1)S(1)}, bf16[4,256,256]{2,1,0:T(8,128)(2,1)S(1)}, u32[]{:S(2)}, u32[]{:S(2)}) collective-permute-start(bf16[4,256,256]{2,1,0:T(8,128)(2,1)S(1)} %pad_maximum_fusion.3), channel_id=1, source_target_pairs={{0,32},{32,0},{1,33},{33,1},{2,34},{34,2},{3,35},{35,3},{4,36},{36... | collective-permute-start | bytes 1572872 | tf_op jit(solution)/shard_map/ppermute | solution.py:71
  73.2 0.3 fusion.12
  73.5 0.1 collective-permute-start.8
  73.6 0.6 slice_bitcast_fusion.13
  74.2 0.7 collective-permute-done.8
  75.0 0.8 copy.30
  75.7 0.0 collective-permute-done.3
  75.7 0.2 select_bitcast_fusion.1
  76.0 0.1 pad_maximum_fusion
  76.1 0.0 copy-start.3
  76.1 0.1 copy.24
  76.1 0.1 slice_negate_fusion
  76.3 2.0 %copy-done.3 = bf16[2,512,2048]{2,1,0:T(8,128)(2,1)S(1)} copy-done((bf16[2,512,2048]{2,1,0:T(8,128)(2,1)S(1)}, bf16[2,512,2048]{2,1,0:T(8,128)(2,1)}, u32[]{:S(2)}) %copy-start.3) | copy-done | bytes 4194328
  78.2 0.8 fusion
  79.0 0.8 fusion.9
  79.8 0.1 fusion.20
  79.9 1.0 %copy.29 = f32[2,512,128]{2,1,0:T(8,128)} copy(f32[2,512,128]{1,2,0:T(8,128)S(1)} %pad_maximum_fusion.4) | data formatting | bytes 1048576
  (14 shorter events, 0.3 us)
Async XLA Ops:
  0.6 2.9 %copy-start = (bf16[2,256,128]{2,1,0:T(8,128)(2,1)S(1)}, bf16[2,256,128]{2,1,0:T(8,128)(2,1)}, u32[]{:S(2)}) copy-start(bf16[2,256,128]{2,1,0:T(8,128)(2,1)} %param.11) | copy-start | bytes 393220
  0.6 29.6 %copy-start.2 = (bf16[8,128]{1,0:T(8,128)(2,1)S(1)}, bf16[8,128]{1,0:T(8,128)(2,1)}, u32[]{:S(2)}) copy-start(bf16[8,128]{1,0:T(8,128)(2,1)} %param.13) | copy-start | bytes 6148
  3.6 48.0 %copy-start.1 = (f32[2,512,128]{2,1,0:T(8,128)S(1)}, f32[2,512,128]{2,1,0:T(8,128)}, u32[]{:S(2)}) copy-start(f32[2,512,128]{2,1,0:T(8,128)} %param.10) | copy-start | bytes 1572868
  31.1 16.2 %all-to-all-start.1 = ((bf16[32,40,128]{2,1,0:T(8,128)(2,1)}), bf16[32,40,128]{2,1,0:T(8,128)(2,1)S(1)}, u32[]{:S(2)}, u32[]{:S(2)}) async-start(bf16[32,40,128]{2,1,0:T(8,128)(2,1)} %broadcast_in_dim.11), calls=%async_computation.1 | async-start | bytes 655360 | tf_op jit(solution)/shard_map/all_to_all | solution.py:51
  47.5 5.0 %collective-permute-start.4 = (f32[128,128]{0,1:T(8,128)S(1)}, f32[128,128]{0,1:T(8,128)S(1)}, u32[]{:S(2)}, u32[]{:S(2)}) collective-permute-start(f32[128,128]{0,1:T(8,128)S(1)} %bitcast.99), channel_id=1, source_target_pairs={{0,32},{32,0},{1,33},{33,1},{2,34},{34,2},{3,35},{35,3},{4,36},{36... | collective-permute-start | bytes 196616 | tf_op jit(solution)/shard_map/ppermute | solution.py:64
  52.5 7.4 %collective-permute-start.5 = (f32[128,128]{0,1:T(8,128)S(1)}, f32[128,128]{0,1:T(8,128)S(1)}, u32[]{:S(2)}, u32[]{:S(2)}) collective-permute-start(f32[128,128]{0,1:T(8,128)S(1)} %bitcast_add_fusion), channel_id=1, source_target_pairs={{0,128},{64,192},{128,0},{192,64},{1,129},{65,193},{129,1},{193,65... | collective-permute-start | bytes 196616 | tf_op jit(solution)/shard_map/ppermute | solution.py:13
  55.5 4.8 %collective-permute-start.6 = (f32[128,128]{0,1:T(8,128)S(1)}, f32[128,128]{0,1:T(8,128)S(1)}, u32[]{:S(2)}, u32[]{:S(2)}) collective-permute-start(f32[128,128]{0,1:T(8,128)S(1)} %bitcast_add_fusion), channel_id=1, source_target_pairs={{0,64},{64,0},{128,192},{192,128},{1,65},{65,1},{129,193},{193,129... | collective-permute-start | bytes 196616 | tf_op jit(solution)/shard_map/ppermute | solution.py:13
  55.9 4.4 %collective-permute-start.7 = (f32[128,128]{0,1:T(8,128)S(1)}, f32[128,128]{0,1:T(8,128)S(1)}, u32[]{:S(2)}, u32[]{:S(2)}) collective-permute-start(f32[128,128]{0,1:T(8,128)S(1)} %bitcast_add_fusion), channel_id=1, source_target_pairs={{0,192},{64,128},{128,64},{192,0},{1,193},{65,129},{129,65},{193,1... | collective-permute-start | bytes 196616 | tf_op jit(solution)/shard_map/ppermute | solution.py:13
  56.3 7.3 %collective-permute-start = (bf16[3,256,128]{2,1,0:T(8,128)(2,1)S(1)}, bf16[3,256,128]{2,1,0:T(8,128)(2,1)S(1)}, u32[]{:S(2)}, u32[]{:S(2)}) collective-permute-start(bf16[3,256,128]{2,1,0:T(8,128)(2,1)S(1)} %get-tuple-element.30), channel_id=1, source_target_pairs={{0,64},{64,0},{128,192},{192,128},{1,65},{65,1},{129,193},{193,129... | collective-permute-start | bytes 589832 | tf_op jit(solution)/shard_map/ppermute | solution.py:13
  57.2 10.6 %collective-permute-start.1 = (bf16[3,256,128]{2,1,0:T(8,128)(2,1)S(1)}, bf16[3,256,128]{2,1,0:T(8,128)(2,1)S(1)}, u32[]{:S(2)}, u32[]{:S(2)}) collective-permute-start(bf16[3,256,128]{2,1,0:T(8,128)(2,1)S(1)} %get-tuple-element.30), channel_id=1, source_target_pairs={{0,128},{64,192},{128,0},{192,64},{1,129},{65,193},{129,1},{193,65... | collective-permute-start | bytes 589832 | tf_op jit(solution)/shard_map/ppermute | solution.py:13
  59.9 11.1 %collective-permute-start.2 = (bf16[3,256,128]{2,1,0:T(8,128)(2,1)S(1)}, bf16[3,256,128]{2,1,0:T(8,128)(2,1)S(1)}, u32[]{:S(2)}, u32[]{:S(2)}) collective-permute-start(bf16[3,256,128]{2,1,0:T(8,128)(2,1)S(1)} %get-tuple-element.30), channel_id=1, source_target_pairs={{0,192},{64,128},{128,64},{192,0},{1,193},{65,129},{129,65},{193,1... | collective-permute-start | bytes 589832 | tf_op jit(solution)/shard_map/ppermute | solution.py:13
  71.5 4.2 %collective-permute-start.3 = (bf16[4,256,256]{2,1,0:T(8,128)(2,1)S(1)}, bf16[4,256,256]{2,1,0:T(8,128)(2,1)S(1)}, u32[]{:S(2)}, u32[]{:S(2)}) collective-permute-start(bf16[4,256,256]{2,1,0:T(8,128)(2,1)S(1)} %pad_maximum_fusion.3), channel_id=1, source_target_pairs={{0,32},{32,0},{1,33},{33,1},{2,34},{34,2},{3,35},{35,3},{4,36},{36... | collective-permute-start | bytes 1572872 | tf_op jit(solution)/shard_map/ppermute | solution.py:71
  73.5 1.4 %collective-permute-start.8 = (f32[2,128,128]{1,2,0:T(8,128)S(1)}, f32[2,128,128]{1,2,0:T(8,128)S(1)}, u32[]{:S(2)}, u32[]{:S(2)}) collective-permute-start(f32[2,128,128]{1,2,0:T(8,128)S(1)} %fusion.12), channel_id=1, source_target_pairs={{0,32},{32,0},{1,33},{33,1},{2,34},{34,2},{3,35},{35,3},{4,36},{36... | collective-permute-start | bytes 393224 | tf_op jit(solution)/shard_map/ppermute | solution.py:89
  76.1 2.2 %copy-start.3 = (bf16[2,512,2048]{2,1,0:T(8,128)(2,1)S(1)}, bf16[2,512,2048]{2,1,0:T(8,128)(2,1)}, u32[]{:S(2)}) copy-start(bf16[2,512,2048]{2,1,0:T(8,128)(2,1)} %param.9) | copy-start | bytes 12582916

commit v2 on v1

v2 whole, which is shorter than its diff:
```python
import functools

import jax
import jax.numpy as jnp
from jax import lax
from jax.experimental import pallas as pl
from jax.experimental.pallas import tpu as pltpu
from jax.sharding import Mesh, PartitionSpec as P

F32 = jnp.float32
BF16 = jnp.bfloat16
COL = ("z", "x")
SWAP = [(0, 1), (1, 0)]
CHUNK = 128
TURNS = (0, 1, 3, 2)


def swapped(value):
    return lax.ppermute(value, "core", SWAP)


def flipped(value, bits):
    return lax.ppermute(value, "y", [(i, i ^ bits) for i in range(4)])


def first_kernel(diag_hbm, rhs_hbm, modes_hbm, solved_hbm, out_ref, diag_ref, rhs_ref, modes_ref, solved_ref, sems):
    peers, rows, width = out_ref.shape
    own = rows // 3
    moves = [
        pltpu.make_async_copy(source, target, sems.at[i])
        for i, (source, target) in enumerate(
            (
                (modes_hbm, modes_ref),
                (solved_hbm, solved_ref),
                (rhs_hbm, rhs_ref),
                (diag_hbm, diag_ref),
            )
        )
    ]
    for move in moves:
        move.start()
    over_first = (((0,), (0,)), ((), ()))
    half = peers // 2
    moves[0].wait()
    moves[1].wait()
    for c in range(2):
        earlier = lax.dot_general(
            modes_ref[...], solved_ref[c], over_first, preferred_element_type=F32
        )
        out_ref[c * half : (c + 1) * half, 2 * own :, :] = earlier.reshape(half, own, width)
    moves[2].wait()
    moves[3].wait()
    left = jnp.concatenate([diag_ref[0], diag_ref[1]], axis=0)
    real, imag = rhs_ref[0], rhs_ref[1]
    right = jnp.concatenate(
        [jnp.concatenate([real, imag], axis=1), jnp.concatenate([-imag, real], axis=1)], axis=0
    )
    partial = lax.dot_general(
        left, right, over_first, precision=lax.Precision.HIGHEST, preferred_element_type=F32
    )
    out_ref[:, :own, :] = partial[:, :width].reshape(peers, own, width)
    out_ref[:, own : 2 * own, :] = partial[:, width:].reshape(peers, own, width)


def first_partials(diag_inverse, panel_rhs, modes_prev, solved_prev, peers, own):
    width = panel_rhs.shape[2]
    args = (jnp.swapaxes(diag_inverse, 1, 2), panel_rhs, modes_prev, solved_prev)
    return pl.pallas_call(
        first_kernel,
        out_shape=jax.ShapeDtypeStruct((peers, 3 * own, width), F32),
        in_specs=[pl.BlockSpec(memory_space=pltpu.HBM)] * 4,
        out_specs=pl.BlockSpec(memory_space=pltpu.VMEM),
        scratch_shapes=[pltpu.VMEM(a.shape, a.dtype) for a in args]
        + [pltpu.SemaphoreType.DMA((4,))],
        name="partials",
    )(*args)


def update_kernel(turns, factor_ref, rhs_ref, *rest):
    out_ref = rest[-1]
    depth = rest[0].shape[0]
    rows = factor_ref.shape[1]
    width = out_ref.shape[2]
    y = lax.axis_index("y")
    core = lax.axis_index("core")
    for j, block_ref in enumerate(rest[:-1]):
        place = jnp.bitwise_xor(y, turns[j // 2]) * 2 + jnp.bitwise_xor(core, j % 2)
        columns = pl.ds(pl.multiple_of(place * depth, depth), depth)
        straight = block_ref[...]
        crossed = jnp.concatenate([-straight[:, width:], straight[:, :width]], axis=1)
        base = rhs_ref if j == 0 else out_ref
        for at in range(0, rows, CHUNK):
            span = slice(at, at + CHUNK)
            product = jnp.dot(factor_ref[0, span, columns], straight, preferred_element_type=F32)
            product += jnp.dot(factor_ref[1, span, columns], crossed, preferred_element_type=F32)
            out_ref[0, span, :] = base[0, span, :] - product[:, :width]
            out_ref[1, span, :] = base[1, span, :] - product[:, width:]


def update(turns, factor_slab, rhs, blocks, name):
    depth = blocks[0].shape[0]
    rows = factor_slab.shape[1]
    vmem = pl.BlockSpec(memory_space=pltpu.VMEM)
    return pl.pallas_call(
        functools.partial(update_kernel, turns),
        out_shape=jax.ShapeDtypeStruct(rhs.shape, F32),
        in_specs=[vmem] * (2 + len(blocks)),
        out_specs=vmem,
        cost_estimate=pl.CostEstimate(
            flops=len(blocks) * 4 * rows * depth * 2 * rhs.shape[2],
            bytes_accessed=len(blocks) * 4 * rows * depth,
            transcendentals=0,
        ),
        compiler_params=pltpu.CompilerParams(vmem_limit_bytes=24 << 20),
        name=name,
    )(factor_slab, rhs, *blocks)


def on_device(
    diag_inverse, panel_rhs, factor_slab, pending_rhs, solved_prev, modes_prev, modes_panel
):
    width = panel_rhs.shape[2]
    own = modes_panel.shape[0]
    peers = diag_inverse.shape[1] // own
    core = lax.axis_index("core")
    outgoing = first_partials(diag_inverse, panel_rhs, modes_prev, solved_prev, peers, own)
    summed = jnp.sum(lax.all_to_all(outgoing, COL, 0, 0, tiled=True), axis=0)
    panel_solution = summed[: 2 * own].reshape(2, own, width)
    share = summed[2 * own :]
    high = lax.reduce_precision(share, 8, 7)
    low = share - high
    packed = jnp.concatenate(
        [summed[: 2 * own].astype(BF16), modes_panel, high.astype(BF16), low.astype(BF16)], axis=0
    )
    rows = packed.shape[0]
    gathered = lax.all_to_all(
        jnp.broadcast_to(packed[None], (peers, rows, width)), COL, 0, 0, tiled=True
    )
    block = jnp.concatenate(
        [
            gathered[:, :own].reshape(peers * own, width),
            gathered[:, own : 2 * own].reshape(peers * own, width),
        ],
        axis=1,
    )
    beside = {k: flipped(block, k) for k in TURNS[1:]}
    twin = swapped(block)
    modes_block = gathered[:, 2 * own : 3 * own].reshape(peers * own, width)
    share = gathered[:, 3 * own : 4 * own].astype(F32) + gathered[:, 4 * own :].astype(F32)
    latest = lax.dot_general(
        modes_block, block, (((0,), (0,)), ((), ())), preferred_element_type=F32
    )
    share = share.reshape(2, width, width) + jnp.stack([latest[:, :width], latest[:, width:]])
    mine = lax.dynamic_index_in_dim(share, core, 0, keepdims=False)
    other = lax.dynamic_index_in_dim(share, 1 - core, 0, keepdims=False)
    half = mine + swapped(other)
    half, beside[1] = lax.optimization_barrier((half, beside[1]))
    half = (half + flipped(half, 2)) + (flipped(half, 1) + flipped(half, 3))
    back = swapped(half)
    started = update(TURNS[:1], factor_slab, pending_rhs, [block, twin], "update_own")
    twins = {k: swapped(beside[k]) for k in TURNS[1:]}
    updated_rhs = update(
        TURNS[1:],
        factor_slab,
        started,
        [b for k in TURNS[1:] for b in (beside[k], twins[k])],
        "update_rest",
    )
    modal_forces = jnp.stack(
        [jnp.where(core == 0, half, back), jnp.where(core == 0, back, half)]
    )
    return (panel_solution, updated_rhs, modal_forces)


def solution(mesh):
    fine = Mesh(mesh.devices.reshape(4, 2, 8, 4), ("y", "core", "z", "x"))
    row = ("y", "core")
    every = ("y", "core", "z", "x")
    placed = (
        P(None, row, COL),
        P(None, COL, None),
        P(None, every, None),
        P(None, every, None),
        P(None, every, None),
        P(every, None),
        P(every, None),
    )
    return jax.shard_map(
        on_device,
        mesh=fine,
        in_specs=placed,
        out_specs=(P(None, every, None), P(None, every, None), P()),
        check_vma=False,
    )
```

time: 81.3 us -> 77.6 us (0.954)
  Pallas kernels: 0 us -> 4.69 us
  local copies, waits for them, and re-layouts: 7.7 us -> 3.6 us
  waiting for transfers between devices: 23.1 us -> 19.3 us
  matrix products: 3.37 us -> 0.19 us
  starting transfers between devices: 18.6 us -> 21.5 us
    pallas_call x0 -> x3, Pallas kernels: none -> 4.69 us  [the longest x1 2.42 us: first_partials(): pl.pallas_call(first_kernel, out_shape=jax.ShapeDtypeStruct((peers, 3 * o...]
    dot_general x5 -> x1, matrix products: 3.37 us -> 0.19 us  [on_device(): lax.dot_general(modes_block, block, (((0,), (0,)), ((), ())), preferred_e...]
    ppermute x3 -> x6, starting transfers between devices: 5.86 us -> 8.53 us  [swapped(): return lax.ppermute(value, 'core', SWAP)]
    ppermute x6, waiting for transfers between devices: 10.7 us -> 8.05 us  [flipped(): return lax.ppermute(value, 'y', [(i, i ^ bits) for i in range(4)])]
    unnamed x12 -> x4, local copies, waits for them, and re-layouts: 4 us -> 2.19 us
    squeeze x2 -> x1, local copies, waits for them, and re-layouts: 1.7 us -> 0.01 us  [on_device(): other = lax.dynamic_index_in_dim(share, 1 - core, 0, keepdims=False)]
    ppermute x3 -> x6, waiting for transfers between devices: 1.18 us -> 0.02 us  [swapped(): return lax.ppermute(value, 'core', SWAP)]
    neg x2 -> x0, other arithmetic: 0.89 us -> none  [the longest x1 0.76 us: on_device(): -panel_rhs[1]]
  transfers between devices with their start and end apart: 10 -> 13, of which waited for: 6 -> 3; matrix products, arithmetic and copies ran while one was open for 3% -> 2% of each run, Pallas kernels for 0% -> 1%
where the time goes in v2:
time: 77.6 us; the launch traced here: 77.2 us
  blocking collectives  25.7 us (33%)
  starting transfers between devices  21.5 us (28%)
  waiting for transfers between devices  19.3 us (25%)
  Pallas kernels  4.69 us (6%)
  local copies, waits for them, and re-layouts  3.6 us (5%)
  other arithmetic  1.49 us (2%)
  between operations  0.78 us (1%)
    all_to_all x1, blocking collectives, on_device(): summed = jnp.sum(lax.all_to_all(outgoing, COL, 0, 0, tiled=True), axis=0)  25.7 us
    all_to_all x1, waiting for transfers between devices, on_device(): lax.all_to_all(jnp.broadcast_to(packed[None], (peers, rows, width)), COL,...  11.2 us
    ppermute x6, starting transfers between devices, swapped(): return lax.ppermute(value, 'core', SWAP)  8.53 us
    ppermute x6, waiting for transfers between devices, flipped(): return lax.ppermute(value, 'y', [(i, i ^ bits) for i in range(4)])  8.05 us
    ppermute x6, starting transfers between devices, flipped(): return lax.ppermute(value, 'y', [(i, i ^ bits) for i in range(4)])  7.99 us
    all_to_all x1, starting transfers between devices, on_device(): lax.all_to_all(jnp.broadcast_to(packed[None], (peers, rows, width)), COL,...  5 us
    pallas_call x1, Pallas kernels, first_partials(): pl.pallas_call(first_kernel, out_shape=jax.ShapeDtypeStruct((peers, 3 * o...  2.42 us
    pallas_call x2, Pallas kernels, update(): pl.pallas_call(functools.partial(update_kernel, turns), out_shape=jax.Sha...  2.27 us
  transfers between devices with their start and end apart: 13, of which 3 were waited for; matrix products, arithmetic and copies ran while one was open for 2% of the time, Pallas kernels for 1%

profile of v2, /device:TPU:1, one launch (start us, length us, event | category | flops | bytes accessed | tf_op | source)
XLA Modules:
  0.0 77.2 jit_solution(8805099042147401011)
XLA Ops:
  0.6 0.0 copy-start.1
  0.6 2.4 %partials.1 = f32[32,24,128]{2,1,0:T(8,128)} custom-call(f32[2,64,256]{2,1,0:T(8,128)} %bitcast.26, f32[2,64,128]{2,1,0:T(8,128)} %rhs_hbm.1, bf16[256,128]{1,0:T(8,128)(2,1)} %modes_hbm.1, bf16[2,256,128]{2,1,0:T(8,128)(2,1)} %solved_hbm.1), custom_call_target="tpu_custom_call" | custom-call | tf_op jit(solution)/shard_map/partials/pallas_call | solution.py:68
  3.1 25.7 %all_to_all.10 = f32[32,24,128]{2,1,0:T(8,128)S(1)} all-to-all(f32[32,24,128]{2,1,0:T(8,128)} %partials.1), channel_id=1, replica_groups=mesh['y'=4,'core'=2,'z'=8,'x'=4] {'z','x'}, dimensions={0} | all-to-all | bytes 786432 | tf_op jit(solution)/shard_map/all_to_all | solution.py:127
  28.8 0.7 pad_maximum_fusion.2
  29.5 0.8 broadcast_in_dim.2
  30.3 5.0 %all-to-all-start.1 = ((bf16[32,40,128]{2,1,0:T(8,128)(2,1)}), bf16[32,40,128]{2,1,0:T(8,128)(2,1)S(1)}, u32[]{:S(2)}, u32[]{:S(2)}) async-start(bf16[32,40,128]{2,1,0:T(8,128)(2,1)} %broadcast_in_dim.2), calls=%async_computation.1 | async-start | bytes 655360 | tf_op jit(solution)/shard_map/all_to_all | solution.py:136
  35.3 11.2 %all-to-all-done.1 = bf16[32,40,128]{2,1,0:T(8,128)(2,1)S(1)} async-done(((bf16[32,40,128]{2,1,0:T(8,128)(2,1)}), bf16[32,40,128]{2,1,0:T(8,128)(2,1)S(1)}, u32[]{:S(2)}, u32[]{:S(2)}) %all-to-all-start.1) | async-done | bytes 327712 | tf_op jit(solution)/shard_map/all_to_all | solution.py:136
  46.5 0.2 fusion
  46.8 4.1 %collective-permute-start.1 = (f32[128,128]{1,0:T(8,128)S(1)}, f32[128,128]{1,0:T(8,128)S(1)}, u32[]{:S(2)}, u32[]{:S(2)}) collective-permute-start(f32[128,128]{1,0:T(8,128)S(1)} %dynamic-slice_bitcast_fusion), channel_id=1, source_target_pairs={{0,32},{32,0},{1,33},{33,1},{2,34},{34,2},{3,35},{35,3},{4,36},{36... | collective-permute-start | bytes 196616 | tf_op jit(solution)/shard_map/ppermute | solution.py:19
  50.9 1.4 %collective-permute-start.2 = (bf16[256,256]{1,0:T(8,128)(2,1)S(1)}, bf16[256,256]{1,0:T(8,128)(2,1)S(1)}, u32[]{:S(2)}, u32[]{:S(2)}) collective-permute-start(bf16[256,256]{1,0:T(8,128)(2,1)S(1)} %pad_maximum_fusion.rest_0_), channel_id=1, source_target_pairs={{0,64},{64,0},{128,192},{192,128},{1,65},{65,1},{129,193},{193,129... | collective-permute-start | bytes 393224 | tf_op jit(solution)/shard_map/ppermute | solution.py:23
  52.3 0.0 collective-permute-done.1
  52.3 3.8 %collective-permute-done.2.rest_0_ = bf16[256,256]{1,0:T(8,128)(2,1)S(1)} collective-permute-done((bf16[256,256]{1,0:T(8,128)(2,1)S(1)}, bf16[256,256]{1,0:T(8,128)(2,1)S(1)}, u32[]{:S(2)}, u32[]{:S(2)}) %collective-permute-start.2) | collective-permute-done | bytes 131104 | tf_op jit(solution)/shard_map/ppermute | solution.py:23
  56.1 1.3 %collective-permute-start.9 = (f32[128,128]{1,0:T(8,128)S(1)}, f32[128,128]{1,0:T(8,128)S(1)}, u32[]{:S(2)}, u32[]{:S(2)}) collective-permute-start(f32[128,128]{1,0:T(8,128)S(1)} %bitcast_add_fusion), channel_id=1, source_target_pairs={{0,64},{64,0},{128,192},{192,128},{1,65},{65,1},{129,193},{193,129... | collective-permute-start | bytes 196616 | tf_op jit(solution)/shard_map/ppermute | solution.py:23
  57.4 1.9 %collective-permute-start.10 = (f32[128,128]{1,0:T(8,128)S(1)}, f32[128,128]{1,0:T(8,128)S(1)}, u32[]{:S(2)}, u32[]{:S(2)}) collective-permute-start(f32[128,128]{1,0:T(8,128)S(1)} %bitcast_add_fusion), channel_id=1, source_target_pairs={{0,192},{64,128},{128,64},{192,0},{1,193},{65,129},{129,65},{193,1... | collective-permute-start | bytes 196616 | tf_op jit(solution)/shard_map/ppermute | solution.py:23
  59.3 0.7 collective-permute-start.8
  60.0 1.4 %collective-permute-start = (bf16[256,256]{1,0:T(8,128)(2,1)S(1)}, bf16[256,256]{1,0:T(8,128)(2,1)S(1)}, u32[]{:S(2)}, u32[]{:S(2)}) collective-permute-start(bf16[256,256]{1,0:T(8,128)(2,1)S(1)} %pad_maximum_fusion.rest_0_), channel_id=1, source_target_pairs={{0,32},{32,0},{1,33},{33,1},{2,34},{34,2},{3,35},{35,3},{4,36},{36... | collective-permute-start | bytes 393224 | tf_op jit(solution)/shard_map/ppermute | solution.py:19
  61.4 2.3 %collective-permute-start.4 = (bf16[256,256]{1,0:T(8,128)(2,1)S(1)}, bf16[256,256]{1,0:T(8,128)(2,1)S(1)}, u32[]{:S(2)}, u32[]{:S(2)}) collective-permute-start(bf16[256,256]{1,0:T(8,128)(2,1)S(1)} %pad_maximum_fusion.rest_0_), channel_id=1, source_target_pairs={{0,192},{64,128},{128,64},{192,0},{1,193},{65,129},{129,65},{193,1... | collective-permute-start | bytes 393224 | tf_op jit(solution)/shard_map/ppermute | solution.py:23
  63.8 0.0 collective-permute-done.9
  63.8 0.3 collective-permute-start.6
  64.1 0.0 collective-permute-done.10
  64.1 0.0 collective-permute-done.8
  64.1 2.5 %collective-permute-start.11 = (f32[128,128]{1,0:T(8,128)S(1)}, f32[128,128]{1,0:T(8,128)S(1)}, u32[]{:S(2)}, u32[]{:S(2)}) collective-permute-start(f32[128,128]{1,0:T(8,128)S(1)} %add_add_fusion), channel_id=1, source_target_pairs={{0,32},{32,0},{1,33},{33,1},{2,34},{34,2},{3,35},{35,3},{4,36},{36... | collective-permute-start | bytes 196616 | tf_op jit(solution)/shard_map/ppermute | solution.py:19
  66.7 0.6 slice_bitcast_fusion.6
  67.3 0.0 collective-permute-start.3
  67.3 4.2 %collective-permute-done.4.rest_2_ = bf16[256,256]{1,0:T(8,128)(2,1)S(1)} collective-permute-done((bf16[256,256]{1,0:T(8,128)(2,1)S(1)}, bf16[256,256]{1,0:T(8,128)(2,1)S(1)}, u32[]{:S(2)}, u32[]{:S(2)}) %collective-permute-start.4) | collective-permute-done | bytes 131104 | tf_op jit(solution)/shard_map/ppermute | solution.py:23
  71.5 0.5 collective-permute-start.5
  72.0 0.0 collective-permute-done.6.rest_4_
  72.0 0.0 collective-permute-start.7
  72.1 0.0 collective-permute-done.rest_1_
  72.1 0.0 copy-done.1
  72.1 0.0 copy-start
  72.1 2.2 %copy-done = bf16[2,512,2048]{2,1,0:T(8,128)(2,1)S(1)} copy-done((bf16[2,512,2048]{2,1,0:T(8,128)(2,1)S(1)}, bf16[2,512,2048]{2,1,0:T(8,128)(2,1)}, u32[]{:S(2)}) %copy-start) | copy-done | bytes 4194328
  74.3 0.4 update_own.1.rhs_ref
  74.7 0.0 collective-permute-done.11
  74.7 0.7 pad_maximum_fusion.1
  75.4 0.0 collective-permute-done.3.rest_1_
  75.4 0.0 collective-permute-done.5.rest_3_
  75.4 0.0 collective-permute-done.7.rest_5_
  75.4 1.8 %update_rest.1 = f32[2,512,128]{2,1,0:T(8,128)} custom-call(bf16[2,512,2048]{2,1,0:T(8,128)(2,1)S(1)} %copy-done, f32[2,512,128]{2,1,0:T(8,128)S(1)} %update_own.1.rhs_ref, bf16[256,256]{1,0:T(8,128)(2,1)S(1)} %collective-permute-done.2.rest_0_, bf16[256,256]{1,0:T(8,128)(2,1)S(1)} %collective-permute-done.3.rest_1_, ...), custom_call_target="tpu_custom_call" | custom-call | flops 805306368 | bytes 3145728 | tf_op jit(solution)/shard_map/update_rest/pallas_call | solution.py:104
  (12 shorter events, 0.2 us)
Async XLA Ops:
  0.6 71.4 %copy-start.1 = (f32[2,512,128]{2,1,0:T(8,128)S(1)}, f32[2,512,128]{2,1,0:T(8,128)}, u32[]{:S(2)}) copy-start(f32[2,512,128]{2,1,0:T(8,128)} %rhs_ref.1) | copy-start | bytes 1572868
  30.3 16.2 %all-to-all-start.1 = ((bf16[32,40,128]{2,1,0:T(8,128)(2,1)}), bf16[32,40,128]{2,1,0:T(8,128)(2,1)S(1)}, u32[]{:S(2)}, u32[]{:S(2)}) async-start(bf16[32,40,128]{2,1,0:T(8,128)(2,1)} %broadcast_in_dim.2), calls=%async_computation.1 | async-start | bytes 655360 | tf_op jit(solution)/shard_map/all_to_all | solution.py:136
  46.8 5.5 %collective-permute-start.1 = (f32[128,128]{1,0:T(8,128)S(1)}, f32[128,128]{1,0:T(8,128)S(1)}, u32[]{:S(2)}, u32[]{:S(2)}) collective-permute-start(f32[128,128]{1,0:T(8,128)S(1)} %dynamic-slice_bitcast_fusion), channel_id=1, source_target_pairs={{0,32},{32,0},{1,33},{33,1},{2,34},{34,2},{3,35},{35,3},{4,36},{36... | collective-permute-start | bytes 196616 | tf_op jit(solution)/shard_map/ppermute | solution.py:19
  50.9 5.2 %collective-permute-start.2 = (bf16[256,256]{1,0:T(8,128)(2,1)S(1)}, bf16[256,256]{1,0:T(8,128)(2,1)S(1)}, u32[]{:S(2)}, u32[]{:S(2)}) collective-permute-start(bf16[256,256]{1,0:T(8,128)(2,1)S(1)} %pad_maximum_fusion.rest_0_), channel_id=1, source_target_pairs={{0,64},{64,0},{128,192},{192,128},{1,65},{65,1},{129,193},{193,129... | collective-permute-start | bytes 393224 | tf_op jit(solution)/shard_map/ppermute | solution.py:23
  56.1 7.6 %collective-permute-start.9 = (f32[128,128]{1,0:T(8,128)S(1)}, f32[128,128]{1,0:T(8,128)S(1)}, u32[]{:S(2)}, u32[]{:S(2)}) collective-permute-start(f32[128,128]{1,0:T(8,128)S(1)} %bitcast_add_fusion), channel_id=1, source_target_pairs={{0,64},{64,0},{128,192},{192,128},{1,65},{65,1},{129,193},{193,129... | collective-permute-start | bytes 196616 | tf_op jit(solution)/shard_map/ppermute | solution.py:23
  57.4 6.7 %collective-permute-start.10 = (f32[128,128]{1,0:T(8,128)S(1)}, f32[128,128]{1,0:T(8,128)S(1)}, u32[]{:S(2)}, u32[]{:S(2)}) collective-permute-start(f32[128,128]{1,0:T(8,128)S(1)} %bitcast_add_fusion), channel_id=1, source_target_pairs={{0,192},{64,128},{128,64},{192,0},{1,193},{65,129},{129,65},{193,1... | collective-permute-start | bytes 196616 | tf_op jit(solution)/shard_map/ppermute | solution.py:23
  59.3 4.8 %collective-permute-start.8 = (f32[128,128]{1,0:T(8,128)S(1)}, f32[128,128]{1,0:T(8,128)S(1)}, u32[]{:S(2)}, u32[]{:S(2)}) collective-permute-start(f32[128,128]{1,0:T(8,128)S(1)} %bitcast_add_fusion), channel_id=1, source_target_pairs={{0,128},{64,192},{128,0},{192,64},{1,129},{65,193},{129,1},{193,65... | collective-permute-start | bytes 196616 | tf_op jit(solution)/shard_map/ppermute | solution.py:23
  60.0 12.0 %collective-permute-start = (bf16[256,256]{1,0:T(8,128)(2,1)S(1)}, bf16[256,256]{1,0:T(8,128)(2,1)S(1)}, u32[]{:S(2)}, u32[]{:S(2)}) collective-permute-start(bf16[256,256]{1,0:T(8,128)(2,1)S(1)} %pad_maximum_fusion.rest_0_), channel_id=1, source_target_pairs={{0,32},{32,0},{1,33},{33,1},{2,34},{34,2},{3,35},{35,3},{4,36},{36... | collective-permute-start | bytes 393224 | tf_op jit(solution)/shard_map/ppermute | solution.py:19
  61.4 10.1 %collective-permute-start.4 = (bf16[256,256]{1,0:T(8,128)(2,1)S(1)}, bf16[256,256]{1,0:T(8,128)(2,1)S(1)}, u32[]{:S(2)}, u32[]{:S(2)}) collective-permute-start(bf16[256,256]{1,0:T(8,128)(2,1)S(1)} %pad_maximum_fusion.rest_0_), channel_id=1, source_target_pairs={{0,192},{64,128},{128,64},{192,0},{1,193},{65,129},{129,65},{193,1... | collective-permute-start | bytes 393224 | tf_op jit(solution)/shard_map/ppermute | solution.py:23
  63.8 8.3 %collective-permute-start.6 = (bf16[256,256]{1,0:T(8,128)(2,1)S(1)}, bf16[256,256]{1,0:T(8,128)(2,1)S(1)}, u32[]{:S(2)}, u32[]{:S(2)}) collective-permute-start(bf16[256,256]{1,0:T(8,128)(2,1)S(1)} %pad_maximum_fusion.rest_0_), channel_id=1, source_target_pairs={{0,128},{64,192},{128,0},{192,64},{1,129},{65,193},{129,1},{193,65... | collective-permute-start | bytes 393224 | tf_op jit(solution)/shard_map/ppermute | solution.py:23
  64.1 10.6 %collective-permute-start.11 = (f32[128,128]{1,0:T(8,128)S(1)}, f32[128,128]{1,0:T(8,128)S(1)}, u32[]{:S(2)}, u32[]{:S(2)}) collective-permute-start(f32[128,128]{1,0:T(8,128)S(1)} %add_add_fusion), channel_id=1, source_target_pairs={{0,32},{32,0},{1,33},{33,1},{2,34},{34,2},{3,35},{35,3},{4,36},{36... | collective-permute-start | bytes 196616 | tf_op jit(solution)/shard_map/ppermute | solution.py:19
  67.3 8.1 %collective-permute-start.3 = (bf16[256,256]{1,0:T(8,128)(2,1)S(1)}, bf16[256,256]{1,0:T(8,128)(2,1)S(1)}, u32[]{:S(2)}, u32[]{:S(2)}) collective-permute-start(bf16[256,256]{1,0:T(8,128)(2,1)S(1)} %collective-permute-done.2.rest_0_), channel_id=1, source_target_pairs={{0,32},{32,0},{1,33},{33,1},{2,34},{34,2},{3,35},{35,3},{4,36},{36... | collective-permute-start | bytes 393224 | tf_op jit(solution)/shard_map/ppermute | solution.py:19
  71.5 3.9 %collective-permute-start.5 = (bf16[256,256]{1,0:T(8,128)(2,1)S(1)}, bf16[256,256]{1,0:T(8,128)(2,1)S(1)}, u32[]{:S(2)}, u32[]{:S(2)}) collective-permute-start(bf16[256,256]{1,0:T(8,128)(2,1)S(1)} %collective-permute-done.4.rest_2_), channel_id=1, source_target_pairs={{0,32},{32,0},{1,33},{33,1},{2,34},{34,2},{3,35},{35,3},{4,36},{36... | collective-permute-start | bytes 393224 | tf_op jit(solution)/shard_map/ppermute | solution.py:19
  72.0 3.4 %collective-permute-start.7 = (bf16[256,256]{1,0:T(8,128)(2,1)S(1)}, bf16[256,256]{1,0:T(8,128)(2,1)S(1)}, u32[]{:S(2)}, u32[]{:S(2)}) collective-permute-start(bf16[256,256]{1,0:T(8,128)(2,1)S(1)} %collective-permute-done.6.rest_4_), channel_id=1, source_target_pairs={{0,32},{32,0},{1,33},{33,1},{2,34},{34,2},{3,35},{35,3},{4,36},{36... | collective-permute-start | bytes 393224 | tf_op jit(solution)/shard_map/ppermute | solution.py:19
  72.1 2.2 %copy-start = (bf16[2,512,2048]{2,1,0:T(8,128)(2,1)S(1)}, bf16[2,512,2048]{2,1,0:T(8,128)(2,1)}, u32[]{:S(2)}) copy-start(bf16[2,512,2048]{2,1,0:T(8,128)(2,1)} %factor_ref.3) | copy-start | bytes 12582916

commit v3 on v2

--- a/solution.py
+++ b/solution.py
@@ -154,11 +154,13 @@
     mine = lax.dynamic_index_in_dim(share, core, 0, keepdims=False)
     other = lax.dynamic_index_in_dim(share, 1 - core, 0, keepdims=False)
     half = mine + swapped(other)
-    half, beside[1] = lax.optimization_barrier((half, beside[1]))
-    half = (half + flipped(half, 2)) + (flipped(half, 1) + flipped(half, 3))
-    back = swapped(half)
     started = update(TURNS[:1], factor_slab, pending_rhs, [block, twin], "update_own")
+    half, started, landed = lax.optimization_barrier(
+        (half, started, [beside[k] for k in TURNS[1:]])
+    )
+    beside = dict(zip(TURNS[1:], landed))
     twins = {k: swapped(beside[k]) for k in TURNS[1:]}
+    others = [flipped(half, k) for k in (1, 2, 3)]
     updated_rhs = update(
         TURNS[1:],
         factor_slab,
@@ -166,6 +168,9 @@
         [b for k in TURNS[1:] for b in (beside[k], twins[k])],
         "update_rest",
     )
+    others, updated_rhs = lax.optimization_barrier((others, updated_rhs))
+    half = (half + others[1]) + (others[0] + others[2])
+    back = swapped(half)
     modal_forces = jnp.stack(
         [jnp.where(core == 0, half, back), jnp.where(core == 0, back, half)]
     )

time: 77.6 us -> 74 us (0.954)
  waiting for transfers between devices: 19.3 us -> 14.8 us
  local copies, waits for them, and re-layouts: 3.6 us -> 5.78 us
  starting transfers between devices: 21.5 us -> 20.3 us
    ppermute x6, waiting for transfers between devices: 8.05 us -> 3.24 us  [flipped(): return lax.ppermute(value, 'y', [(i, i ^ bits) for i in range(4)])]
    unnamed x4 -> x6, local copies, waits for them, and re-layouts: 2.19 us -> 4.37 us
    ppermute x6, starting transfers between devices: 8.53 us -> 7.41 us  [swapped(): return lax.ppermute(value, 'core', SWAP)]
  transfers between devices with their start and end apart: 13 -> 13, of which waited for: 3 -> 4; matrix products, arithmetic and copies ran while one was open for 2% -> 1% of each run, Pallas kernels for 1% -> 3%
where the time goes in v3:
time: 74 us; the launch traced here: 73.7 us
  blocking collectives  25.7 us (35%)
  starting transfers between devices  20.3 us (27%)
  waiting for transfers between devices  14.8 us (20%)
  local copies, waits for them, and re-layouts  5.78 us (8%)
  Pallas kernels  4.7 us (6%)
  other arithmetic  1.49 us (2%)
  between operations  0.79 us (1%)
    all_to_all x1, blocking collectives, on_device(): summed = jnp.sum(lax.all_to_all(outgoing, COL, 0, 0, tiled=True), axis=0)  25.7 us
    all_to_all x1, waiting for transfers between devices, on_device(): lax.all_to_all(jnp.broadcast_to(packed[None], (peers, rows, width)), COL,...  11.2 us
    ppermute x6, starting transfers between devices, flipped(): return lax.ppermute(value, 'y', [(i, i ^ bits) for i in range(4)])  7.85 us
    ppermute x6, starting transfers between devices, swapped(): return lax.ppermute(value, 'core', SWAP)  7.41 us
    all_to_all x1, starting transfers between devices, on_device(): lax.all_to_all(jnp.broadcast_to(packed[None], (peers, rows, width)), COL,...  5 us
    unnamed x6, local copies, waits for them, and re-layouts  4.37 us
    ppermute x6, waiting for transfers between devices, flipped(): return lax.ppermute(value, 'y', [(i, i ^ bits) for i in range(4)])  3.24 us
    pallas_call x1, Pallas kernels, first_partials(): pl.pallas_call(first_kernel, out_shape=jax.ShapeDtypeStruct((peers, 3 * o...  2.42 us
  transfers between devices with their start and end apart: 13, of which 4 were waited for; matrix products, arithmetic and copies ran while one was open for 1% of the time, Pallas kernels for 3%

profile of v3, /device:TPU:1, one launch (start us, length us, event | category | flops | bytes accessed | tf_op | source)
XLA Modules:
  0.0 73.7 jit_solution(4163010547281178622)
XLA Ops:
  0.6 0.0 copy-start.2
  0.6 2.4 %partials.1 = f32[32,24,128]{2,1,0:T(8,128)} custom-call(f32[2,64,256]{2,1,0:T(8,128)} %bitcast.26, f32[2,64,128]{2,1,0:T(8,128)} %rhs_hbm.1, bf16[256,128]{1,0:T(8,128)(2,1)} %modes_hbm.1, bf16[2,256,128]{2,1,0:T(8,128)(2,1)} %solved_hbm.1), custom_call_target="tpu_custom_call" | custom-call | tf_op jit(solution)/shard_map/partials/pallas_call | solution.py:68
  3.1 25.7 %all_to_all.10 = f32[32,24,128]{2,1,0:T(8,128)S(1)} all-to-all(f32[32,24,128]{2,1,0:T(8,128)} %partials.1), channel_id=1, replica_groups=mesh['y'=4,'core'=2,'z'=8,'x'=4] {'z','x'}, dimensions={0} | all-to-all | bytes 786432 | tf_op jit(solution)/shard_map/all_to_all | solution.py:127
  28.8 0.7 pad_maximum_fusion.2
  29.5 0.8 %broadcast_in_dim.2 = bf16[32,40,128]{2,1,0:T(8,128)(2,1)} broadcast(bf16[40,128]{1,0:T(8,128)(2,1)S(1)} %pad_maximum_fusion.2), dimensions={1,2} | broadcast | bytes 337920 | tf_op jit(solution)/shard_map/broadcast_in_dim | solution.py:137
  30.3 5.0 %all-to-all-start.1 = ((bf16[32,40,128]{2,1,0:T(8,128)(2,1)}), bf16[32,40,128]{2,1,0:T(8,128)(2,1)S(1)}, u32[]{:S(2)}, u32[]{:S(2)}) async-start(bf16[32,40,128]{2,1,0:T(8,128)(2,1)} %broadcast_in_dim.2), calls=%async_computation.1 | async-start | bytes 655360 | tf_op jit(solution)/shard_map/all_to_all | solution.py:136
  35.3 11.2 %all-to-all-done.1 = bf16[32,40,128]{2,1,0:T(8,128)(2,1)S(1)} async-done(((bf16[32,40,128]{2,1,0:T(8,128)(2,1)}), bf16[32,40,128]{2,1,0:T(8,128)(2,1)S(1)}, u32[]{:S(2)}, u32[]{:S(2)}) %all-to-all-start.1) | async-done | bytes 327712 | tf_op jit(solution)/shard_map/all_to_all | solution.py:136
  46.5 0.2 fusion
  46.8 4.1 %collective-permute-start = (f32[128,128]{1,0:T(8,128)S(1)}, f32[128,128]{1,0:T(8,128)S(1)}, u32[]{:S(2)}, u32[]{:S(2)}) collective-permute-start(f32[128,128]{1,0:T(8,128)S(1)} %dynamic-slice_bitcast_fusion), channel_id=1, source_target_pairs={{0,32},{32,0},{1,33},{33,1},{2,34},{34,2},{3,35},{35,3},{4,36},{36... | collective-permute-start | bytes 196616 | tf_op jit(solution)/shard_map/ppermute | solution.py:19
  50.9 0.1 collective-permute-start.1
  51.0 1.4 %collective-permute-start.2 = (bf16[256,256]{1,0:T(8,128)(2,1)S(1)}, bf16[256,256]{1,0:T(8,128)(2,1)S(1)}, u32[]{:S(2)}, u32[]{:S(2)}) collective-permute-start(bf16[256,256]{1,0:T(8,128)(2,1)S(1)} %pad_maximum_fusion.rest_0_), channel_id=1, source_target_pairs={{0,64},{64,0},{128,192},{192,128},{1,65},{65,1},{129,193},{193,129... | collective-permute-start | bytes 393224 | tf_op jit(solution)/shard_map/ppermute | solution.py:23
  52.4 1.9 %collective-permute-start.3 = (bf16[256,256]{1,0:T(8,128)(2,1)S(1)}, bf16[256,256]{1,0:T(8,128)(2,1)S(1)}, u32[]{:S(2)}, u32[]{:S(2)}) collective-permute-start(bf16[256,256]{1,0:T(8,128)(2,1)S(1)} %pad_maximum_fusion.rest_0_), channel_id=1, source_target_pairs={{0,192},{64,128},{128,64},{192,0},{1,193},{65,129},{129,65},{193,1... | collective-permute-start | bytes 393224 | tf_op jit(solution)/shard_map/ppermute | solution.py:23
  54.3 0.7 collective-permute-start.4
  55.0 0.0 collective-permute-done
  55.1 0.0 collective-permute-done.1.rest_1_
  55.1 0.0 copy-done.2
  55.1 0.0 copy-start
  55.1 2.2 %copy-done = bf16[2,512,2048]{2,1,0:T(8,128)(2,1)S(1)} copy-done((bf16[2,512,2048]{2,1,0:T(8,128)(2,1)S(1)}, bf16[2,512,2048]{2,1,0:T(8,128)(2,1)}, u32[]{:S(2)}) %copy-start) | copy-done | bytes 4194328
  57.3 0.4 update_own.1.rhs_ref
  57.7 0.0 collective-permute-done.2.rest_0_
  57.7 1.4 %collective-permute-done.3.rest_2_ = bf16[256,256]{1,0:T(8,128)(2,1)S(1)} collective-permute-done((bf16[256,256]{1,0:T(8,128)(2,1)S(1)}, bf16[256,256]{1,0:T(8,128)(2,1)S(1)}, u32[]{:S(2)}, u32[]{:S(2)}) %collective-permute-start.3) | collective-permute-done | bytes 131104 | tf_op jit(solution)/shard_map/ppermute | solution.py:23
  59.1 1.8 %collective-permute-done.4.rest_4_ = bf16[256,256]{1,0:T(8,128)(2,1)S(1)} collective-permute-done((bf16[256,256]{1,0:T(8,128)(2,1)S(1)}, bf16[256,256]{1,0:T(8,128)(2,1)S(1)}, u32[]{:S(2)}, u32[]{:S(2)}) %collective-permute-start.4) | collective-permute-done | bytes 131104 | tf_op jit(solution)/shard_map/ppermute | solution.py:23
  61.0 1.4 %collective-permute-start.10 = (bf16[256,256]{1,0:T(8,128)(2,1)S(1)}, bf16[256,256]{1,0:T(8,128)(2,1)S(1)}, u32[]{:S(2)}, u32[]{:S(2)}) collective-permute-start(bf16[256,256]{1,0:T(8,128)(2,1)S(1)} %collective-permute-done.4.rest_4_), channel_id=1, source_target_pairs={{0,32},{32,0},{1,33},{33,1},{2,34},{34,2},{3,35},{35,3},{4,36},{36... | collective-permute-start | bytes 393224 | tf_op jit(solution)/shard_map/ppermute | solution.py:19
  62.3 0.0 collective-permute-start.8
  62.3 0.5 collective-permute-start.9
  62.9 0.0 collective-permute-start.5
  62.9 3.1 %collective-permute-start.6 = (f32[128,128]{1,0:T(8,128)S(1)}, f32[128,128]{1,0:T(8,128)S(1)}, u32[]{:S(2)}, u32[]{:S(2)}) collective-permute-start(f32[128,128]{1,0:T(8,128)S(1)} %bitcast_add_fusion), channel_id=1, source_target_pairs={{0,128},{64,192},{128,0},{192,64},{1,129},{65,193},{129,1},{193,65... | collective-permute-start | bytes 196616 | tf_op jit(solution)/shard_map/ppermute | solution.py:23
  65.9 0.0 collective-permute-done.10.rest_5_
  65.9 0.8 %collective-permute-start.7 = (f32[128,128]{1,0:T(8,128)S(1)}, f32[128,128]{1,0:T(8,128)S(1)}, u32[]{:S(2)}, u32[]{:S(2)}) collective-permute-start(f32[128,128]{1,0:T(8,128)S(1)} %bitcast_add_fusion), channel_id=1, source_target_pairs={{0,192},{64,128},{128,64},{192,0},{1,193},{65,129},{129,65},{193,1... | collective-permute-start | bytes 196616 | tf_op jit(solution)/shard_map/ppermute | solution.py:23
  66.7 0.0 collective-permute-done.8.rest_1_
  66.7 0.0 collective-permute-done.9.rest_3_
  66.7 0.0 copy-start.1
  66.7 2.2 %copy-done.1 = bf16[2,512,2048]{2,1,0:T(8,128)(2,1)S(1)} copy-done((bf16[2,512,2048]{2,1,0:T(8,128)(2,1)S(1)}, bf16[2,512,2048]{2,1,0:T(8,128)(2,1)}, u32[]{:S(2)}) %copy-start.1) | copy-done | bytes 4194328
  68.9 1.8 %update_rest.1 = f32[2,512,128]{2,1,0:T(8,128)} custom-call(bf16[2,512,2048]{2,1,0:T(8,128)(2,1)S(1)} %copy-done.1, f32[2,512,128]{2,1,0:T(8,128)S(1)} %update_own.1.rhs_ref, bf16[256,256]{1,0:T(8,128)(2,1)S(1)} %collective-permute-done.2.rest_0_, bf16[256,256]{1,0:T(8,128)(2,1)S(1)} %collective-permute-done.8.rest_1_, ...), custom_call_target="tpu_custom_call" | custom-call | flops 805306368 | bytes 3145728 | tf_op jit(solution)/shard_map/update_rest/pallas_call | solution.py:104
  70.7 0.0 collective-permute-done.5
  70.8 0.0 collective-permute-done.6
  70.8 0.0 collective-permute-done.7
  70.8 1.3 %collective-permute-start.11 = (f32[128,128]{1,0:T(8,128)S(1)}, f32[128,128]{1,0:T(8,128)S(1)}, u32[]{:S(2)}, u32[]{:S(2)}) collective-permute-start(f32[128,128]{1,0:T(8,128)S(1)} %add_add_fusion), channel_id=1, source_target_pairs={{0,32},{32,0},{1,33},{33,1},{2,34},{34,2},{3,35},{35,3},{4,36},{36... | collective-permute-start | bytes 196616 | tf_op jit(solution)/shard_map/ppermute | solution.py:19
  72.1 0.6 slice_bitcast_fusion.6
  72.7 0.3 collective-permute-done.11
  73.0 0.7 pad_maximum_fusion.1
  (12 shorter events, 0.2 us)
Async XLA Ops:
  0.6 54.4 %copy-start.2 = (f32[2,512,128]{2,1,0:T(8,128)S(1)}, f32[2,512,128]{2,1,0:T(8,128)}, u32[]{:S(2)}) copy-start(f32[2,512,128]{2,1,0:T(8,128)} %rhs_ref.1) | copy-start | bytes 1572868
  30.3 16.2 %all-to-all-start.1 = ((bf16[32,40,128]{2,1,0:T(8,128)(2,1)}), bf16[32,40,128]{2,1,0:T(8,128)(2,1)S(1)}, u32[]{:S(2)}, u32[]{:S(2)}) async-start(bf16[32,40,128]{2,1,0:T(8,128)(2,1)} %broadcast_in_dim.2), calls=%async_computation.1 | async-start | bytes 655360 | tf_op jit(solution)/shard_map/all_to_all | solution.py:136
  46.8 8.2 %collective-permute-start = (f32[128,128]{1,0:T(8,128)S(1)}, f32[128,128]{1,0:T(8,128)S(1)}, u32[]{:S(2)}, u32[]{:S(2)}) collective-permute-start(f32[128,128]{1,0:T(8,128)S(1)} %dynamic-slice_bitcast_fusion), channel_id=1, source_target_pairs={{0,32},{32,0},{1,33},{33,1},{2,34},{34,2},{3,35},{35,3},{4,36},{36... | collective-permute-start | bytes 196616 | tf_op jit(solution)/shard_map/ppermute | solution.py:19
  50.9 4.1 %collective-permute-start.1 = (bf16[256,256]{1,0:T(8,128)(2,1)S(1)}, bf16[256,256]{1,0:T(8,128)(2,1)S(1)}, u32[]{:S(2)}, u32[]{:S(2)}) collective-permute-start(bf16[256,256]{1,0:T(8,128)(2,1)S(1)} %pad_maximum_fusion.rest_0_), channel_id=1, source_target_pairs={{0,32},{32,0},{1,33},{33,1},{2,34},{34,2},{3,35},{35,3},{4,36},{36... | collective-permute-start | bytes 393224 | tf_op jit(solution)/shard_map/ppermute | solution.py:19
  51.0 6.7 %collective-permute-start.2 = (bf16[256,256]{1,0:T(8,128)(2,1)S(1)}, bf16[256,256]{1,0:T(8,128)(2,1)S(1)}, u32[]{:S(2)}, u32[]{:S(2)}) collective-permute-start(bf16[256,256]{1,0:T(8,128)(2,1)S(1)} %pad_maximum_fusion.rest_0_), channel_id=1, source_target_pairs={{0,64},{64,0},{128,192},{192,128},{1,65},{65,1},{129,193},{193,129... | collective-permute-start | bytes 393224 | tf_op jit(solution)/shard_map/ppermute | solution.py:23
  52.4 6.7 %collective-permute-start.3 = (bf16[256,256]{1,0:T(8,128)(2,1)S(1)}, bf16[256,256]{1,0:T(8,128)(2,1)S(1)}, u32[]{:S(2)}, u32[]{:S(2)}) collective-permute-start(bf16[256,256]{1,0:T(8,128)(2,1)S(1)} %pad_maximum_fusion.rest_0_), channel_id=1, source_target_pairs={{0,192},{64,128},{128,64},{192,0},{1,193},{65,129},{129,65},{193,1... | collective-permute-start | bytes 393224 | tf_op jit(solution)/shard_map/ppermute | solution.py:23
  54.3 6.6 %collective-permute-start.4 = (bf16[256,256]{1,0:T(8,128)(2,1)S(1)}, bf16[256,256]{1,0:T(8,128)(2,1)S(1)}, u32[]{:S(2)}, u32[]{:S(2)}) collective-permute-start(bf16[256,256]{1,0:T(8,128)(2,1)S(1)} %pad_maximum_fusion.rest_0_), channel_id=1, source_target_pairs={{0,128},{64,192},{128,0},{192,64},{1,129},{65,193},{129,1},{193,65... | collective-permute-start | bytes 393224 | tf_op jit(solution)/shard_map/ppermute | solution.py:23
  55.1 2.2 %copy-start = (bf16[2,512,2048]{2,1,0:T(8,128)(2,1)S(1)}, bf16[2,512,2048]{2,1,0:T(8,128)(2,1)}, u32[]{:S(2)}) copy-start(bf16[2,512,2048]{2,1,0:T(8,128)(2,1)} %factor_ref.3) | copy-start | bytes 12582916
  61.0 5.0 %collective-permute-start.10 = (bf16[256,256]{1,0:T(8,128)(2,1)S(1)}, bf16[256,256]{1,0:T(8,128)(2,1)S(1)}, u32[]{:S(2)}, u32[]{:S(2)}) collective-permute-start(bf16[256,256]{1,0:T(8,128)(2,1)S(1)} %collective-permute-done.4.rest_4_), channel_id=1, source_target_pairs={{0,32},{32,0},{1,33},{33,1},{2,34},{34,2},{3,35},{35,3},{4,36},{36... | collective-permute-start | bytes 393224 | tf_op jit(solution)/shard_map/ppermute | solution.py:19
  62.3 4.4 %collective-permute-start.8 = (bf16[256,256]{1,0:T(8,128)(2,1)S(1)}, bf16[256,256]{1,0:T(8,128)(2,1)S(1)}, u32[]{:S(2)}, u32[]{:S(2)}) collective-permute-start(bf16[256,256]{1,0:T(8,128)(2,1)S(1)} %collective-permute-done.2.rest_0_), channel_id=1, source_target_pairs={{0,32},{32,0},{1,33},{33,1},{2,34},{34,2},{3,35},{35,3},{4,36},{36... | collective-permute-start | bytes 393224 | tf_op jit(solution)/shard_map/ppermute | solution.py:19
  62.3 4.4 %collective-permute-start.9 = (bf16[256,256]{1,0:T(8,128)(2,1)S(1)}, bf16[256,256]{1,0:T(8,128)(2,1)S(1)}, u32[]{:S(2)}, u32[]{:S(2)}) collective-permute-start(bf16[256,256]{1,0:T(8,128)(2,1)S(1)} %collective-permute-done.3.rest_2_), channel_id=1, source_target_pairs={{0,32},{32,0},{1,33},{33,1},{2,34},{34,2},{3,35},{35,3},{4,36},{36... | collective-permute-start | bytes 393224 | tf_op jit(solution)/shard_map/ppermute | solution.py:19
  62.9 7.9 %collective-permute-start.5 = (f32[128,128]{1,0:T(8,128)S(1)}, f32[128,128]{1,0:T(8,128)S(1)}, u32[]{:S(2)}, u32[]{:S(2)}) collective-permute-start(f32[128,128]{1,0:T(8,128)S(1)} %bitcast_add_fusion), channel_id=1, source_target_pairs={{0,64},{64,0},{128,192},{192,128},{1,65},{65,1},{129,193},{193,129... | collective-permute-start | bytes 196616 | tf_op jit(solution)/shard_map/ppermute | solution.py:23
  62.9 7.9 %collective-permute-start.6 = (f32[128,128]{1,0:T(8,128)S(1)}, f32[128,128]{1,0:T(8,128)S(1)}, u32[]{:S(2)}, u32[]{:S(2)}) collective-permute-start(f32[128,128]{1,0:T(8,128)S(1)} %bitcast_add_fusion), channel_id=1, source_target_pairs={{0,128},{64,192},{128,0},{192,64},{1,129},{65,193},{129,1},{193,65... | collective-permute-start | bytes 196616 | tf_op jit(solution)/shard_map/ppermute | solution.py:23
  65.9 4.8 %collective-permute-start.7 = (f32[128,128]{1,0:T(8,128)S(1)}, f32[128,128]{1,0:T(8,128)S(1)}, u32[]{:S(2)}, u32[]{:S(2)}) collective-permute-start(f32[128,128]{1,0:T(8,128)S(1)} %bitcast_add_fusion), channel_id=1, source_target_pairs={{0,192},{64,128},{128,64},{192,0},{1,193},{65,129},{129,65},{193,1... | collective-permute-start | bytes 196616 | tf_op jit(solution)/shard_map/ppermute | solution.py:23
  66.7 2.2 %copy-start.1 = (bf16[2,512,2048]{2,1,0:T(8,128)(2,1)S(1)}, bf16[2,512,2048]{2,1,0:T(8,128)(2,1)}, u32[]{:S(2)}) copy-start(bf16[2,512,2048]{2,1,0:T(8,128)(2,1)} %factor_ref.3) | copy-start | bytes 12582916
  70.8 2.2 %collective-permute-start.11 = (f32[128,128]{1,0:T(8,128)S(1)}, f32[128,128]{1,0:T(8,128)S(1)}, u32[]{:S(2)}, u32[]{:S(2)}) collective-permute-start(f32[128,128]{1,0:T(8,128)S(1)} %add_add_fusion), channel_id=1, source_target_pairs={{0,32},{32,0},{1,33},{33,1},{2,34},{34,2},{3,35},{35,3},{4,36},{36... | collective-permute-start | bytes 196616 | tf_op jit(solution)/shard_map/ppermute | solution.py:19

commit v4 on v2

--- a/solution.py
+++ b/solution.py
@@ -19,13 +19,14 @@
     return lax.ppermute(value, "core", SWAP)
 
 
-def flipped(value, bits):
-    return lax.ppermute(value, "y", [(i, i ^ bits) for i in range(4)])
-
-
-def first_kernel(diag_hbm, rhs_hbm, modes_hbm, solved_hbm, out_ref, diag_ref, rhs_ref, modes_ref, solved_ref, sems):
+def flipped(value, axis, bits):
+    size = lax.axis_size(axis)
+    return lax.ppermute(value, axis, [(i, i ^ bits) for i in range(size)])
+
+
+def first_kernel(diag_hbm, rhs_hbm, modes_hbm, solved_hbm, out_ref, earlier_ref, diag_ref, rhs_ref, modes_ref, solved_ref, sems):
     peers, rows, width = out_ref.shape
-    own = rows // 3
+    own = rows // 2
     moves = [
         pltpu.make_async_copy(source, target, sems.at[i])
         for i, (source, target) in enumerate(
@@ -40,14 +41,12 @@
     for move in moves:
         move.start()
     over_first = (((0,), (0,)), ((), ()))
-    half = peers // 2
     moves[0].wait()
     moves[1].wait()
     for c in range(2):
-        earlier = lax.dot_general(
+        earlier_ref[c] = lax.dot_general(
             modes_ref[...], solved_ref[c], over_first, preferred_element_type=F32
         )
-        out_ref[c * half : (c + 1) * half, 2 * own :, :] = earlier.reshape(half, own, width)
     moves[2].wait()
     moves[3].wait()
     left = jnp.concatenate([diag_ref[0], diag_ref[1]], axis=0)
@@ -59,7 +58,7 @@
         left, right, over_first, precision=lax.Precision.HIGHEST, preferred_element_type=F32
     )
     out_ref[:, :own, :] = partial[:, :width].reshape(peers, own, width)
-    out_ref[:, own : 2 * own, :] = partial[:, width:].reshape(peers, own, width)
+    out_ref[:, own:, :] = partial[:, width:].reshape(peers, own, width)
 
 
 def first_partials(diag_inverse, panel_rhs, modes_prev, solved_prev, peers, own):
@@ -67,9 +66,12 @@
     args = (jnp.swapaxes(diag_inverse, 1, 2), panel_rhs, modes_prev, solved_prev)
     return pl.pallas_call(
         first_kernel,
-        out_shape=jax.ShapeDtypeStruct((peers, 3 * own, width), F32),
+        out_shape=(
+            jax.ShapeDtypeStruct((peers, 2 * own, width), F32),
+            jax.ShapeDtypeStruct((2, width, width), F32),
+        ),
         in_specs=[pl.BlockSpec(memory_space=pltpu.HBM)] * 4,
-        out_specs=pl.BlockSpec(memory_space=pltpu.VMEM),
+        out_specs=(pl.BlockSpec(memory_space=pltpu.VMEM),) * 2,
         scratch_shapes=[pltpu.VMEM(a.shape, a.dtype) for a in args]
         + [pltpu.SemaphoreType.DMA((4,))],
         name="partials",
@@ -116,6 +118,34 @@
     )(factor_slab, rhs, *blocks)
 
 
+def split(value):
+    high = lax.reduce_precision(value, 8, 7)
+    return jnp.concatenate([high.astype(BF16), (value - high).astype(BF16)], axis=0)
+
+
+def joined(pair):
+    count = pair.shape[0] // 2
+    return pair[:count].astype(F32) + pair[count:].astype(F32)
+
+
+def once(step, carry):
+    count = lax.optimization_barrier(jnp.int32(1))
+    return lax.fori_loop(0, count, lambda _, held: step(held), carry)
+
+
+def doubled(total, modes, axis, bit):
+    count = 2 * total.shape[0]
+    width = total.shape[1]
+    mine = split(total)
+    sent = jnp.concatenate([mine, modes.reshape(-1, width)], axis=0)
+    came = flipped(sent, axis, bit)
+    total = joined(mine) + joined(came[:count])
+    theirs = came[count:].reshape(modes.shape)
+    lower = (lax.axis_index(axis) & bit) == 0
+    modes = jnp.stack([jnp.where(lower, modes, theirs), jnp.where(lower, theirs, modes)])
+    return total, modes.reshape((-1,) + modes.shape[2:])
+
+
 def on_device(
     diag_inverse, panel_rhs, factor_slab, pending_rhs, solved_prev, modes_prev, modes_panel
 ):
@@ -123,52 +153,95 @@
     own = modes_panel.shape[0]
     peers = diag_inverse.shape[1] // own
     core = lax.axis_index("core")
-    outgoing = first_partials(diag_inverse, panel_rhs, modes_prev, solved_prev, peers, own)
-    summed = jnp.sum(lax.all_to_all(outgoing, COL, 0, 0, tiled=True), axis=0)
-    panel_solution = summed[: 2 * own].reshape(2, own, width)
-    share = summed[2 * own :]
-    high = lax.reduce_precision(share, 8, 7)
-    low = share - high
-    packed = jnp.concatenate(
-        [summed[: 2 * own].astype(BF16), modes_panel, high.astype(BF16), low.astype(BF16)], axis=0
-    )
-    rows = packed.shape[0]
+    y = lax.axis_index("y")
+    outgoing, earlier = first_partials(
+        diag_inverse, panel_rhs, modes_prev, solved_prev, peers, own
+    )
+    came = lax.all_to_all(outgoing, COL, 0, 0, tiled=True)
+
+    def near(carry):
+        earlier, total, modes = carry
+        mine = lax.dynamic_index_in_dim(earlier, core, 0, keepdims=False)
+        other = lax.dynamic_index_in_dim(earlier, 1 - core, 0, keepdims=False)
+        half = (mine + swapped(other)).reshape(4, width // 4, width)
+        total = lax.dynamic_index_in_dim(half, y, 0, keepdims=False)
+        rows = [modes_panel]
+        for k in (1, 2, 3):
+            chunk = lax.dynamic_index_in_dim(half, y ^ k, 0, keepdims=False)
+            part = flipped(jnp.concatenate([split(chunk), modes_panel], axis=0), "y", k)
+            total = total + joined(part[: 2 * width // 4])
+            rows.append(part[2 * width // 4 :])
+        rows = jnp.stack(rows)[None]
+        total, rows = doubled(total, rows, "x", 1)
+        total, rows = doubled(total, rows, "x", 2)
+        return earlier, total, rows
+
+    total = jnp.zeros((width // 4, width), F32)
+    modes = jnp.zeros((4, 4, own, width), BF16)
+    earlier, total, modes = once(near, (earlier, total, modes))
+    came, total, modes = lax.optimization_barrier((came, total, modes))
+
+    panel_solution = jnp.sum(came, axis=0)
+    rounded = panel_solution.astype(BF16)
+    panel_solution = panel_solution.reshape(2, own, width)
     gathered = lax.all_to_all(
-        jnp.broadcast_to(packed[None], (peers, rows, width)), COL, 0, 0, tiled=True
-    )
+        jnp.broadcast_to(rounded[None], (peers, 2 * own, width)), COL, 0, 0, tiled=True
+    )
+
+    def far(carry):
+        total, rows, _ = carry
+        after, rows = doubled(total, rows, "z", 1)
+        after, wide = doubled(after, rows, "z", 2)
+        return total, carry[1], (after, wide)
+
+    wide = (jnp.zeros_like(total), jnp.zeros((16, 4, own, width), BF16))
+    _, _, (total, modes) = once(far, (total, modes, wide))
+    gathered, total, modes = lax.optimization_barrier((gathered, total, modes))
+
     block = jnp.concatenate(
         [
             gathered[:, :own].reshape(peers * own, width),
-            gathered[:, own : 2 * own].reshape(peers * own, width),
+            gathered[:, own:].reshape(peers * own, width),
         ],
         axis=1,
     )
-    beside = {k: flipped(block, k) for k in TURNS[1:]}
+    beside = [flipped(block, "y", k) for k in TURNS[1:]]
     twin = swapped(block)
-    modes_block = gathered[:, 2 * own : 3 * own].reshape(peers * own, width)
-    share = gathered[:, 3 * own : 4 * own].astype(F32) + gathered[:, 4 * own :].astype(F32)
-    latest = lax.dot_general(
-        modes_block, block, (((0,), (0,)), ((), ())), preferred_element_type=F32
-    )
-    share = share.reshape(2, width, width) + jnp.stack([latest[:, :width], latest[:, width:]])
-    mine = lax.dynamic_index_in_dim(share, core, 0, keepdims=False)
-    other = lax.dynamic_index_in_dim(share, 1 - core, 0, keepdims=False)
-    half = mine + swapped(other)
-    half, beside[1] = lax.optimization_barrier((half, beside[1]))
-    half = (half + flipped(half, 2)) + (flipped(half, 1) + flipped(half, 3))
-    back = swapped(half)
+    total, modes = doubled(total, modes, "z", 4)
     started = update(TURNS[:1], factor_slab, pending_rhs, [block, twin], "update_own")
-    twins = {k: swapped(beside[k]) for k in TURNS[1:]}
+    started, beside, total, modes = lax.optimization_barrier((started, beside, total, modes))
+
+    totals = [total] + [flipped(total, "y", k) for k in (1, 2, 3)]
+    blocks = dict(zip(TURNS, [block] + beside))
+    twins = [swapped(b) for b in beside]
+    latest = [
+        lax.dot_general(
+            modes[:, k].reshape(peers * own, width),
+            blocks[k],
+            (((0,), (0,)), ((), ())),
+            preferred_element_type=F32,
+        )
+        for k in range(4)
+    ]
+    latest = (latest[0] + latest[2]) + (latest[1] + latest[3])
     updated_rhs = update(
         TURNS[1:],
         factor_slab,
         started,
-        [b for k in TURNS[1:] for b in (beside[k], twins[k])],
+        [b for two in zip(beside, twins) for b in two],
         "update_rest",
     )
-    modal_forces = jnp.stack(
-        [jnp.where(core == 0, half, back), jnp.where(core == 0, back, half)]
-    )
+    totals, updated_rhs = lax.optimization_barrier((jnp.stack(totals), updated_rhs))
+    earlier = jnp.concatenate(
+        [lax.dynamic_index_in_dim(totals, y ^ k, 0, keepdims=False) for k in range(4)], axis=0
+    )
+    both = jnp.stack(
+        [
+            latest[:, :width] + jnp.where(core == 0, earlier, 0.0),
+            latest[:, width:] + jnp.where(core == 1, earlier, 0.0),
+        ]
+    )
+    modal_forces = both + swapped(both)
     return (panel_solution, updated_rhs, modal_forces)
 
 

time: 77.6 us -> 94.3 us (1.22)
  starting transfers between devices: 21.5 us -> 55 us
  blocking collectives: 25.7 us -> 0 us
  other arithmetic: 1.49 us -> 10.3 us
  waiting for transfers between devices: 19.3 us -> 15.8 us
  local copies, waits for them, and re-layouts: 3.6 us -> 6.26 us
    all_to_all x1 -> x0, blocking collectives: 25.7 us -> none  [on_device(): summed = jnp.sum(lax.all_to_all(outgoing, COL, 0, 0, tiled=True), axis=0)]
    ppermute x6 -> x14, starting transfers between devices: 7.99 us -> 23.1 us  [flipped(): return lax.ppermute(value, axis, [(i, i ^ bits) for i in range(size)])]
    all_to_all x1 -> x2, starting transfers between devices: 5 us -> 17.2 us  [the longest x1 9.3 us: on_device(): came = lax.all_to_all(outgoing, COL, 0, 0, tiled=True)]
    all_to_all x1 -> x2, waiting for transfers between devices: 11.2 us -> 1.66 us  [the longest x1 1.66 us: on_device(): lax.all_to_all(jnp.broadcast_to(rounded[None], (peers, 2 * own, width)),...]
    ppermute x6, starting transfers between devices: 8.53 us -> 14.7 us  [swapped(): return lax.ppermute(value, 'core', SWAP)]
    ppermute x6 -> x14, waiting for transfers between devices: 8.05 us -> 13.1 us  [flipped(): return lax.ppermute(value, axis, [(i, i ^ bits) for i in range(size)])]
    add x4 -> x5, other arithmetic: 0.06 us -> 2.75 us  [the longest x3 1.23 us: doubled(): total = joined(mine) + joined(came[:count])]
    another operation x2 -> x11, other arithmetic: 0.68 us -> 2.76 us  [the longest x2 1.38 us: near(): rows = jnp.stack(rows)[None]]
  transfers between devices with their start and end apart: 13 -> 22, of which waited for: 3 -> 10; matrix products, arithmetic and copies ran while one was open for 2% -> 12% of each run, Pallas kernels for 1% -> 0%
where the time goes in v4:
time: 94.3 us; the launch traced here: 93.7 us
  starting transfers between devices  55 us (58%)
  waiting for transfers between devices  15.8 us (17%)
  other arithmetic  10.3 us (11%)
  local copies, waits for them, and re-layouts  6.26 us (7%)
  Pallas kernels  4.61 us (5%)
    ppermute x14, starting transfers between devices, flipped(): return lax.ppermute(value, axis, [(i, i ^ bits) for i in range(size)])  23.1 us
    ppermute x6, starting transfers between devices, swapped(): return lax.ppermute(value, 'core', SWAP)  14.7 us
    ppermute x14, waiting for transfers between devices, flipped(): return lax.ppermute(value, axis, [(i, i ^ bits) for i in range(size)])  13.1 us
    all_to_all x1, starting transfers between devices, on_device(): came = lax.all_to_all(outgoing, COL, 0, 0, tiled=True)  9.3 us
    all_to_all x1, starting transfers between devices, on_device(): lax.all_to_all(jnp.broadcast_to(rounded[None], (peers, 2 * own, width)),...  7.88 us
    pallas_call x1, Pallas kernels, first_partials(): pl.pallas_call(first_kernel, out_shape=(jax.ShapeDtypeStruct((peers, 2 *...  2.33 us
    pallas_call x2, Pallas kernels, update(): pl.pallas_call(functools.partial(update_kernel, turns), out_shape=jax.Sha...  2.28 us
    unnamed x8, local copies, waits for them, and re-layouts  2.2 us
  transfers between devices with their start and end apart: 22, of which 10 were waited for; matrix products, arithmetic and copies ran while one was open for 12% of the time, Pallas kernels for 0%

profile of v4, /device:TPU:1, one launch (start us, length us, event | category | flops | bytes accessed | tf_op | source)
XLA Modules:
  0.0 93.7 jit_solution(18278887319850223768)
XLA Ops:
  0.6 2.3 %partials.1 = (f32[32,16,128]{2,1,0:T(8,128)}, f32[2,128,128]{2,1,0:T(8,128)}) custom-call(f32[2,64,256]{2,1,0:T(8,128)} %bitcast.146, f32[2,64,128]{2,1,0:T(8,128)} %rhs_hbm.1, bf16[256,128]{1,0:T(8,128)(2,1)} %modes_hbm.1, bf16[2,256,128]{2,1,0:T(8,128)(2,1)} %solved_hbm.1), custom_call_target="tpu_custom_call" | custom-call | tf_op jit(solution)/shard_map/partials/pallas_call | solution.py:67
  3.0 0.9 dynamic-slice_bitcast_fusion
  3.8 3.2 %collective-permute-start.3 = (f32[128,128]{1,0:T(8,128)S(1)}, f32[128,128]{1,0:T(8,128)S(1)}, u32[]{:S(2)}, u32[]{:S(2)}) collective-permute-start(f32[128,128]{1,0:T(8,128)S(1)} %dynamic-slice_bitcast_fusion), channel_id=1, source_target_pairs={{0,32},{32,0},{1,33},{33,1},{2,34},{34,2},{3,35},{35,3},{4,36},{36... | collective-permute-start | bytes 196616 | tf_op jit(solution)/shard_map/while/body/ppermute | solution.py:19
  7.1 9.3 %all-to-all-start = ((f32[32,16,128]{2,1,0:T(8,128)}), f32[32,16,128]{2,1,0:T(8,128)S(1)}, u32[]{:S(2)}, u32[]{:S(2)}) async-start(f32[32,16,128]{2,1,0:T(8,128)} %get-tuple-element.377), calls=%async_computation | async-start | bytes 524288 | tf_op jit(solution)/shard_map/all_to_all | solution.py:160
  16.4 0.9 bitcast_add_fusion.1
  17.3 0.7 pad_maximum_fusion.14
  18.0 1.3 %collective-permute-start.4 = (bf16[72,128]{1,0:T(8,128)(2,1)S(1)}, bf16[72,128]{1,0:T(8,128)(2,1)S(1)}, u32[]{:S(2)}, u32[]{:S(2)}) collective-permute-start(bf16[72,128]{1,0:T(8,128)(2,1)S(1)} %get-tuple-element.475), channel_id=1, source_target_pairs={{0,64},{64,0},{128,192},{192,128},{1,65},{65,1},{129,193},{193,129... | collective-permute-start | bytes 55304 | tf_op jit(solution)/shard_map/while/body/ppermute | solution.py:24
  19.3 2.6 %collective-permute-start.5 = (bf16[72,128]{1,0:T(8,128)(2,1)S(1)}, bf16[72,128]{1,0:T(8,128)(2,1)S(1)}, u32[]{:S(2)}, u32[]{:S(2)}) collective-permute-start(bf16[72,128]{1,0:T(8,128)(2,1)S(1)} %get-tuple-element.474), channel_id=1, source_target_pairs={{0,128},{64,192},{128,0},{192,64},{1,129},{65,193},{129,1},{193,65... | collective-permute-start | bytes 55304 | tf_op jit(solution)/shard_map/while/body/ppermute | solution.py:24
  21.9 0.0 collective-permute-done.4
  21.9 1.8 %collective-permute-done.5 = bf16[72,128]{1,0:T(8,128)(2,1)S(1)} collective-permute-done((bf16[72,128]{1,0:T(8,128)(2,1)S(1)}, bf16[72,128]{1,0:T(8,128)(2,1)S(1)}, u32[]{:S(2)}, u32[]{:S(2)}) %collective-permute-start.5) | collective-permute-done | bytes 18464 | tf_op jit(solution)/shard_map/while/body/ppermute | solution.py:24
  23.7 2.3 %collective-permute-done.6 = bf16[72,128]{1,0:T(8,128)(2,1)S(1)} collective-permute-done((bf16[72,128]{1,0:T(8,128)(2,1)S(1)}, bf16[72,128]{1,0:T(8,128)(2,1)S(1)}, u32[]{:S(2)}, u32[]{:S(2)}) %collective-permute-start.6) | collective-permute-done | bytes 18464 | tf_op jit(solution)/shard_map/while/body/ppermute | solution.py:24
  26.0 0.7 pad_maximum_fusion.18
  26.7 0.7 pad_maximum_fusion.17
  27.4 0.6 broadcast_in_dim.24
  28.0 0.6 broadcast.83.clone
  28.6 8.5 %while.29 = (s32[]{:T(128)}, f32[32,128]{1,0:T(8,128)}, bf16[4,4,8,128]{3,2,1,0:T(8,128)(2,1)}, s32[]{:T(128)}, f32[1,32,128]{2,1,0:T(8,128)S(1)}, /*index=5*/bf...) while((s32[]{:T(128)}, f32[32,128]{1,0:T(8,128)}, ...), condition=%wide.region_1.2_spmd, body=%wide.region_0.1_spmd.sunk | while | flops 385032 | bytes 794901 | solution.py:133
  28.6 1.3 %collective-permute-start = (bf16[96,128]{1,0:T(8,128)(2,1)S(1)}, bf16[96,128]{1,0:T(8,128)(2,1)S(1)}, u32[]{:S(2)}, u32[]{:S(2)}) collective-permute-start(bf16[96,128]{1,0:T(8,128)(2,1)S(1)} %pad_maximum_fusion.27), channel_id=1, source_target_pairs={{0,1},{1,0},{2,3},{3,2},{4,5},{5,4},{6,7},{7,6},{8,9},{9,8},{10,11... | collective-permute-start | bytes 73736 | tf_op jit(solution)/shard_map/while/body/ppermute | solution.py:24
  30.0 1.4 %collective-permute-done = bf16[96,128]{1,0:T(8,128)(2,1)S(1)} collective-permute-done((bf16[96,128]{1,0:T(8,128)(2,1)S(1)}, bf16[96,128]{1,0:T(8,128)(2,1)S(1)}, u32[]{:S(2)}, u32[]{:S(2)}) %collective-permute-start) | collective-permute-done | bytes 24608 | tf_op jit(solution)/shard_map/while/body/ppermute | solution.py:24
  31.5 2.8 %collective-permute-start.1 = (bf16[128,128]{1,0:T(8,128)(2,1)S(1)}, bf16[128,128]{1,0:T(8,128)(2,1)S(1)}, u32[]{:S(2)}, u32[]{:S(2)}) collective-permute-start(bf16[128,128]{1,0:T(8,128)(2,1)S(1)} %pad_maximum_fusion.29), channel_id=1, source_target_pairs={{0,2},{1,3},{2,0},{3,1},{4,6},{5,7},{6,4},{7,5},{8,10},{9,11},{10,... | collective-permute-start | bytes 98312 | tf_op jit(solution)/shard_map/while/body/ppermute | solution.py:24
  34.3 1.6 %collective-permute-done.1 = bf16[128,128]{1,0:T(8,128)(2,1)S(1)} collective-permute-done((bf16[128,128]{1,0:T(8,128)(2,1)S(1)}, bf16[128,128]{1,0:T(8,128)(2,1)S(1)}, u32[]{:S(2)}, u32[]{:S(2)}) %collective-permute-start.1) | collective-permute-done | bytes 32800 | tf_op jit(solution)/shard_map/while/body/ppermute | solution.py:24
  35.9 0.6 pad_maximum_fusion.30
  36.5 0.6 add_add_fusion.7
  37.1 0.0 all-to-all-done
  37.1 0.7 fusion.21
  37.8 0.8 pad_maximum_fusion.13
  38.7 1.3 %collective-permute-start.7 = (bf16[192,128]{1,0:T(8,128)(2,1)S(1)}, bf16[192,128]{1,0:T(8,128)(2,1)S(1)}, u32[]{:S(2)}, u32[]{:S(2)}) collective-permute-start(bf16[192,128]{1,0:T(8,128)(2,1)S(1)} %pad_maximum_fusion.13), channel_id=1, source_target_pairs={{0,4},{4,0},{8,12},{12,8},{16,20},{20,16},{24,28},{28,24},{1,5},{5... | collective-permute-start | bytes 147464 | tf_op jit(solution)/shard_map/while/body/ppermute | solution.py:24
  40.0 0.0 copy-start.3
  40.0 0.7 broadcast_in_dim.25
  40.7 7.9 %all-to-all-start.1 = ((bf16[32,16,128]{2,1,0:T(8,128)(2,1)}), bf16[32,16,128]{2,1,0:T(8,128)(2,1)S(1)}, u32[]{:S(2)}, u32[]{:S(2)}) async-start(bf16[32,16,128]{2,1,0:T(8,128)(2,1)} %broadcast_in_dim.25), calls=%async_computation.1 | async-start | bytes 262144 | tf_op jit(solution)/shard_map/all_to_all | solution.py:187
  48.6 0.7 broadcast_in_dim.26
  49.3 0.6 broadcast.83
  49.9 6.4 %while.30 = (s32[]{:T(128)}, f32[32,128]{1,0:T(8,128)}, bf16[16,4,8,128]{3,2,1,0:T(8,128)(2,1)}, s32[]{:T(128)}, bf16[32,128]{1,0:T(8,128)(2,1)S(1)}, /*index=5*...) while((s32[]{:T(128)}, f32[32,128]{1,0:T(8,128)}, ...), condition=%wide.region_4.5_spmd, body=%wide.region_3.4_spmd.sunk | while | flops 516105 | bytes 1573105 | solution.py:133
  49.9 0.8 bitcast_select_fusion.10
  50.7 2.2 %collective-permute-start.2 = (bf16[320,128]{1,0:T(8,128)(2,1)S(1)}, bf16[320,128]{1,0:T(8,128)(2,1)S(1)}, u32[]{:S(2)}, u32[]{:S(2)}) collective-permute-start(bf16[320,128]{1,0:T(8,128)(2,1)S(1)} %pad_maximum_fusion.32), channel_id=1, source_target_pairs={{0,8},{4,12},{8,0},{12,4},{16,24},{20,28},{24,16},{28,20},{1,9},{5... | collective-permute-start | bytes 245768 | tf_op jit(solution)/shard_map/while/body/ppermute | solution.py:24
  52.9 2.1 %collective-permute-done.2 = bf16[320,128]{1,0:T(8,128)(2,1)S(1)} collective-permute-done((bf16[320,128]{1,0:T(8,128)(2,1)S(1)}, bf16[320,128]{1,0:T(8,128)(2,1)S(1)}, u32[]{:S(2)}, u32[]{:S(2)}) %collective-permute-start.2) | collective-permute-done | bytes 81952 | tf_op jit(solution)/shard_map/while/body/ppermute | solution.py:24
  55.0 0.7 pad_maximum_fusion.33
  55.7 0.6 add_add_fusion.8
  56.3 1.7 %all-to-all-done.1 = bf16[32,16,128]{2,1,0:T(8,128)(2,1)S(1)} async-done(((bf16[32,16,128]{2,1,0:T(8,128)(2,1)}), bf16[32,16,128]{2,1,0:T(8,128)(2,1)S(1)}, u32[]{:S(2)}, u32[]{:S(2)}) %all-to-all-start.1) | async-done | bytes 131104 | tf_op jit(solution)/shard_map/all_to_all | solution.py:187
  57.9 0.7 reduce-precision_convert_fusion.3
  58.7 6.4 %collective-permute-start.8 = (bf16[256,256]{1,0:T(8,128)(2,1)S(1)}, bf16[256,256]{1,0:T(8,128)(2,1)S(1)}, u32[]{:S(2)}, u32[]{:S(2)}) collective-permute-start(bf16[256,256]{1,0:T(8,128)(2,1)S(1)} %pad_maximum_fusion.9.rest_0_), channel_id=1, source_target_pairs={{0,32},{32,0},{1,33},{33,1},{2,34},{34,2},{3,35},{35,3},{4,36},{36... | collective-permute-start | bytes 393224 | tf_op jit(solution)/shard_map/ppermute | solution.py:19
  65.1 0.9 pad_maximum_fusion.8
  66.0 4.8 %collective-permute-start.12 = (bf16[576,128]{1,0:T(8,128)(2,1)S(1)}, bf16[576,128]{1,0:T(8,128)(2,1)S(1)}, u32[]{:S(2)}, u32[]{:S(2)}) collective-permute-start(bf16[576,128]{1,0:T(8,128)(2,1)S(1)} %pad_maximum_fusion.8), channel_id=1, source_target_pairs={{0,16},{4,20},{8,24},{12,28},{16,0},{20,4},{24,8},{28,12},{1,17},{... | collective-permute-start | bytes 442376 | tf_op jit(solution)/shard_map/ppermute | solution.py:24
  70.7 0.0 collective-permute-start.10
  70.7 0.4 collective-permute-start.11
  71.2 2.8 %collective-permute-start.9 = (bf16[256,256]{1,0:T(8,128)(2,1)S(1)}, bf16[256,256]{1,0:T(8,128)(2,1)S(1)}, u32[]{:S(2)}, u32[]{:S(2)}) collective-permute-start(bf16[256,256]{1,0:T(8,128)(2,1)S(1)} %pad_maximum_fusion.9.rest_0_), channel_id=1, source_target_pairs={{0,64},{64,0},{128,192},{192,128},{1,65},{65,1},{129,193},{193,129... | collective-permute-start | bytes 393224 | tf_op jit(solution)/shard_map/ppermute | solution.py:24
  74.0 0.0 collective-permute-done.8.rest_1_
  74.0 2.2 %copy-done = bf16[2,512,2048]{2,1,0:T(8,128)(2,1)S(1)} copy-done((bf16[2,512,2048]{2,1,0:T(8,128)(2,1)S(1)}, bf16[2,512,2048]{2,1,0:T(8,128)(2,1)}, u32[]{:S(2)}) %copy-start) | copy-done | bytes 4194328
  76.2 0.5 update_own.1.rhs_ref
  76.6 1.9 %collective-permute-done.12 = bf16[576,128]{1,0:T(8,128)(2,1)S(1)} collective-permute-done((bf16[576,128]{1,0:T(8,128)(2,1)S(1)}, bf16[576,128]{1,0:T(8,128)(2,1)S(1)}, u32[]{:S(2)}, u32[]{:S(2)}) %collective-permute-start.12) | collective-permute-done | bytes 147488 | tf_op jit(solution)/shard_map/ppermute | solution.py:24
  78.7 1.2 %collective-permute-done.10.rest_2_ = bf16[256,256]{1,0:T(8,128)(2,1)S(1)} collective-permute-done((bf16[256,256]{1,0:T(8,128)(2,1)S(1)}, bf16[256,256]{1,0:T(8,128)(2,1)S(1)}, u32[]{:S(2)}, u32[]{:S(2)}) %collective-permute-start.10) | collective-permute-done | bytes 131104 | tf_op jit(solution)/shard_map/ppermute | solution.py:24
  79.9 1.2 %collective-permute-start.14 = (f32[32,128]{1,0:T(8,128)S(1)}, f32[32,128]{1,0:T(8,128)S(1)}, u32[]{:S(2)}, u32[]{:S(2)}) collective-permute-start(f32[32,128]{1,0:T(8,128)S(1)} %add_add_fusion.4), channel_id=1, source_target_pairs={{0,128},{64,192},{128,0},{192,64},{1,129},{65,193},{129,1},{193,65... | collective-permute-start | bytes 49160 | tf_op jit(solution)/shard_map/ppermute | solution.py:24
  81.1 2.5 %collective-permute-start.17 = (bf16[256,256]{1,0:T(8,128)(2,1)S(1)}, bf16[256,256]{1,0:T(8,128)(2,1)S(1)}, u32[]{:S(2)}, u32[]{:S(2)}) collective-permute-start(bf16[256,256]{1,0:T(8,128)(2,1)S(1)} %collective-permute-done.10.rest_2_), channel_id=1, source_target_pairs={{0,32},{32,0},{1,33},{33,1},{2,34},{34,2},{3,35},{35,3},{4,36},{36... | collective-permute-start | bytes 393224 | tf_op jit(solution)/shard_map/ppermute | solution.py:19
  83.6 0.2 fusion.8
  83.8 0.1 collective-permute-start.16
  83.9 0.2 convolution_add_fusion
  84.1 0.2 fusion.12
  84.3 2.3 %collective-permute-start.15 = (f32[32,128]{1,0:T(8,128)S(1)}, f32[32,128]{1,0:T(8,128)S(1)}, u32[]{:S(2)}, u32[]{:S(2)}) collective-permute-start(f32[32,128]{1,0:T(8,128)S(1)} %add_add_fusion.4), channel_id=1, source_target_pairs={{0,192},{64,128},{128,64},{192,0},{1,193},{65,129},{129,65},{193,1... | collective-permute-start | bytes 49160 | tf_op jit(solution)/shard_map/ppermute | solution.py:24
  86.6 0.8 collective-permute-start.18
  87.4 0.2 fusion.5
  87.6 0.8 collective-permute-done.15
  88.4 1.8 %update_rest.1 = f32[2,512,128]{2,1,0:T(8,128)} custom-call(bf16[2,512,2048]{2,1,0:T(8,128)(2,1)S(1)} %copy-done, f32[2,512,128]{2,1,0:T(8,128)S(1)} %update_own.1.rhs_ref, bf16[256,256]{1,0:T(8,128)(2,1)S(1)} %collective-permute-done.9.rest_0_, bf16[256,256]{1,0:T(8,128)(2,1)S(1)} %collective-permute-done.16.rest_1_, ...), custom_call_target="tpu_custom_call" | custom-call | flops 805306368 | bytes 3145728 | tf_op jit(solution)/shard_map/update_rest/pallas_call | solution.py:106
  90.3 1.7 %collective-permute-start.19 = (f32[2,128,128]{2,1,0:T(8,128)S(1)}, f32[2,128,128]{2,1,0:T(8,128)S(1)}, u32[]{:S(2)}, u32[]{:S(2)}) collective-permute-start(f32[2,128,128]{2,1,0:T(8,128)S(1)} %pad_maximum_fusion.10), channel_id=1, source_target_pairs={{0,32},{32,0},{1,33},{33,1},{2,34},{34,2},{3,35},{35,3},{4,36},{36... | collective-permute-start | bytes 393224 | tf_op jit(solution)/shard_map/ppermute | solution.py:19
  92.0 1.0 %collective-permute-done.19 = f32[2,128,128]{2,1,0:T(8,128)S(1)} collective-permute-done((f32[2,128,128]{2,1,0:T(8,128)S(1)}, f32[2,128,128]{2,1,0:T(8,128)S(1)}, u32[]{:S(2)}, u32[]{:S(2)}) %collective-permute-start.19) | collective-permute-done | bytes 131104 | tf_op jit(solution)/shard_map/ppermute | solution.py:19
  93.0 0.7 fusion.23
  (49 shorter events, 0.4 us)
Async XLA Ops:
  3.8 12.6 %collective-permute-start.3 = (f32[128,128]{1,0:T(8,128)S(1)}, f32[128,128]{1,0:T(8,128)S(1)}, u32[]{:S(2)}, u32[]{:S(2)}) collective-permute-start(f32[128,128]{1,0:T(8,128)S(1)} %dynamic-slice_bitcast_fusion), channel_id=1, source_target_pairs={{0,32},{32,0},{1,33},{33,1},{2,34},{34,2},{3,35},{35,3},{4,36},{36... | collective-permute-start | bytes 196616 | tf_op jit(solution)/shard_map/while/body/ppermute | solution.py:19
  7.1 30.1 %all-to-all-start = ((f32[32,16,128]{2,1,0:T(8,128)}), f32[32,16,128]{2,1,0:T(8,128)S(1)}, u32[]{:S(2)}, u32[]{:S(2)}) async-start(f32[32,16,128]{2,1,0:T(8,128)} %get-tuple-element.377), calls=%async_computation | async-start | bytes 524288 | tf_op jit(solution)/shard_map/all_to_all | solution.py:160
  18.0 3.9 %collective-permute-start.4 = (bf16[72,128]{1,0:T(8,128)(2,1)S(1)}, bf16[72,128]{1,0:T(8,128)(2,1)S(1)}, u32[]{:S(2)}, u32[]{:S(2)}) collective-permute-start(bf16[72,128]{1,0:T(8,128)(2,1)S(1)} %get-tuple-element.475), channel_id=1, source_target_pairs={{0,64},{64,0},{128,192},{192,128},{1,65},{65,1},{129,193},{193,129... | collective-permute-start | bytes 55304 | tf_op jit(solution)/shard_map/while/body/ppermute | solution.py:24
  19.3 4.4 %collective-permute-start.5 = (bf16[72,128]{1,0:T(8,128)(2,1)S(1)}, bf16[72,128]{1,0:T(8,128)(2,1)S(1)}, u32[]{:S(2)}, u32[]{:S(2)}) collective-permute-start(bf16[72,128]{1,0:T(8,128)(2,1)S(1)} %get-tuple-element.474), channel_id=1, source_target_pairs={{0,128},{64,192},{128,0},{192,64},{1,129},{65,193},{129,1},{193,65... | collective-permute-start | bytes 55304 | tf_op jit(solution)/shard_map/while/body/ppermute | solution.py:24
  21.9 4.1 %collective-permute-start.6 = (bf16[72,128]{1,0:T(8,128)(2,1)S(1)}, bf16[72,128]{1,0:T(8,128)(2,1)S(1)}, u32[]{:S(2)}, u32[]{:S(2)}) collective-permute-start(bf16[72,128]{1,0:T(8,128)(2,1)S(1)} %get-tuple-element.473), channel_id=1, source_target_pairs={{0,192},{64,128},{128,64},{192,0},{1,193},{65,129},{129,65},{193,1... | collective-permute-start | bytes 55304 | tf_op jit(solution)/shard_map/while/body/ppermute | solution.py:24
  28.6 2.8 %collective-permute-start = (bf16[96,128]{1,0:T(8,128)(2,1)S(1)}, bf16[96,128]{1,0:T(8,128)(2,1)S(1)}, u32[]{:S(2)}, u32[]{:S(2)}) collective-permute-start(bf16[96,128]{1,0:T(8,128)(2,1)S(1)} %pad_maximum_fusion.27), channel_id=1, source_target_pairs={{0,1},{1,0},{2,3},{3,2},{4,5},{5,4},{6,7},{7,6},{8,9},{9,8},{10,11... | collective-permute-start | bytes 73736 | tf_op jit(solution)/shard_map/while/body/ppermute | solution.py:24
  31.5 4.4 %collective-permute-start.1 = (bf16[128,128]{1,0:T(8,128)(2,1)S(1)}, bf16[128,128]{1,0:T(8,128)(2,1)S(1)}, u32[]{:S(2)}, u32[]{:S(2)}) collective-permute-start(bf16[128,128]{1,0:T(8,128)(2,1)S(1)} %pad_maximum_fusion.29), channel_id=1, source_target_pairs={{0,2},{1,3},{2,0},{3,1},{4,6},{5,7},{6,4},{7,5},{8,10},{9,11},{10,... | collective-permute-start | bytes 98312 | tf_op jit(solution)/shard_map/while/body/ppermute | solution.py:24
  37.8 36.1 %copy-start.1 = (f32[2,512,128]{2,1,0:T(8,128)S(1)}, f32[2,512,128]{2,1,0:T(8,128)}, u32[]{:S(2)}) copy-start(f32[2,512,128]{2,1,0:T(8,128)} %rhs_ref.1) | copy-start | bytes 1572868
  38.7 9.9 %collective-permute-start.7 = (bf16[192,128]{1,0:T(8,128)(2,1)S(1)}, bf16[192,128]{1,0:T(8,128)(2,1)S(1)}, u32[]{:S(2)}, u32[]{:S(2)}) collective-permute-start(bf16[192,128]{1,0:T(8,128)(2,1)S(1)} %pad_maximum_fusion.13), channel_id=1, source_target_pairs={{0,4},{4,0},{8,12},{12,8},{16,20},{20,16},{24,28},{28,24},{1,5},{5... | collective-permute-start | bytes 147464 | tf_op jit(solution)/shard_map/while/body/ppermute | solution.py:24
  40.0 36.7 %copy-start.3 = (f32[16,128]{1,0:T(8,128)}, f32[16,128]{1,0:T(8,128)S(1)}, u32[]{:S(2)}) copy-start(f32[16,128]{1,0:T(8,128)S(1)} %reduce_sum.9) | copy-start | bytes 24580
  40.7 17.2 %all-to-all-start.1 = ((bf16[32,16,128]{2,1,0:T(8,128)(2,1)}), bf16[32,16,128]{2,1,0:T(8,128)(2,1)S(1)}, u32[]{:S(2)}, u32[]{:S(2)}) async-start(bf16[32,16,128]{2,1,0:T(8,128)(2,1)} %broadcast_in_dim.25), calls=%async_computation.1 | async-start | bytes 262144 | tf_op jit(solution)/shard_map/all_to_all | solution.py:187
  50.7 4.3 %collective-permute-start.2 = (bf16[320,128]{1,0:T(8,128)(2,1)S(1)}, bf16[320,128]{1,0:T(8,128)(2,1)S(1)}, u32[]{:S(2)}, u32[]{:S(2)}) collective-permute-start(bf16[320,128]{1,0:T(8,128)(2,1)S(1)} %pad_maximum_fusion.32), channel_id=1, source_target_pairs={{0,8},{4,12},{8,0},{12,4},{16,24},{20,28},{24,16},{28,20},{1,9},{5... | collective-permute-start | bytes 245768 | tf_op jit(solution)/shard_map/while/body/ppermute | solution.py:24
  56.3 22.3 %copy-start.2 = (bf16[16,4,8,128]{3,2,1,0:T(8,128)(2,1)S(1)}, bf16[16,4,8,128]{3,2,1,0:T(8,128)(2,1)}, u32[]{:S(2)}) copy-start(bf16[16,4,8,128]{3,2,1,0:T(8,128)(2,1)} %get-tuple-element.388) | copy-start | bytes 393220
  58.7 15.3 %collective-permute-start.8 = (bf16[256,256]{1,0:T(8,128)(2,1)S(1)}, bf16[256,256]{1,0:T(8,128)(2,1)S(1)}, u32[]{:S(2)}, u32[]{:S(2)}) collective-permute-start(bf16[256,256]{1,0:T(8,128)(2,1)S(1)} %pad_maximum_fusion.9.rest_0_), channel_id=1, source_target_pairs={{0,32},{32,0},{1,33},{33,1},{2,34},{34,2},{3,35},{35,3},{4,36},{36... | collective-permute-start | bytes 393224 | tf_op jit(solution)/shard_map/ppermute | solution.py:19
  66.0 12.6 %collective-permute-start.12 = (bf16[576,128]{1,0:T(8,128)(2,1)S(1)}, bf16[576,128]{1,0:T(8,128)(2,1)S(1)}, u32[]{:S(2)}, u32[]{:S(2)}) collective-permute-start(bf16[576,128]{1,0:T(8,128)(2,1)S(1)} %pad_maximum_fusion.8), channel_id=1, source_target_pairs={{0,16},{4,20},{8,24},{12,28},{16,0},{20,4},{24,8},{28,12},{1,17},{... | collective-permute-start | bytes 442376 | tf_op jit(solution)/shard_map/ppermute | solution.py:24
  70.7 9.2 %collective-permute-start.10 = (bf16[256,256]{1,0:T(8,128)(2,1)S(1)}, bf16[256,256]{1,0:T(8,128)(2,1)S(1)}, u32[]{:S(2)}, u32[]{:S(2)}) collective-permute-start(bf16[256,256]{1,0:T(8,128)(2,1)S(1)} %pad_maximum_fusion.9.rest_0_), channel_id=1, source_target_pairs={{0,192},{64,128},{128,64},{192,0},{1,193},{65,129},{129,65},{193,1... | collective-permute-start | bytes 393224 | tf_op jit(solution)/shard_map/ppermute | solution.py:24
  70.7 9.2 %collective-permute-start.11 = (bf16[256,256]{1,0:T(8,128)(2,1)S(1)}, bf16[256,256]{1,0:T(8,128)(2,1)S(1)}, u32[]{:S(2)}, u32[]{:S(2)}) collective-permute-start(bf16[256,256]{1,0:T(8,128)(2,1)S(1)} %pad_maximum_fusion.9.rest_0_), channel_id=1, source_target_pairs={{0,128},{64,192},{128,0},{192,64},{1,129},{65,193},{129,1},{193,65... | collective-permute-start | bytes 393224 | tf_op jit(solution)/shard_map/ppermute | solution.py:24
  71.2 8.7 %collective-permute-start.9 = (bf16[256,256]{1,0:T(8,128)(2,1)S(1)}, bf16[256,256]{1,0:T(8,128)(2,1)S(1)}, u32[]{:S(2)}, u32[]{:S(2)}) collective-permute-start(bf16[256,256]{1,0:T(8,128)(2,1)S(1)} %pad_maximum_fusion.9.rest_0_), channel_id=1, source_target_pairs={{0,64},{64,0},{128,192},{192,128},{1,65},{65,1},{129,193},{193,129... | collective-permute-start | bytes 393224 | tf_op jit(solution)/shard_map/ppermute | solution.py:24
  74.0 2.2 %copy-start = (bf16[2,512,2048]{2,1,0:T(8,128)(2,1)S(1)}, bf16[2,512,2048]{2,1,0:T(8,128)(2,1)}, u32[]{:S(2)}) copy-start(bf16[2,512,2048]{2,1,0:T(8,128)(2,1)} %factor_ref.3) | copy-start | bytes 12582916
  79.9 6.7 %collective-permute-start.13 = (f32[32,128]{1,0:T(8,128)S(1)}, f32[32,128]{1,0:T(8,128)S(1)}, u32[]{:S(2)}, u32[]{:S(2)}) collective-permute-start(f32[32,128]{1,0:T(8,128)S(1)} %add_add_fusion.4), channel_id=1, source_target_pairs={{0,64},{64,0},{128,192},{192,128},{1,65},{65,1},{129,193},{193,129... | collective-permute-start | bytes 49160 | tf_op jit(solution)/shard_map/ppermute | solution.py:24
  79.9 7.7 %collective-permute-start.14 = (f32[32,128]{1,0:T(8,128)S(1)}, f32[32,128]{1,0:T(8,128)S(1)}, u32[]{:S(2)}, u32[]{:S(2)}) collective-permute-start(f32[32,128]{1,0:T(8,128)S(1)} %add_add_fusion.4), channel_id=1, source_target_pairs={{0,128},{64,192},{128,0},{192,64},{1,129},{65,193},{129,1},{193,65... | collective-permute-start | bytes 49160 | tf_op jit(solution)/shard_map/ppermute | solution.py:24
  81.1 7.3 %collective-permute-start.17 = (bf16[256,256]{1,0:T(8,128)(2,1)S(1)}, bf16[256,256]{1,0:T(8,128)(2,1)S(1)}, u32[]{:S(2)}, u32[]{:S(2)}) collective-permute-start(bf16[256,256]{1,0:T(8,128)(2,1)S(1)} %collective-permute-done.10.rest_2_), channel_id=1, source_target_pairs={{0,32},{32,0},{1,33},{33,1},{2,34},{34,2},{3,35},{35,3},{4,36},{36... | collective-permute-start | bytes 393224 | tf_op jit(solution)/shard_map/ppermute | solution.py:19
  83.8 4.6 %collective-permute-start.16 = (bf16[256,256]{1,0:T(8,128)(2,1)S(1)}, bf16[256,256]{1,0:T(8,128)(2,1)S(1)}, u32[]{:S(2)}, u32[]{:S(2)}) collective-permute-start(bf16[256,256]{1,0:T(8,128)(2,1)S(1)} %collective-permute-done.9.rest_0_), channel_id=1, source_target_pairs={{0,32},{32,0},{1,33},{33,1},{2,34},{34,2},{3,35},{35,3},{4,36},{36... | collective-permute-start | bytes 393224 | tf_op jit(solution)/shard_map/ppermute | solution.py:19
  84.3 4.1 %collective-permute-start.15 = (f32[32,128]{1,0:T(8,128)S(1)}, f32[32,128]{1,0:T(8,128)S(1)}, u32[]{:S(2)}, u32[]{:S(2)}) collective-permute-start(f32[32,128]{1,0:T(8,128)S(1)} %add_add_fusion.4), channel_id=1, source_target_pairs={{0,192},{64,128},{128,64},{192,0},{1,193},{65,129},{129,65},{193,1... | collective-permute-start | bytes 49160 | tf_op jit(solution)/shard_map/ppermute | solution.py:24
  86.6 1.8 %collective-permute-start.18 = (bf16[256,256]{1,0:T(8,128)(2,1)S(1)}, bf16[256,256]{1,0:T(8,128)(2,1)S(1)}, u32[]{:S(2)}, u32[]{:S(2)}) collective-permute-start(bf16[256,256]{1,0:T(8,128)(2,1)S(1)} %collective-permute-done.11.rest_4_), channel_id=1, source_target_pairs={{0,32},{32,0},{1,33},{33,1},{2,34},{34,2},{3,35},{35,3},{4,36},{36... | collective-permute-start | bytes 393224 | tf_op jit(solution)/shard_map/ppermute | solution.py:19
  90.3 2.7 %collective-permute-start.19 = (f32[2,128,128]{2,1,0:T(8,128)S(1)}, f32[2,128,128]{2,1,0:T(8,128)S(1)}, u32[]{:S(2)}, u32[]{:S(2)}) collective-permute-start(f32[2,128,128]{2,1,0:T(8,128)S(1)} %pad_maximum_fusion.10), channel_id=1, source_target_pairs={{0,32},{32,0},{1,33},{33,1},{2,34},{34,2},{3,35},{35,3},{4,36},{36... | collective-permute-start | bytes 393224 | tf_op jit(solution)/shard_map/ppermute | solution.py:19

commit v5 on v2

--- a/solution.py
+++ b/solution.py
@@ -21,6 +21,16 @@
 
 def flipped(value, bits):
     return lax.ppermute(value, "y", [(i, i ^ bits) for i in range(4)])
+
+
+def split(value):
+    high = lax.reduce_precision(value, 8, 7)
+    return jnp.concatenate([high.astype(BF16), (value - high).astype(BF16)], axis=1)
+
+
+def joined(pair):
+    width = pair.shape[1] // 2
+    return pair[:, :width].astype(F32) + pair[:, width:].astype(F32)
 
 
 def first_kernel(diag_hbm, rhs_hbm, modes_hbm, solved_hbm, out_ref, diag_ref, rhs_ref, modes_ref, solved_ref, sems):
@@ -78,15 +88,15 @@
 
 def update_kernel(turns, factor_ref, rhs_ref, *rest):
     out_ref = rest[-1]
-    depth = rest[0].shape[0]
+    width = out_ref.shape[2]
+    depth = 2 * width
     rows = factor_ref.shape[1]
-    width = out_ref.shape[2]
     y = lax.axis_index("y")
     core = lax.axis_index("core")
     for j, block_ref in enumerate(rest[:-1]):
         place = jnp.bitwise_xor(y, turns[j // 2]) * 2 + jnp.bitwise_xor(core, j % 2)
         columns = pl.ds(pl.multiple_of(place * depth, depth), depth)
-        straight = block_ref[...]
+        straight = block_ref[:depth, :]
         crossed = jnp.concatenate([-straight[:, width:], straight[:, :width]], axis=1)
         base = rhs_ref if j == 0 else out_ref
         for at in range(0, rows, CHUNK):
@@ -98,7 +108,7 @@
 
 
 def update(turns, factor_slab, rhs, blocks, name):
-    depth = blocks[0].shape[0]
+    depth = 2 * rhs.shape[2]
     rows = factor_slab.shape[1]
     vmem = pl.BlockSpec(memory_space=pltpu.VMEM)
     return pl.pallas_call(
@@ -143,7 +153,6 @@
         ],
         axis=1,
     )
-    beside = {k: flipped(block, k) for k in TURNS[1:]}
     twin = swapped(block)
     modes_block = gathered[:, 2 * own : 3 * own].reshape(peers * own, width)
     share = gathered[:, 3 * own : 4 * own].astype(F32) + gathered[:, 4 * own :].astype(F32)
@@ -153,17 +162,21 @@
     share = share.reshape(2, width, width) + jnp.stack([latest[:, :width], latest[:, width:]])
     mine = lax.dynamic_index_in_dim(share, core, 0, keepdims=False)
     other = lax.dynamic_index_in_dim(share, 1 - core, 0, keepdims=False)
-    half = mine + swapped(other)
-    half, beside[1] = lax.optimization_barrier((half, beside[1]))
-    half = (half + flipped(half, 2)) + (flipped(half, 1) + flipped(half, 3))
+    half = split(mine + swapped(other))
+    sent = jnp.concatenate([block, half], axis=0)
+    came = [flipped(sent, k) for k in TURNS[1:]]
+    started = update(TURNS[:1], factor_slab, pending_rhs, [block, twin], "update_own")
+    started, came = lax.optimization_barrier((started, came))
+    depth = block.shape[0]
+    twins = [swapped(c[:depth]) for c in came]
+    first, third, second = (joined(c[depth:]) for c in came)
+    half = (joined(half) + second) + (first + third)
     back = swapped(half)
-    started = update(TURNS[:1], factor_slab, pending_rhs, [block, twin], "update_own")
-    twins = {k: swapped(beside[k]) for k in TURNS[1:]}
     updated_rhs = update(
         TURNS[1:],
         factor_slab,
         started,
-        [b for k in TURNS[1:] for b in (beside[k], twins[k])],
+        [b for two in zip(came, twins) for b in two],
         "update_rest",
     )
     modal_forces = jnp.stack(

time: 77.6 us -> 70.9 us (0.914)
  starting transfers between devices: 21.5 us -> 16.1 us
  waiting for transfers between devices: 19.3 us -> 17.9 us
    ppermute x6 -> x3, starting transfers between devices: 7.99 us -> 4 us  [flipped(): return lax.ppermute(value, 'y', [(i, i ^ bits) for i in range(4)])]
    ppermute x6 -> x3, waiting for transfers between devices: 8.05 us -> 4.21 us  [flipped(): return lax.ppermute(value, 'y', [(i, i ^ bits) for i in range(4)])]
    ppermute x6, waiting for transfers between devices: 0.02 us -> 2.45 us  [swapped(): return lax.ppermute(value, 'core', SWAP)]
    ppermute x6, starting transfers between devices: 8.53 us -> 7.12 us  [swapped(): return lax.ppermute(value, 'core', SWAP)]
  transfers between devices with their start and end apart: 13 -> 10, of which waited for: 3 -> 8; matrix products, arithmetic and copies ran while one was open for 2% -> 2% of each run, Pallas kernels for 1% -> 1%
where the time goes in v5:
time: 70.9 us; the launch traced here: 70.5 us
  blocking collectives  25.7 us (36%)
  waiting for transfers between devices  17.9 us (25%)
  starting transfers between devices  16.1 us (23%)
  Pallas kernels  4.7 us (7%)
  local copies, waits for them, and re-layouts  3.63 us (5%)
  other arithmetic  1.54 us (2%)
  between operations  0.78 us (1%)
    all_to_all x1, blocking collectives, on_device(): summed = jnp.sum(lax.all_to_all(outgoing, COL, 0, 0, tiled=True), axis=0)  25.7 us
    all_to_all x1, waiting for transfers between devices, on_device(): lax.all_to_all(jnp.broadcast_to(packed[None], (peers, rows, width)), COL,...  11.2 us
    ppermute x6, starting transfers between devices, swapped(): return lax.ppermute(value, 'core', SWAP)  7.12 us
    all_to_all x1, starting transfers between devices, on_device(): lax.all_to_all(jnp.broadcast_to(packed[None], (peers, rows, width)), COL,...  5 us
    ppermute x3, waiting for transfers between devices, flipped(): return lax.ppermute(value, 'y', [(i, i ^ bits) for i in range(4)])  4.21 us
    ppermute x3, starting transfers between devices, flipped(): return lax.ppermute(value, 'y', [(i, i ^ bits) for i in range(4)])  4 us
    ppermute x6, waiting for transfers between devices, swapped(): return lax.ppermute(value, 'core', SWAP)  2.45 us
    pallas_call x1, Pallas kernels, first_partials(): pl.pallas_call(first_kernel, out_shape=jax.ShapeDtypeStruct((peers, 3 * o...  2.42 us
  transfers between devices with their start and end apart: 10, of which 8 were waited for; matrix products, arithmetic and copies ran while one was open for 2% of the time, Pallas kernels for 1%

profile of v5, /device:TPU:1, one launch (start us, length us, event | category | flops | bytes accessed | tf_op | source)
XLA Modules:
  0.0 70.5 jit_solution(3305577768057055798)
XLA Ops:
  0.6 0.0 copy-start.1
  0.6 2.4 %partials.1 = f32[32,24,128]{2,1,0:T(8,128)} custom-call(f32[2,64,256]{2,1,0:T(8,128)} %bitcast.30, f32[2,64,128]{2,1,0:T(8,128)} %rhs_hbm.1, bf16[256,128]{1,0:T(8,128)(2,1)} %modes_hbm.1, bf16[2,256,128]{2,1,0:T(8,128)(2,1)} %solved_hbm.1), custom_call_target="tpu_custom_call" | custom-call | tf_op jit(solution)/shard_map/partials/pallas_call | solution.py:78
  3.1 25.7 %all_to_all.10 = f32[32,24,128]{2,1,0:T(8,128)S(1)} all-to-all(f32[32,24,128]{2,1,0:T(8,128)} %partials.1), channel_id=1, replica_groups=mesh['y'=4,'core'=2,'z'=8,'x'=4] {'z','x'}, dimensions={0} | all-to-all | bytes 786432 | tf_op jit(solution)/shard_map/all_to_all | solution.py:137
  28.8 0.7 pad_maximum_fusion.2
  29.5 0.8 %broadcast_in_dim.2 = bf16[32,40,128]{2,1,0:T(8,128)(2,1)} broadcast(bf16[40,128]{1,0:T(8,128)(2,1)S(1)} %pad_maximum_fusion.2), dimensions={1,2} | broadcast | bytes 337920 | tf_op jit(solution)/shard_map/broadcast_in_dim | solution.py:147
  30.3 5.0 %all-to-all-start.1 = ((bf16[32,40,128]{2,1,0:T(8,128)(2,1)}), bf16[32,40,128]{2,1,0:T(8,128)(2,1)S(1)}, u32[]{:S(2)}, u32[]{:S(2)}) async-start(bf16[32,40,128]{2,1,0:T(8,128)(2,1)} %broadcast_in_dim.2), calls=%async_computation.1 | async-start | bytes 655360 | tf_op jit(solution)/shard_map/all_to_all | solution.py:146
  35.3 11.2 %all-to-all-done.1 = bf16[32,40,128]{2,1,0:T(8,128)(2,1)S(1)} async-done(((bf16[32,40,128]{2,1,0:T(8,128)(2,1)}), bf16[32,40,128]{2,1,0:T(8,128)(2,1)S(1)}, u32[]{:S(2)}, u32[]{:S(2)}) %all-to-all-start.1) | async-done | bytes 327712 | tf_op jit(solution)/shard_map/all_to_all | solution.py:146
  46.5 0.2 fusion.1
  46.8 4.1 %collective-permute-start.1 = (f32[128,128]{1,0:T(8,128)S(1)}, f32[128,128]{1,0:T(8,128)S(1)}, u32[]{:S(2)}, u32[]{:S(2)}) collective-permute-start(f32[128,128]{1,0:T(8,128)S(1)} %dynamic-slice_bitcast_fusion), channel_id=1, source_target_pairs={{0,32},{32,0},{1,33},{33,1},{2,34},{34,2},{3,35},{35,3},{4,36},{36... | collective-permute-start | bytes 196616 | tf_op jit(solution)/shard_map/ppermute | solution.py:19
  50.9 0.9 %collective-permute-done.1 = f32[128,128]{1,0:T(8,128)S(1)} collective-permute-done((f32[128,128]{1,0:T(8,128)S(1)}, f32[128,128]{1,0:T(8,128)S(1)}, u32[]{:S(2)}, u32[]{:S(2)}) %collective-permute-start.1) | collective-permute-done | bytes 65568 | tf_op jit(solution)/shard_map/ppermute | solution.py:19
  51.9 1.4 %collective-permute-start.2 = (bf16[384,256]{1,0:T(8,128)(2,1)S(1)}, bf16[384,256]{1,0:T(8,128)(2,1)S(1)}, u32[]{:S(2)}, u32[]{:S(2)}) collective-permute-start(bf16[384,256]{1,0:T(8,128)(2,1)S(1)} %maximum_maximum_fusion), channel_id=1, source_target_pairs={{0,64},{64,0},{128,192},{192,128},{1,65},{65,1},{129,193},{193,129... | collective-permute-start | bytes 589832 | tf_op jit(solution)/shard_map/ppermute | solution.py:23
  53.2 1.9 %collective-permute-start.3 = (bf16[384,256]{1,0:T(8,128)(2,1)S(1)}, bf16[384,256]{1,0:T(8,128)(2,1)S(1)}, u32[]{:S(2)}, u32[]{:S(2)}) collective-permute-start(bf16[384,256]{1,0:T(8,128)(2,1)S(1)} %maximum_maximum_fusion), channel_id=1, source_target_pairs={{0,192},{64,128},{128,64},{192,0},{1,193},{65,129},{129,65},{193,1... | collective-permute-start | bytes 589832 | tf_op jit(solution)/shard_map/ppermute | solution.py:23
  55.2 0.7 %collective-permute-start.4 = (bf16[384,256]{1,0:T(8,128)(2,1)S(1)}, bf16[384,256]{1,0:T(8,128)(2,1)S(1)}, u32[]{:S(2)}, u32[]{:S(2)}) collective-permute-start(bf16[384,256]{1,0:T(8,128)(2,1)S(1)} %maximum_maximum_fusion), channel_id=1, source_target_pairs={{0,128},{64,192},{128,0},{192,64},{1,129},{65,193},{129,1},{193,65... | collective-permute-start | bytes 589832 | tf_op jit(solution)/shard_map/ppermute | solution.py:23
  55.9 1.0 %collective-permute-start = (bf16[256,256]{1,0:T(8,128)(2,1)S(1)}, bf16[256,256]{1,0:T(8,128)(2,1)S(1)}, u32[]{:S(2)}, u32[]{:S(2)}) collective-permute-start(bf16[256,256]{1,0:T(8,128)(2,1)S(1)} %pad_maximum_fusion.rest_0_), channel_id=1, source_target_pairs={{0,32},{32,0},{1,33},{33,1},{2,34},{34,2},{3,35},{35,3},{4,36},{36... | collective-permute-start | bytes 393224 | tf_op jit(solution)/shard_map/ppermute | solution.py:19
  56.9 1.0 %collective-permute-done.rest_1_ = bf16[256,256]{1,0:T(8,128)(2,1)S(1)} collective-permute-done((bf16[256,256]{1,0:T(8,128)(2,1)S(1)}, bf16[256,256]{1,0:T(8,128)(2,1)S(1)}, u32[]{:S(2)}, u32[]{:S(2)}) %collective-permute-start) | collective-permute-done | bytes 131104 | tf_op jit(solution)/shard_map/ppermute | solution.py:19
  57.9 0.0 copy-done.1
  57.9 0.0 copy-start
  57.9 2.2 %copy-done = bf16[2,512,2048]{2,1,0:T(8,128)(2,1)S(1)} copy-done((bf16[2,512,2048]{2,1,0:T(8,128)(2,1)S(1)}, bf16[2,512,2048]{2,1,0:T(8,128)(2,1)}, u32[]{:S(2)}) %copy-start) | copy-done | bytes 4194328
  60.1 0.5 update_own.1.rhs_ref
  60.5 0.0 collective-permute-done.2.rest_0_
  60.5 2.3 %collective-permute-done.3.rest_2_ = bf16[384,256]{1,0:T(8,128)(2,1)S(1)} collective-permute-done((bf16[384,256]{1,0:T(8,128)(2,1)S(1)}, bf16[384,256]{1,0:T(8,128)(2,1)S(1)}, u32[]{:S(2)}, u32[]{:S(2)}) %collective-permute-start.3) | collective-permute-done | bytes 196640 | tf_op jit(solution)/shard_map/ppermute | solution.py:23
  62.8 1.9 %collective-permute-done.4.rest_4_ = bf16[384,256]{1,0:T(8,128)(2,1)S(1)} collective-permute-done((bf16[384,256]{1,0:T(8,128)(2,1)S(1)}, bf16[384,256]{1,0:T(8,128)(2,1)S(1)}, u32[]{:S(2)}, u32[]{:S(2)}) %collective-permute-start.4) | collective-permute-done | bytes 196640 | tf_op jit(solution)/shard_map/ppermute | solution.py:23
  64.8 1.3 %collective-permute-start.8 = (f32[128,128]{1,0:T(8,128)S(1)}, f32[128,128]{1,0:T(8,128)S(1)}, u32[]{:S(2)}, u32[]{:S(2)}) collective-permute-start(f32[128,128]{1,0:T(8,128)S(1)} %add_add_fusion), channel_id=1, source_target_pairs={{0,32},{32,0},{1,33},{33,1},{2,34},{34,2},{3,35},{35,3},{4,36},{36... | collective-permute-start | bytes 196616 | tf_op jit(solution)/shard_map/ppermute | solution.py:19
  66.1 0.6 slice_bitcast_fusion.6
  66.8 0.1 collective-permute-start.5
  66.9 0.5 collective-permute-start.6
  67.4 0.1 collective-permute-start.7
  67.5 0.0 collective-permute-done.8
  67.5 0.7 pad_maximum_fusion.1
  68.1 0.1 collective-permute-done.5.rest_1_
  68.2 0.2 collective-permute-done.6.rest_3_
  68.4 0.3 collective-permute-done.7.rest_5_
  68.7 1.8 %update_rest.1 = f32[2,512,128]{2,1,0:T(8,128)} custom-call(bf16[2,512,2048]{2,1,0:T(8,128)(2,1)S(1)} %copy-done, f32[2,512,128]{2,1,0:T(8,128)S(1)} %update_own.1.rhs_ref, bf16[384,256]{1,0:T(8,128)(2,1)S(1)} %collective-permute-done.2.rest_0_, bf16[256,256]{1,0:T(8,128)(2,1)S(1)} %collective-permute-done.5.rest_1_, ...), custom_call_target="tpu_custom_call" | custom-call | flops 805306368 | bytes 3145728 | tf_op jit(solution)/shard_map/update_rest/pallas_call | solution.py:114
  (16 shorter events, 0.3 us)
Async XLA Ops:
  0.6 57.3 %copy-start.1 = (f32[2,512,128]{2,1,0:T(8,128)S(1)}, f32[2,512,128]{2,1,0:T(8,128)}, u32[]{:S(2)}) copy-start(f32[2,512,128]{2,1,0:T(8,128)} %rhs_ref.1) | copy-start | bytes 1572868
  30.3 16.2 %all-to-all-start.1 = ((bf16[32,40,128]{2,1,0:T(8,128)(2,1)}), bf16[32,40,128]{2,1,0:T(8,128)(2,1)S(1)}, u32[]{:S(2)}, u32[]{:S(2)}) async-start(bf16[32,40,128]{2,1,0:T(8,128)(2,1)} %broadcast_in_dim.2), calls=%async_computation.1 | async-start | bytes 655360 | tf_op jit(solution)/shard_map/all_to_all | solution.py:146
  46.8 5.0 %collective-permute-start.1 = (f32[128,128]{1,0:T(8,128)S(1)}, f32[128,128]{1,0:T(8,128)S(1)}, u32[]{:S(2)}, u32[]{:S(2)}) collective-permute-start(f32[128,128]{1,0:T(8,128)S(1)} %dynamic-slice_bitcast_fusion), channel_id=1, source_target_pairs={{0,32},{32,0},{1,33},{33,1},{2,34},{34,2},{3,35},{35,3},{4,36},{36... | collective-permute-start | bytes 196616 | tf_op jit(solution)/shard_map/ppermute | solution.py:19
  51.9 8.7 %collective-permute-start.2 = (bf16[384,256]{1,0:T(8,128)(2,1)S(1)}, bf16[384,256]{1,0:T(8,128)(2,1)S(1)}, u32[]{:S(2)}, u32[]{:S(2)}) collective-permute-start(bf16[384,256]{1,0:T(8,128)(2,1)S(1)} %maximum_maximum_fusion), channel_id=1, source_target_pairs={{0,64},{64,0},{128,192},{192,128},{1,65},{65,1},{129,193},{193,129... | collective-permute-start | bytes 589832 | tf_op jit(solution)/shard_map/ppermute | solution.py:23
  53.2 9.6 %collective-permute-start.3 = (bf16[384,256]{1,0:T(8,128)(2,1)S(1)}, bf16[384,256]{1,0:T(8,128)(2,1)S(1)}, u32[]{:S(2)}, u32[]{:S(2)}) collective-permute-start(bf16[384,256]{1,0:T(8,128)(2,1)S(1)} %maximum_maximum_fusion), channel_id=1, source_target_pairs={{0,192},{64,128},{128,64},{192,0},{1,193},{65,129},{129,65},{193,1... | collective-permute-start | bytes 589832 | tf_op jit(solution)/shard_map/ppermute | solution.py:23
  55.2 9.6 %collective-permute-start.4 = (bf16[384,256]{1,0:T(8,128)(2,1)S(1)}, bf16[384,256]{1,0:T(8,128)(2,1)S(1)}, u32[]{:S(2)}, u32[]{:S(2)}) collective-permute-start(bf16[384,256]{1,0:T(8,128)(2,1)S(1)} %maximum_maximum_fusion), channel_id=1, source_target_pairs={{0,128},{64,192},{128,0},{192,64},{1,129},{65,193},{129,1},{193,65... | collective-permute-start | bytes 589832 | tf_op jit(solution)/shard_map/ppermute | solution.py:23
  55.9 2.0 %collective-permute-start = (bf16[256,256]{1,0:T(8,128)(2,1)S(1)}, bf16[256,256]{1,0:T(8,128)(2,1)S(1)}, u32[]{:S(2)}, u32[]{:S(2)}) collective-permute-start(bf16[256,256]{1,0:T(8,128)(2,1)S(1)} %pad_maximum_fusion.rest_0_), channel_id=1, source_target_pairs={{0,32},{32,0},{1,33},{33,1},{2,34},{34,2},{3,35},{35,3},{4,36},{36... | collective-permute-start | bytes 393224 | tf_op jit(solution)/shard_map/ppermute | solution.py:19
  57.9 2.2 %copy-start = (bf16[2,512,2048]{2,1,0:T(8,128)(2,1)S(1)}, bf16[2,512,2048]{2,1,0:T(8,128)(2,1)}, u32[]{:S(2)}) copy-start(bf16[2,512,2048]{2,1,0:T(8,128)(2,1)} %factor_ref.3) | copy-start | bytes 12582916
  64.8 2.7 %collective-permute-start.8 = (f32[128,128]{1,0:T(8,128)S(1)}, f32[128,128]{1,0:T(8,128)S(1)}, u32[]{:S(2)}, u32[]{:S(2)}) collective-permute-start(f32[128,128]{1,0:T(8,128)S(1)} %add_add_fusion), channel_id=1, source_target_pairs={{0,32},{32,0},{1,33},{33,1},{2,34},{34,2},{3,35},{35,3},{4,36},{36... | collective-permute-start | bytes 196616 | tf_op jit(solution)/shard_map/ppermute | solution.py:19
  66.8 1.4 %collective-permute-start.5 = (bf16[256,256]{1,0:T(8,128)(2,1)S(1)}, bf16[256,256]{1,0:T(8,128)(2,1)S(1)}, u32[]{:S(2)}, u32[]{:S(2)}) collective-permute-start(bf16[256,256]{1,0:T(8,128)(2,1)S(1)} %slice.73), channel_id=1, source_target_pairs={{0,32},{32,0},{1,33},{33,1},{2,34},{34,2},{3,35},{35,3},{4,36},{36... | collective-permute-start | bytes 393224 | tf_op jit(solution)/shard_map/ppermute | solution.py:19
  66.9 1.5 %collective-permute-start.6 = (bf16[256,256]{1,0:T(8,128)(2,1)S(1)}, bf16[256,256]{1,0:T(8,128)(2,1)S(1)}, u32[]{:S(2)}, u32[]{:S(2)}) collective-permute-start(bf16[256,256]{1,0:T(8,128)(2,1)S(1)} %slice.74), channel_id=1, source_target_pairs={{0,32},{32,0},{1,33},{33,1},{2,34},{34,2},{3,35},{35,3},{4,36},{36... | collective-permute-start | bytes 393224 | tf_op jit(solution)/shard_map/ppermute | solution.py:19
  67.4 1.3 %collective-permute-start.7 = (bf16[256,256]{1,0:T(8,128)(2,1)S(1)}, bf16[256,256]{1,0:T(8,128)(2,1)S(1)}, u32[]{:S(2)}, u32[]{:S(2)}) collective-permute-start(bf16[256,256]{1,0:T(8,128)(2,1)S(1)} %slice.75), channel_id=1, source_target_pairs={{0,32},{32,0},{1,33},{33,1},{2,34},{34,2},{3,35},{35,3},{4,36},{36... | collective-permute-start | bytes 393224 | tf_op jit(solution)/shard_map/ppermute | solution.py:19

commit v6 on v5

--- a/solution.py
+++ b/solution.py
@@ -12,6 +12,8 @@
 COL = ("z", "x")
 SWAP = [(0, 1), (1, 0)]
 CHUNK = 128
+GRANT = 50 << 20
+PACK_FLOPS = 1_000_000
 TURNS = (0, 1, 3, 2)
 
 
@@ -86,23 +88,69 @@
     )(*args)
 
 
-def update_kernel(turns, factor_ref, rhs_ref, *rest):
-    out_ref = rest[-1]
+def pack_kernel(came_ref, modes_ref, panel_ref, packed_ref):
+    own = modes_ref.shape[0]
+    summed = jnp.sum(came_ref[...], axis=0)
+    panel_ref[0] = summed[:own]
+    panel_ref[1] = summed[own : 2 * own]
+    share = summed[2 * own :]
+    high = share.astype(BF16).astype(F32)
+    rows = jnp.concatenate(
+        [summed[: 2 * own], modes_ref[...].astype(F32), high, share - high], axis=0
+    )
+    packed_ref[...] = jnp.broadcast_to(rows.astype(BF16)[None], packed_ref.shape)
+
+
+def pack(came, modes_panel):
+    peers, rows, width = came.shape
+    own = rows // 3
+    vmem = pl.BlockSpec(memory_space=pltpu.VMEM)
+    return pl.pallas_call(
+        pack_kernel,
+        out_shape=(
+            jax.ShapeDtypeStruct((2, own, width), F32),
+            jax.ShapeDtypeStruct((peers, 5 * own, width), BF16),
+        ),
+        in_specs=[vmem] * 2,
+        out_specs=(vmem, vmem),
+        cost_estimate=pl.CostEstimate(
+            flops=PACK_FLOPS, bytes_accessed=came.size * 4, transcendentals=0
+        ),
+        compiler_params=pltpu.CompilerParams(vmem_limit_bytes=24 << 20),
+        name="pack",
+    )(came, modes_panel)
+
+
+def update_kernel(turns, factor_hbm, rhs_ref, *rest):
+    count = 2 * len(turns)
+    blocks, (out_ref, held, sems) = rest[:count], rest[count:]
     width = out_ref.shape[2]
     depth = 2 * width
-    rows = factor_ref.shape[1]
+    rows = held.shape[2]
     y = lax.axis_index("y")
     core = lax.axis_index("core")
-    for j, block_ref in enumerate(rest[:-1]):
+    moves = []
+    for j in range(count):
         place = jnp.bitwise_xor(y, turns[j // 2]) * 2 + jnp.bitwise_xor(core, j % 2)
         columns = pl.ds(pl.multiple_of(place * depth, depth), depth)
+        for c in range(2):
+            moves.append(
+                pltpu.make_async_copy(
+                    factor_hbm.at[c, :, columns], held.at[j, c], sems.at[j, c]
+                )
+            )
+    for move in moves:
+        move.start()
+    for j, block_ref in enumerate(blocks):
         straight = block_ref[:depth, :]
         crossed = jnp.concatenate([-straight[:, width:], straight[:, :width]], axis=1)
         base = rhs_ref if j == 0 else out_ref
+        moves[2 * j].wait()
+        moves[2 * j + 1].wait()
         for at in range(0, rows, CHUNK):
             span = slice(at, at + CHUNK)
-            product = jnp.dot(factor_ref[0, span, columns], straight, preferred_element_type=F32)
-            product += jnp.dot(factor_ref[1, span, columns], crossed, preferred_element_type=F32)
+            product = jnp.dot(held[j, 0, span, :], straight, preferred_element_type=F32)
+            product += jnp.dot(held[j, 1, span, :], crossed, preferred_element_type=F32)
             out_ref[0, span, :] = base[0, span, :] - product[:, :width]
             out_ref[1, span, :] = base[1, span, :] - product[:, width:]
 
@@ -110,18 +158,23 @@
 def update(turns, factor_slab, rhs, blocks, name):
     depth = 2 * rhs.shape[2]
     rows = factor_slab.shape[1]
+    count = len(blocks)
     vmem = pl.BlockSpec(memory_space=pltpu.VMEM)
     return pl.pallas_call(
         functools.partial(update_kernel, turns),
         out_shape=jax.ShapeDtypeStruct(rhs.shape, F32),
-        in_specs=[vmem] * (2 + len(blocks)),
+        in_specs=[pl.BlockSpec(memory_space=pl.ANY)] + [vmem] * (1 + count),
         out_specs=vmem,
+        scratch_shapes=[
+            pltpu.VMEM((count, 2, rows, depth), BF16),
+            pltpu.SemaphoreType.DMA((count, 2)),
+        ],
         cost_estimate=pl.CostEstimate(
-            flops=len(blocks) * 4 * rows * depth * 2 * rhs.shape[2],
-            bytes_accessed=len(blocks) * 4 * rows * depth,
+            flops=count * 4 * rows * depth * 2 * rhs.shape[2],
+            bytes_accessed=count * 4 * rows * depth,
             transcendentals=0,
         ),
-        compiler_params=pltpu.CompilerParams(vmem_limit_bytes=24 << 20),
+        compiler_params=pltpu.CompilerParams(vmem_limit_bytes=GRANT),
         name=name,
     )(factor_slab, rhs, *blocks)
 
@@ -134,18 +187,9 @@
     peers = diag_inverse.shape[1] // own
     core = lax.axis_index("core")
     outgoing = first_partials(diag_inverse, panel_rhs, modes_prev, solved_prev, peers, own)
-    summed = jnp.sum(lax.all_to_all(outgoing, COL, 0, 0, tiled=True), axis=0)
-    panel_solution = summed[: 2 * own].reshape(2, own, width)
-    share = summed[2 * own :]
-    high = lax.reduce_precision(share, 8, 7)
-    low = share - high
-    packed = jnp.concatenate(
-        [summed[: 2 * own].astype(BF16), modes_panel, high.astype(BF16), low.astype(BF16)], axis=0
-    )
-    rows = packed.shape[0]
-    gathered = lax.all_to_all(
-        jnp.broadcast_to(packed[None], (peers, rows, width)), COL, 0, 0, tiled=True
-    )
+    came = lax.all_to_all(outgoing, COL, 0, 0, tiled=True)
+    panel_solution, packed = pack(came, modes_panel)
+    gathered = lax.all_to_all(packed, COL, 0, 0, tiled=True)
     block = jnp.concatenate(
         [
             gathered[:, :own].reshape(peers * own, width),

time: 70.9 us -> 72.2 us (1.018)
  Pallas kernels: 4.7 us -> 8.73 us
  local copies, waits for them, and re-layouts: 3.63 us -> 0.76 us
  waiting for transfers between devices: 17.9 us -> 18.8 us
  other arithmetic: 1.54 us -> 0.81 us
    pallas_call x2, Pallas kernels: 2.28 us -> 5.53 us  [update(): pl.pallas_call(functools.partial(update_kernel, turns), out_shape=jax.Sha...]
    unnamed x4, local copies, waits for them, and re-layouts: 2.19 us -> 0.69 us
    ppermute x3, waiting for transfers between devices: 4.21 us -> 5.15 us  [flipped(): return lax.ppermute(value, 'y', [(i, i ^ bits) for i in range(4)])]
    pallas_call x0 -> x1, Pallas kernels: none -> 0.78 us  [pack(): pl.pallas_call(pack_kernel, out_shape=(jax.ShapeDtypeStruct((2, own, widt...]
    broadcast_in_dim x1 -> x0, local copies, waits for them, and re-layouts: 0.77 us -> none  [on_device(): jnp.broadcast_to(packed[None], (peers, rows, width))]
  transfers between devices with their start and end apart: 10 -> 10, of which waited for: 8 -> 8; matrix products, arithmetic and copies ran while one was open for 2% -> 1% of each run, Pallas kernels for 1% -> 2%
where the time goes in v6:
time: 72.2 us; the launch traced here: 71.9 us
  blocking collectives  25.7 us (36%)
  waiting for transfers between devices  18.8 us (26%)
  starting transfers between devices  16.1 us (22%)
  Pallas kernels  8.73 us (12%)
  other arithmetic  0.81 us (1%)
  local copies, waits for them, and re-layouts  0.76 us (1%)
  between operations  0.76 us (1%)
    all_to_all x1, blocking collectives, on_device(): came = lax.all_to_all(outgoing, COL, 0, 0, tiled=True)  25.7 us
    all_to_all x1, waiting for transfers between devices, on_device(): gathered = lax.all_to_all(packed, COL, 0, 0, tiled=True)  11.2 us
    ppermute x6, starting transfers between devices, swapped(): return lax.ppermute(value, 'core', SWAP)  7.12 us
    pallas_call x2, Pallas kernels, update(): pl.pallas_call(functools.partial(update_kernel, turns), out_shape=jax.Sha...  5.53 us
    ppermute x3, waiting for transfers between devices, flipped(): return lax.ppermute(value, 'y', [(i, i ^ bits) for i in range(4)])  5.15 us
    all_to_all x1, starting transfers between devices, on_device(): gathered = lax.all_to_all(packed, COL, 0, 0, tiled=True)  5 us
    ppermute x3, starting transfers between devices, flipped(): return lax.ppermute(value, 'y', [(i, i ^ bits) for i in range(4)])  4 us
    ppermute x6, waiting for transfers between devices, swapped(): return lax.ppermute(value, 'core', SWAP)  2.45 us
  transfers between devices with their start and end apart: 10, of which 8 were waited for; matrix products, arithmetic and copies ran while one was open for 1% of the time, Pallas kernels for 2%

profile of v6, /device:TPU:1, one launch (start us, length us, event | category | flops | bytes accessed | tf_op | source)
XLA Modules:
  0.0 71.9 jit_solution(3678132898671171184)
XLA Ops:
  0.6 0.0 copy-start
  0.6 2.4 %partials.1 = f32[32,24,128]{2,1,0:T(8,128)} custom-call(f32[2,64,256]{2,1,0:T(8,128)} %bitcast.28, f32[2,64,128]{2,1,0:T(8,128)} %rhs_hbm.1, bf16[256,128]{1,0:T(8,128)(2,1)} %modes_hbm.1, bf16[2,256,128]{2,1,0:T(8,128)(2,1)} %solved_hbm.1), custom_call_target="tpu_custom_call" | custom-call | tf_op jit(solution)/shard_map/partials/pallas_call | solution.py:80
  3.1 25.7 %all_to_all.10.came_ref = f32[32,24,128]{2,1,0:T(8,128)S(1)} all-to-all(f32[32,24,128]{2,1,0:T(8,128)} %partials.1), channel_id=1, replica_groups=mesh['y'=4,'core'=2,'z'=8,'x'=4] {'z','x'}, dimensions={0} | all-to-all | bytes 786432 | tf_op jit(solution)/shard_map/all_to_all | solution.py:190
  28.8 0.0 copy-start.1
  28.8 0.7 copy-done.1
  29.4 0.8 %pack.1 = (f32[2,8,128]{2,1,0:T(8,128)}, bf16[32,40,128]{2,1,0:T(8,128)(2,1)}) custom-call(f32[32,24,128]{2,1,0:T(8,128)S(1)} %all_to_all.10.came_ref, bf16[8,128]{1,0:T(8,128)(2,1)S(1)} %copy-done.1), custom_call_target="tpu_custom_call" | custom-call | flops 1000000 | bytes 393216 | tf_op jit(solution)/shard_map/pack/pallas_call | solution.py:108
  30.2 5.0 %all-to-all-start.1 = ((bf16[32,40,128]{2,1,0:T(8,128)(2,1)}), bf16[32,40,128]{2,1,0:T(8,128)(2,1)S(1)}, u32[]{:S(2)}, u32[]{:S(2)}) async-start(bf16[32,40,128]{2,1,0:T(8,128)(2,1)} %get-tuple-element.10), calls=%async_computation.1 | async-start | bytes 655360 | tf_op jit(solution)/shard_map/all_to_all | solution.py:192
  35.2 11.2 %all-to-all-done.1 = bf16[32,40,128]{2,1,0:T(8,128)(2,1)S(1)} async-done(((bf16[32,40,128]{2,1,0:T(8,128)(2,1)}), bf16[32,40,128]{2,1,0:T(8,128)(2,1)S(1)}, u32[]{:S(2)}, u32[]{:S(2)}) %all-to-all-start.1) | async-done | bytes 327712 | tf_op jit(solution)/shard_map/all_to_all | solution.py:192
  46.5 0.2 fusion.1
  46.8 4.1 %collective-permute-start.1 = (f32[128,128]{1,0:T(8,128)S(1)}, f32[128,128]{1,0:T(8,128)S(1)}, u32[]{:S(2)}, u32[]{:S(2)}) collective-permute-start(f32[128,128]{1,0:T(8,128)S(1)} %dynamic-slice_bitcast_fusion), channel_id=1, source_target_pairs={{0,32},{32,0},{1,33},{33,1},{2,34},{34,2},{3,35},{35,3},{4,36},{36... | collective-permute-start | bytes 196616 | tf_op jit(solution)/shard_map/ppermute | solution.py:21
  50.9 0.9 %collective-permute-done.1 = f32[128,128]{1,0:T(8,128)S(1)} collective-permute-done((f32[128,128]{1,0:T(8,128)S(1)}, f32[128,128]{1,0:T(8,128)S(1)}, u32[]{:S(2)}, u32[]{:S(2)}) %collective-permute-start.1) | collective-permute-done | bytes 65568 | tf_op jit(solution)/shard_map/ppermute | solution.py:21
  51.8 1.4 %collective-permute-start.2 = (bf16[384,256]{1,0:T(8,128)(2,1)S(1)}, bf16[384,256]{1,0:T(8,128)(2,1)S(1)}, u32[]{:S(2)}, u32[]{:S(2)}) collective-permute-start(bf16[384,256]{1,0:T(8,128)(2,1)S(1)} %maximum_maximum_fusion), channel_id=1, source_target_pairs={{0,64},{64,0},{128,192},{192,128},{1,65},{65,1},{129,193},{193,129... | collective-permute-start | bytes 589832 | tf_op jit(solution)/shard_map/ppermute | solution.py:25
  53.2 1.9 %collective-permute-start.3 = (bf16[384,256]{1,0:T(8,128)(2,1)S(1)}, bf16[384,256]{1,0:T(8,128)(2,1)S(1)}, u32[]{:S(2)}, u32[]{:S(2)}) collective-permute-start(bf16[384,256]{1,0:T(8,128)(2,1)S(1)} %maximum_maximum_fusion), channel_id=1, source_target_pairs={{0,192},{64,128},{128,64},{192,0},{1,193},{65,129},{129,65},{193,1... | collective-permute-start | bytes 589832 | tf_op jit(solution)/shard_map/ppermute | solution.py:25
  55.1 0.7 %collective-permute-start.4 = (bf16[384,256]{1,0:T(8,128)(2,1)S(1)}, bf16[384,256]{1,0:T(8,128)(2,1)S(1)}, u32[]{:S(2)}, u32[]{:S(2)}) collective-permute-start(bf16[384,256]{1,0:T(8,128)(2,1)S(1)} %maximum_maximum_fusion), channel_id=1, source_target_pairs={{0,128},{64,192},{128,0},{192,64},{1,129},{65,193},{129,1},{193,65... | collective-permute-start | bytes 589832 | tf_op jit(solution)/shard_map/ppermute | solution.py:25
  55.8 1.0 %collective-permute-start = (bf16[256,256]{1,0:T(8,128)(2,1)S(1)}, bf16[256,256]{1,0:T(8,128)(2,1)S(1)}, u32[]{:S(2)}, u32[]{:S(2)}) collective-permute-start(bf16[256,256]{1,0:T(8,128)(2,1)S(1)} %pad_maximum_fusion.rest_0_), channel_id=1, source_target_pairs={{0,32},{32,0},{1,33},{33,1},{2,34},{34,2},{3,35},{35,3},{4,36},{36... | collective-permute-start | bytes 393224 | tf_op jit(solution)/shard_map/ppermute | solution.py:21
  56.8 1.0 %collective-permute-done.rest_1_ = bf16[256,256]{1,0:T(8,128)(2,1)S(1)} collective-permute-done((bf16[256,256]{1,0:T(8,128)(2,1)S(1)}, bf16[256,256]{1,0:T(8,128)(2,1)S(1)}, u32[]{:S(2)}, u32[]{:S(2)}) %collective-permute-start) | collective-permute-done | bytes 131104 | tf_op jit(solution)/shard_map/ppermute | solution.py:21
  57.8 0.0 copy-done
  57.8 1.7 %update_own.1.rhs_ref = f32[2,512,128]{2,1,0:T(8,128)S(1)} custom-call(bf16[2,512,2048]{2,1,0:T(8,128)(2,1)} %factor_hbm.3, f32[2,512,128]{2,1,0:T(8,128)S(1)} %copy-done, bf16[256,256]{1,0:T(8,128)(2,1)S(1)} %pad_maximum_fusion.rest_0_, bf16[256,256]{1,0:T(8,128)(2,1)S(1)} %collective-permute-done.rest_1_), custom_call_target="tpu_custom_call" | custom-call | flops 268435456 | bytes 1048576 | tf_op jit(solution)/shard_map/update_own/pallas_call | solution.py:163
  59.5 0.0 collective-permute-done.2.rest_0_
  59.5 3.2 %collective-permute-done.3.rest_2_ = bf16[384,256]{1,0:T(8,128)(2,1)S(1)} collective-permute-done((bf16[384,256]{1,0:T(8,128)(2,1)S(1)}, bf16[384,256]{1,0:T(8,128)(2,1)S(1)}, u32[]{:S(2)}, u32[]{:S(2)}) %collective-permute-start.3) | collective-permute-done | bytes 196640 | tf_op jit(solution)/shard_map/ppermute | solution.py:25
  62.8 1.9 %collective-permute-done.4.rest_4_ = bf16[384,256]{1,0:T(8,128)(2,1)S(1)} collective-permute-done((bf16[384,256]{1,0:T(8,128)(2,1)S(1)}, bf16[384,256]{1,0:T(8,128)(2,1)S(1)}, u32[]{:S(2)}, u32[]{:S(2)}) %collective-permute-start.4) | collective-permute-done | bytes 196640 | tf_op jit(solution)/shard_map/ppermute | solution.py:25
  64.7 1.3 %collective-permute-start.8 = (f32[128,128]{1,0:T(8,128)S(1)}, f32[128,128]{1,0:T(8,128)S(1)}, u32[]{:S(2)}, u32[]{:S(2)}) collective-permute-start(f32[128,128]{1,0:T(8,128)S(1)} %add_add_fusion), channel_id=1, source_target_pairs={{0,32},{32,0},{1,33},{33,1},{2,34},{34,2},{3,35},{35,3},{4,36},{36... | collective-permute-start | bytes 196616 | tf_op jit(solution)/shard_map/ppermute | solution.py:21
  66.1 0.1 collective-permute-start.5
  66.2 0.5 collective-permute-start.6
  66.7 0.1 collective-permute-start.7
  66.8 0.2 collective-permute-done.8
  67.0 0.7 pad_maximum_fusion.1
  67.6 0.0 collective-permute-done.5.rest_1_
  67.7 0.1 collective-permute-done.6.rest_3_
  67.7 0.3 collective-permute-done.7.rest_5_
  68.1 3.8 %update_rest.1 = f32[2,512,128]{2,1,0:T(8,128)} custom-call(bf16[2,512,2048]{2,1,0:T(8,128)(2,1)} %factor_hbm.3, f32[2,512,128]{2,1,0:T(8,128)S(1)} %update_own.1.rhs_ref, bf16[384,256]{1,0:T(8,128)(2,1)S(1)} %collective-permute-done.2.rest_0_, bf16[256,256]{1,0:T(8,128)(2,1)S(1)} %collective-permute-done.5.rest_1_, ...), custom_call_target="tpu_custom_call" | custom-call | flops 805306368 | bytes 3145728 | tf_op jit(solution)/shard_map/update_rest/pallas_call | solution.py:163
  (13 shorter events, 0.2 us)
Async XLA Ops:
  0.6 57.2 %copy-start = (f32[2,512,128]{2,1,0:T(8,128)S(1)}, f32[2,512,128]{2,1,0:T(8,128)}, u32[]{:S(2)}) copy-start(f32[2,512,128]{2,1,0:T(8,128)} %rhs_ref.1) | copy-start | bytes 1572868
  28.8 0.7 copy-start.1
  30.2 16.2 %all-to-all-start.1 = ((bf16[32,40,128]{2,1,0:T(8,128)(2,1)}), bf16[32,40,128]{2,1,0:T(8,128)(2,1)S(1)}, u32[]{:S(2)}, u32[]{:S(2)}) async-start(bf16[32,40,128]{2,1,0:T(8,128)(2,1)} %get-tuple-element.10), calls=%async_computation.1 | async-start | bytes 655360 | tf_op jit(solution)/shard_map/all_to_all | solution.py:192
  46.8 5.0 %collective-permute-start.1 = (f32[128,128]{1,0:T(8,128)S(1)}, f32[128,128]{1,0:T(8,128)S(1)}, u32[]{:S(2)}, u32[]{:S(2)}) collective-permute-start(f32[128,128]{1,0:T(8,128)S(1)} %dynamic-slice_bitcast_fusion), channel_id=1, source_target_pairs={{0,32},{32,0},{1,33},{33,1},{2,34},{34,2},{3,35},{35,3},{4,36},{36... | collective-permute-start | bytes 196616 | tf_op jit(solution)/shard_map/ppermute | solution.py:21
  51.8 7.7 %collective-permute-start.2 = (bf16[384,256]{1,0:T(8,128)(2,1)S(1)}, bf16[384,256]{1,0:T(8,128)(2,1)S(1)}, u32[]{:S(2)}, u32[]{:S(2)}) collective-permute-start(bf16[384,256]{1,0:T(8,128)(2,1)S(1)} %maximum_maximum_fusion), channel_id=1, source_target_pairs={{0,64},{64,0},{128,192},{192,128},{1,65},{65,1},{129,193},{193,129... | collective-permute-start | bytes 589832 | tf_op jit(solution)/shard_map/ppermute | solution.py:25
  53.2 9.6 %collective-permute-start.3 = (bf16[384,256]{1,0:T(8,128)(2,1)S(1)}, bf16[384,256]{1,0:T(8,128)(2,1)S(1)}, u32[]{:S(2)}, u32[]{:S(2)}) collective-permute-start(bf16[384,256]{1,0:T(8,128)(2,1)S(1)} %maximum_maximum_fusion), channel_id=1, source_target_pairs={{0,192},{64,128},{128,64},{192,0},{1,193},{65,129},{129,65},{193,1... | collective-permute-start | bytes 589832 | tf_op jit(solution)/shard_map/ppermute | solution.py:25
  55.1 9.6 %collective-permute-start.4 = (bf16[384,256]{1,0:T(8,128)(2,1)S(1)}, bf16[384,256]{1,0:T(8,128)(2,1)S(1)}, u32[]{:S(2)}, u32[]{:S(2)}) collective-permute-start(bf16[384,256]{1,0:T(8,128)(2,1)S(1)} %maximum_maximum_fusion), channel_id=1, source_target_pairs={{0,128},{64,192},{128,0},{192,64},{1,129},{65,193},{129,1},{193,65... | collective-permute-start | bytes 589832 | tf_op jit(solution)/shard_map/ppermute | solution.py:25
  55.8 2.0 %collective-permute-start = (bf16[256,256]{1,0:T(8,128)(2,1)S(1)}, bf16[256,256]{1,0:T(8,128)(2,1)S(1)}, u32[]{:S(2)}, u32[]{:S(2)}) collective-permute-start(bf16[256,256]{1,0:T(8,128)(2,1)S(1)} %pad_maximum_fusion.rest_0_), channel_id=1, source_target_pairs={{0,32},{32,0},{1,33},{33,1},{2,34},{34,2},{3,35},{35,3},{4,36},{36... | collective-permute-start | bytes 393224 | tf_op jit(solution)/shard_map/ppermute | solution.py:21
  64.7 2.2 %collective-permute-start.8 = (f32[128,128]{1,0:T(8,128)S(1)}, f32[128,128]{1,0:T(8,128)S(1)}, u32[]{:S(2)}, u32[]{:S(2)}) collective-permute-start(f32[128,128]{1,0:T(8,128)S(1)} %add_add_fusion), channel_id=1, source_target_pairs={{0,32},{32,0},{1,33},{33,1},{2,34},{34,2},{3,35},{35,3},{4,36},{36... | collective-permute-start | bytes 196616 | tf_op jit(solution)/shard_map/ppermute | solution.py:21
  66.1 1.5 %collective-permute-start.5 = (bf16[256,256]{1,0:T(8,128)(2,1)S(1)}, bf16[256,256]{1,0:T(8,128)(2,1)S(1)}, u32[]{:S(2)}, u32[]{:S(2)}) collective-permute-start(bf16[256,256]{1,0:T(8,128)(2,1)S(1)} %slice.64), channel_id=1, source_target_pairs={{0,32},{32,0},{1,33},{33,1},{2,34},{34,2},{3,35},{35,3},{4,36},{36... | collective-permute-start | bytes 393224 | tf_op jit(solution)/shard_map/ppermute | solution.py:21
  66.2 1.5 %collective-permute-start.6 = (bf16[256,256]{1,0:T(8,128)(2,1)S(1)}, bf16[256,256]{1,0:T(8,128)(2,1)S(1)}, u32[]{:S(2)}, u32[]{:S(2)}) collective-permute-start(bf16[256,256]{1,0:T(8,128)(2,1)S(1)} %slice.65), channel_id=1, source_target_pairs={{0,32},{32,0},{1,33},{33,1},{2,34},{34,2},{3,35},{35,3},{4,36},{36... | collective-permute-start | bytes 393224 | tf_op jit(solution)/shard_map/ppermute | solution.py:21
  66.7 1.3 %collective-permute-start.7 = (bf16[256,256]{1,0:T(8,128)(2,1)S(1)}, bf16[256,256]{1,0:T(8,128)(2,1)S(1)}, u32[]{:S(2)}, u32[]{:S(2)}) collective-permute-start(bf16[256,256]{1,0:T(8,128)(2,1)S(1)} %slice.66), channel_id=1, source_target_pairs={{0,32},{32,0},{1,33},{33,1},{2,34},{34,2},{3,35},{35,3},{4,36},{36... | collective-permute-start | bytes 393224 | tf_op jit(solution)/shard_map/ppermute | solution.py:21

commit v7 on v5

--- a/solution.py
+++ b/solution.py
@@ -86,6 +86,38 @@
     )(*args)
 
 
+def pack_kernel(came_ref, modes_ref, panel_ref, packed_ref):
+    own = modes_ref.shape[0]
+    summed = jnp.sum(came_ref[...], axis=0)
+    panel_ref[...] = summed
+    share = summed[2 * own :]
+    high = share.astype(BF16).astype(F32)
+    rows = jnp.concatenate(
+        [summed[: 2 * own], modes_ref[...], high, share - high], axis=0
+    )
+    packed_ref[...] = jnp.broadcast_to(rows.astype(BF16)[None], packed_ref.shape)
+
+
+def pack(came, modes_panel):
+    peers, rows, width = came.shape
+    own = rows // 3
+    vmem = pl.BlockSpec(memory_space=pltpu.VMEM)
+    return pl.pallas_call(
+        pack_kernel,
+        out_shape=(
+            jax.ShapeDtypeStruct((3 * own, width), F32),
+            jax.ShapeDtypeStruct((peers, 5 * own, width), BF16),
+        ),
+        in_specs=[vmem] * 2,
+        out_specs=(vmem, vmem),
+        cost_estimate=pl.CostEstimate(
+            flops=came.size, bytes_accessed=came.size * 4, transcendentals=0
+        ),
+        compiler_params=pltpu.CompilerParams(vmem_limit_bytes=24 << 20),
+        name="pack",
+    )(came, modes_panel)
+
+
 def update_kernel(turns, factor_ref, rhs_ref, *rest):
     out_ref = rest[-1]
     width = out_ref.shape[2]
@@ -132,20 +164,11 @@
     width = panel_rhs.shape[2]
     own = modes_panel.shape[0]
     peers = diag_inverse.shape[1] // own
-    core = lax.axis_index("core")
     outgoing = first_partials(diag_inverse, panel_rhs, modes_prev, solved_prev, peers, own)
-    summed = jnp.sum(lax.all_to_all(outgoing, COL, 0, 0, tiled=True), axis=0)
-    panel_solution = summed[: 2 * own].reshape(2, own, width)
-    share = summed[2 * own :]
-    high = lax.reduce_precision(share, 8, 7)
-    low = share - high
-    packed = jnp.concatenate(
-        [summed[: 2 * own].astype(BF16), modes_panel, high.astype(BF16), low.astype(BF16)], axis=0
-    )
-    rows = packed.shape[0]
-    gathered = lax.all_to_all(
-        jnp.broadcast_to(packed[None], (peers, rows, width)), COL, 0, 0, tiled=True
-    )
+    came = lax.all_to_all(outgoing, COL, 0, 0, tiled=True)
+    panel_solution, packed = pack(came, modes_panel.astype(F32))
+    panel_solution = panel_solution[: 2 * own].reshape(2, own, width)
+    gathered = lax.all_to_all(packed, COL, 0, 0, tiled=True)
     block = jnp.concatenate(
         [
             gathered[:, :own].reshape(peers * own, width),
@@ -160,27 +183,22 @@
         modes_block, block, (((0,), (0,)), ((), ())), preferred_element_type=F32
     )
     share = share.reshape(2, width, width) + jnp.stack([latest[:, :width], latest[:, width:]])
-    mine = lax.dynamic_index_in_dim(share, core, 0, keepdims=False)
-    other = lax.dynamic_index_in_dim(share, 1 - core, 0, keepdims=False)
-    half = split(mine + swapped(other))
-    sent = jnp.concatenate([block, half], axis=0)
+    modal = split(share.reshape(2 * width, width))
+    sent = jnp.concatenate([block, modal], axis=0)
     came = [flipped(sent, k) for k in TURNS[1:]]
     started = update(TURNS[:1], factor_slab, pending_rhs, [block, twin], "update_own")
     started, came = lax.optimization_barrier((started, came))
     depth = block.shape[0]
     twins = [swapped(c[:depth]) for c in came]
     first, third, second = (joined(c[depth:]) for c in came)
-    half = (joined(half) + second) + (first + third)
-    back = swapped(half)
+    modal = (joined(modal) + second) + (first + third)
+    modal_forces = (modal + swapped(modal)).reshape(2, width, width)
     updated_rhs = update(
         TURNS[1:],
         factor_slab,
         started,
         [b for two in zip(came, twins) for b in two],
         "update_rest",
-    )
-    modal_forces = jnp.stack(
-        [jnp.where(core == 0, half, back), jnp.where(core == 0, back, half)]
     )
     return (panel_solution, updated_rhs, modal_forces)
 

time: 70.9 us -> 66.4 us (0.937)
  blocking collectives: 25.7 us -> 16 us
  starting transfers between devices: 16.1 us -> 24.9 us
  waiting for transfers between devices: 17.9 us -> 15.2 us
  local copies, waits for them, and re-layouts: 3.63 us -> 2.85 us
    all_to_all x1, blocking collectives: 25.7 us -> 16 us  [on_device(): gathered = lax.all_to_all(packed, COL, 0, 0, tiled=True)]
    all_to_all x1, starting transfers between devices: 5 us -> 11.9 us  [on_device(): came = lax.all_to_all(outgoing, COL, 0, 0, tiled=True)]
    ppermute x3, waiting for transfers between devices: 4.21 us -> 0.4 us  [flipped(): return lax.ppermute(value, 'y', [(i, i ^ bits) for i in range(4)])]
    ppermute x6 -> x5, starting transfers between devices: 7.12 us -> 9.22 us  [swapped(): return lax.ppermute(value, 'core', SWAP)]
    all_to_all x1, waiting for transfers between devices: 11.2 us -> 13.1 us  [on_device(): came = lax.all_to_all(outgoing, COL, 0, 0, tiled=True)]
    ppermute x6 -> x5, waiting for transfers between devices: 2.45 us -> 1.64 us  [swapped(): return lax.ppermute(value, 'core', SWAP)]
    broadcast_in_dim x1 -> x0, local copies, waits for them, and re-layouts: 0.77 us -> none  [on_device(): jnp.broadcast_to(packed[None], (peers, rows, width))]
  transfers between devices with their start and end apart: 10 -> 9, of which waited for: 8 -> 4; matrix products, arithmetic and copies ran while one was open for 2% -> 3% of each run, Pallas kernels for 1% -> 1%
where the time goes in v7:
time: 66.4 us; the launch traced here: 66.1 us
  starting transfers between devices  24.9 us (38%)
  blocking collectives  16 us (24%)
  waiting for transfers between devices  15.2 us (23%)
  Pallas kernels  4.76 us (7%)
  local copies, waits for them, and re-layouts  2.85 us (4%)
  other arithmetic  1.53 us (2%)
  between operations  0.75 us (1%)
    all_to_all x1, blocking collectives, on_device(): gathered = lax.all_to_all(packed, COL, 0, 0, tiled=True)  16 us
    all_to_all x1, waiting for transfers between devices, on_device(): came = lax.all_to_all(outgoing, COL, 0, 0, tiled=True)  13.1 us
    all_to_all x1, starting transfers between devices, on_device(): came = lax.all_to_all(outgoing, COL, 0, 0, tiled=True)  11.9 us
    ppermute x5, starting transfers between devices, swapped(): return lax.ppermute(value, 'core', SWAP)  9.22 us
    ppermute x3, starting transfers between devices, flipped(): return lax.ppermute(value, 'y', [(i, i ^ bits) for i in range(4)])  3.77 us
    pallas_call x1, Pallas kernels, first_partials(): pl.pallas_call(first_kernel, out_shape=jax.ShapeDtypeStruct((peers, 3 * o...  2.42 us
    pallas_call x2, Pallas kernels, update(): pl.pallas_call(functools.partial(update_kernel, turns), out_shape=jax.Sha...  2.28 us
    unnamed x4, local copies, waits for them, and re-layouts  2.19 us
  transfers between devices with their start and end apart: 9, of which 4 were waited for; matrix products, arithmetic and copies ran while one was open for 3% of the time, Pallas kernels for 1%

profile of v7, /device:TPU:1, one launch (start us, length us, event | category | flops | bytes accessed | tf_op | source)
XLA Modules:
  0.0 66.1 jit_solution(3277630719837806584)
XLA Ops:
  0.6 0.0 copy-start.1
  0.6 2.4 %partials.1 = f32[32,24,128]{2,1,0:T(8,128)} custom-call(f32[2,64,256]{2,1,0:T(8,128)} %bitcast.28, f32[2,64,128]{2,1,0:T(8,128)} %rhs_hbm.1, bf16[256,128]{1,0:T(8,128)(2,1)} %modes_hbm.1, bf16[2,256,128]{2,1,0:T(8,128)(2,1)} %solved_hbm.1), custom_call_target="tpu_custom_call" | custom-call | tf_op jit(solution)/shard_map/partials/pallas_call | solution.py:78
  3.1 11.9 %all-to-all-start = ((f32[32,24,128]{2,1,0:T(8,128)}), f32[32,24,128]{2,1,0:T(8,128)S(1)}, u32[]{:S(2)}, u32[]{:S(2)}) async-start(f32[32,24,128]{2,1,0:T(8,128)} %partials.1), calls=%async_computation | async-start | bytes 786432 | tf_op jit(solution)/shard_map/all_to_all | solution.py:168
  15.0 0.7 %convert_element_type.39.modes_ref = f32[8,128]{1,0:T(8,128)S(1)} convert(bf16[8,128]{1,0:T(8,128)(2,1)} %param.13) | non-fusion elementwise | flops 1024 | bytes 6144 | tf_op jit(solution)/shard_map/convert_element_type | solution.py:169
  15.6 13.1 %all-to-all-done.came_ref = f32[32,24,128]{2,1,0:T(8,128)S(1)} async-done(((f32[32,24,128]{2,1,0:T(8,128)}), f32[32,24,128]{2,1,0:T(8,128)S(1)}, u32[]{:S(2)}, u32[]{:S(2)}) %all-to-all-start) | async-done | bytes 393248 | tf_op jit(solution)/shard_map/all_to_all | solution.py:168
  28.8 0.1 pack.1
  28.8 16.0 %all_to_all.10 = bf16[32,40,128]{2,1,0:T(8,128)(2,1)S(1)} all-to-all(bf16[32,40,128]{2,1,0:T(8,128)(2,1)S(1)} %get-tuple-element.10), channel_id=1, replica_groups=mesh['y'=4,'core'=2,'z'=8,'x'=4] {'z','x'}, dimensions={0} | all-to-all | bytes 655360 | tf_op jit(solution)/shard_map/all_to_all | solution.py:171
  44.9 0.2 fusion.1
  45.2 3.0 %collective-permute-start.3 = (bf16[512,256]{1,0:T(8,128)(2,1)S(1)}, bf16[512,256]{1,0:T(8,128)(2,1)S(1)}, u32[]{:S(2)}, u32[]{:S(2)}) collective-permute-start(bf16[512,256]{1,0:T(8,128)(2,1)S(1)} %maximum_maximum_fusion), channel_id=1, source_target_pairs={{0,128},{64,192},{128,0},{192,64},{1,129},{65,193},{129,1},{193,65... | collective-permute-start | bytes 786440 | tf_op jit(solution)/shard_map/ppermute | solution.py:23
  48.2 0.8 %collective-permute-start.2 = (bf16[512,256]{1,0:T(8,128)(2,1)S(1)}, bf16[512,256]{1,0:T(8,128)(2,1)S(1)}, u32[]{:S(2)}, u32[]{:S(2)}) collective-permute-start(bf16[512,256]{1,0:T(8,128)(2,1)S(1)} %maximum_maximum_fusion), channel_id=1, source_target_pairs={{0,192},{64,128},{128,64},{192,0},{1,193},{65,129},{129,65},{193,1... | collective-permute-start | bytes 786440 | tf_op jit(solution)/shard_map/ppermute | solution.py:23
  49.0 0.0 collective-permute-start.1
  49.0 4.7 %collective-permute-start = (bf16[256,256]{1,0:T(8,128)(2,1)S(1)}, bf16[256,256]{1,0:T(8,128)(2,1)S(1)}, u32[]{:S(2)}, u32[]{:S(2)}) collective-permute-start(bf16[256,256]{1,0:T(8,128)(2,1)S(1)} %pad_maximum_fusion.rest_0_), channel_id=1, source_target_pairs={{0,32},{32,0},{1,33},{33,1},{2,34},{34,2},{3,35},{35,3},{4,36},{36... | collective-permute-start | bytes 393224 | tf_op jit(solution)/shard_map/ppermute | solution.py:19
  53.6 1.0 %collective-permute-done.rest_1_ = bf16[256,256]{1,0:T(8,128)(2,1)S(1)} collective-permute-done((bf16[256,256]{1,0:T(8,128)(2,1)S(1)}, bf16[256,256]{1,0:T(8,128)(2,1)S(1)}, u32[]{:S(2)}, u32[]{:S(2)}) %collective-permute-start) | collective-permute-done | bytes 131104 | tf_op jit(solution)/shard_map/ppermute | solution.py:19
  54.6 0.0 copy-done.1
  54.6 0.0 copy-start
  54.6 2.2 %copy-done = bf16[2,512,2048]{2,1,0:T(8,128)(2,1)S(1)} copy-done((bf16[2,512,2048]{2,1,0:T(8,128)(2,1)S(1)}, bf16[2,512,2048]{2,1,0:T(8,128)(2,1)}, u32[]{:S(2)}) %copy-start) | copy-done | bytes 4194328
  56.8 0.4 update_own.1.rhs_ref
  57.3 0.0 collective-permute-done.3.rest_4_
  57.3 0.4 collective-permute-done.2.rest_2_
  57.7 0.0 collective-permute-done.1.rest_0_
  57.7 0.1 add_add_fusion
  57.8 4.0 %collective-permute-start.6 = (bf16[256,256]{1,0:T(8,128)(2,1)S(1)}, bf16[256,256]{1,0:T(8,128)(2,1)S(1)}, u32[]{:S(2)}, u32[]{:S(2)}) collective-permute-start(bf16[256,256]{1,0:T(8,128)(2,1)S(1)} %slice.70), channel_id=1, source_target_pairs={{0,32},{32,0},{1,33},{33,1},{2,34},{34,2},{3,35},{35,3},{4,36},{36... | collective-permute-start | bytes 393224 | tf_op jit(solution)/shard_map/ppermute | solution.py:19
  61.8 0.1 collective-permute-start.5
  61.9 0.4 collective-permute-start.4
  62.3 0.1 collective-permute-start.7
  62.4 0.6 slice_bitcast_fusion.6
  63.0 0.6 collective-permute-done.7
  63.6 0.7 %add.40 = f32[256,128]{1,0:T(8,128)} add(f32[256,128]{1,0:T(8,128)S(1)} %add_add_fusion, f32[256,128]{1,0:T(8,128)S(1)} %collective-permute-done.7) | non-fusion elementwise | flops 32768 | bytes 393216 | tf_op jit(solution)/shard_map/add | solution.py:195
  64.3 0.0 collective-permute-done.6.rest_5_
  64.3 0.0 collective-permute-done.5.rest_3_
  64.3 0.0 collective-permute-done.4.rest_1_
  64.3 1.8 %update_rest.1 = f32[2,512,128]{2,1,0:T(8,128)} custom-call(bf16[2,512,2048]{2,1,0:T(8,128)(2,1)S(1)} %copy-done, f32[2,512,128]{2,1,0:T(8,128)S(1)} %update_own.1.rhs_ref, bf16[512,256]{1,0:T(8,128)(2,1)S(1)} %collective-permute-done.1.rest_0_, bf16[256,256]{1,0:T(8,128)(2,1)S(1)} %collective-permute-done.4.rest_1_, ...), custom_call_target="tpu_custom_call" | custom-call | flops 805306368 | bytes 3145728 | tf_op jit(solution)/shard_map/update_rest/pallas_call | solution.py:146
  (9 shorter events, 0.2 us)
Async XLA Ops:
  0.6 54.0 %copy-start.1 = (f32[2,512,128]{2,1,0:T(8,128)S(1)}, f32[2,512,128]{2,1,0:T(8,128)}, u32[]{:S(2)}) copy-start(f32[2,512,128]{2,1,0:T(8,128)} %rhs_ref.1) | copy-start | bytes 1572868
  3.1 25.7 %all-to-all-start = ((f32[32,24,128]{2,1,0:T(8,128)}), f32[32,24,128]{2,1,0:T(8,128)S(1)}, u32[]{:S(2)}, u32[]{:S(2)}) async-start(f32[32,24,128]{2,1,0:T(8,128)} %partials.1), calls=%async_computation | async-start | bytes 786432 | tf_op jit(solution)/shard_map/all_to_all | solution.py:168
  45.2 12.1 %collective-permute-start.3 = (bf16[512,256]{1,0:T(8,128)(2,1)S(1)}, bf16[512,256]{1,0:T(8,128)(2,1)S(1)}, u32[]{:S(2)}, u32[]{:S(2)}) collective-permute-start(bf16[512,256]{1,0:T(8,128)(2,1)S(1)} %maximum_maximum_fusion), channel_id=1, source_target_pairs={{0,128},{64,192},{128,0},{192,64},{1,129},{65,193},{129,1},{193,65... | collective-permute-start | bytes 786440 | tf_op jit(solution)/shard_map/ppermute | solution.py:23
  48.2 9.5 %collective-permute-start.2 = (bf16[512,256]{1,0:T(8,128)(2,1)S(1)}, bf16[512,256]{1,0:T(8,128)(2,1)S(1)}, u32[]{:S(2)}, u32[]{:S(2)}) collective-permute-start(bf16[512,256]{1,0:T(8,128)(2,1)S(1)} %maximum_maximum_fusion), channel_id=1, source_target_pairs={{0,192},{64,128},{128,64},{192,0},{1,193},{65,129},{129,65},{193,1... | collective-permute-start | bytes 786440 | tf_op jit(solution)/shard_map/ppermute | solution.py:23
  49.0 8.7 %collective-permute-start.1 = (bf16[512,256]{1,0:T(8,128)(2,1)S(1)}, bf16[512,256]{1,0:T(8,128)(2,1)S(1)}, u32[]{:S(2)}, u32[]{:S(2)}) collective-permute-start(bf16[512,256]{1,0:T(8,128)(2,1)S(1)} %maximum_maximum_fusion), channel_id=1, source_target_pairs={{0,64},{64,0},{128,192},{192,128},{1,65},{65,1},{129,193},{193,129... | collective-permute-start | bytes 786440 | tf_op jit(solution)/shard_map/ppermute | solution.py:23
  49.0 5.6 %collective-permute-start = (bf16[256,256]{1,0:T(8,128)(2,1)S(1)}, bf16[256,256]{1,0:T(8,128)(2,1)S(1)}, u32[]{:S(2)}, u32[]{:S(2)}) collective-permute-start(bf16[256,256]{1,0:T(8,128)(2,1)S(1)} %pad_maximum_fusion.rest_0_), channel_id=1, source_target_pairs={{0,32},{32,0},{1,33},{33,1},{2,34},{34,2},{3,35},{35,3},{4,36},{36... | collective-permute-start | bytes 393224 | tf_op jit(solution)/shard_map/ppermute | solution.py:19
  54.6 2.2 %copy-start = (bf16[2,512,2048]{2,1,0:T(8,128)(2,1)S(1)}, bf16[2,512,2048]{2,1,0:T(8,128)(2,1)}, u32[]{:S(2)}) copy-start(bf16[2,512,2048]{2,1,0:T(8,128)(2,1)} %factor_ref.3) | copy-start | bytes 12582916
  57.8 6.5 %collective-permute-start.6 = (bf16[256,256]{1,0:T(8,128)(2,1)S(1)}, bf16[256,256]{1,0:T(8,128)(2,1)S(1)}, u32[]{:S(2)}, u32[]{:S(2)}) collective-permute-start(bf16[256,256]{1,0:T(8,128)(2,1)S(1)} %slice.70), channel_id=1, source_target_pairs={{0,32},{32,0},{1,33},{33,1},{2,34},{34,2},{3,35},{35,3},{4,36},{36... | collective-permute-start | bytes 393224 | tf_op jit(solution)/shard_map/ppermute | solution.py:19
  61.8 2.5 %collective-permute-start.5 = (bf16[256,256]{1,0:T(8,128)(2,1)S(1)}, bf16[256,256]{1,0:T(8,128)(2,1)S(1)}, u32[]{:S(2)}, u32[]{:S(2)}) collective-permute-start(bf16[256,256]{1,0:T(8,128)(2,1)S(1)} %slice.69), channel_id=1, source_target_pairs={{0,32},{32,0},{1,33},{33,1},{2,34},{34,2},{3,35},{35,3},{4,36},{36... | collective-permute-start | bytes 393224 | tf_op jit(solution)/shard_map/ppermute | solution.py:19
  61.9 2.4 %collective-permute-start.4 = (bf16[256,256]{1,0:T(8,128)(2,1)S(1)}, bf16[256,256]{1,0:T(8,128)(2,1)S(1)}, u32[]{:S(2)}, u32[]{:S(2)}) collective-permute-start(bf16[256,256]{1,0:T(8,128)(2,1)S(1)} %slice.68), channel_id=1, source_target_pairs={{0,32},{32,0},{1,33},{33,1},{2,34},{34,2},{3,35},{35,3},{4,36},{36... | collective-permute-start | bytes 393224 | tf_op jit(solution)/shard_map/ppermute | solution.py:19
  62.3 1.3 %collective-permute-start.7 = (f32[256,128]{1,0:T(8,128)S(1)}, f32[256,128]{1,0:T(8,128)S(1)}, u32[]{:S(2)}, u32[]{:S(2)}) collective-permute-start(f32[256,128]{1,0:T(8,128)S(1)} %add_add_fusion), channel_id=1, source_target_pairs={{0,32},{32,0},{1,33},{33,1},{2,34},{34,2},{3,35},{35,3},{4,36},{36... | collective-permute-start | bytes 393224 | tf_op jit(solution)/shard_map/ppermute | solution.py:19

commit v8 on v7

--- a/solution.py
+++ b/solution.py
@@ -12,15 +12,16 @@
 COL = ("z", "x")
 SWAP = [(0, 1), (1, 0)]
 CHUNK = 128
-TURNS = (0, 1, 3, 2)
+TURNS = ((0, 0), (1, 3), (3, 1), (2, 2))
 
 
 def swapped(value):
     return lax.ppermute(value, "core", SWAP)
 
 
-def flipped(value, bits):
-    return lax.ppermute(value, "y", [(i, i ^ bits) for i in range(4)])
+def flipped(value, turn):
+    pairs = [(2 * y + core, 2 * (y ^ turn[core]) + core) for y in range(4) for core in range(2)]
+    return lax.ppermute(value, ("y", "core"), pairs)
 
 
 def split(value):
@@ -119,35 +120,52 @@
 
 
 def update_kernel(turns, factor_ref, rhs_ref, *rest):
-    out_ref = rest[-1]
+    count = 2 * len(turns)
+    blocks, rest = rest[:count], rest[count:]
+    if len(rest) == 1:
+        (out_ref,) = rest
+    else:
+        modal_ref, back_ref, summed_ref, out_ref, forces_ref, panel_ref = rest
+        forces_ref[...] = modal_ref[...] + back_ref[...]
+        panel_ref[...] = summed_ref[: panel_ref.shape[0], :]
     width = out_ref.shape[2]
     depth = 2 * width
     rows = factor_ref.shape[1]
     y = lax.axis_index("y")
     core = lax.axis_index("core")
-    for j, block_ref in enumerate(rest[:-1]):
-        place = jnp.bitwise_xor(y, turns[j // 2]) * 2 + jnp.bitwise_xor(core, j % 2)
+    pieces = []
+    for j, block_ref in enumerate(blocks):
+        source = core if j % 2 == 0 else 1 - core
+        low, high = turns[j // 2]
+        place = jnp.bitwise_xor(y, low + (high - low) * source) * 2 + source
         columns = pl.ds(pl.multiple_of(place * depth, depth), depth)
         straight = block_ref[:depth, :]
         crossed = jnp.concatenate([-straight[:, width:], straight[:, :width]], axis=1)
-        base = rhs_ref if j == 0 else out_ref
-        for at in range(0, rows, CHUNK):
-            span = slice(at, at + CHUNK)
-            product = jnp.dot(factor_ref[0, span, columns], straight, preferred_element_type=F32)
+        pieces.append((columns, straight, crossed))
+    for at in range(0, rows, CHUNK):
+        span = slice(at, at + CHUNK)
+        product = jnp.zeros((CHUNK, depth), F32)
+        for columns, straight, crossed in pieces:
+            product += jnp.dot(factor_ref[0, span, columns], straight, preferred_element_type=F32)
             product += jnp.dot(factor_ref[1, span, columns], crossed, preferred_element_type=F32)
-            out_ref[0, span, :] = base[0, span, :] - product[:, :width]
-            out_ref[1, span, :] = base[1, span, :] - product[:, width:]
-
-
-def update(turns, factor_slab, rhs, blocks, name):
+        out_ref[0, span, :] = rhs_ref[0, span, :] - product[:, :width]
+        out_ref[1, span, :] = rhs_ref[1, span, :] - product[:, width:]
+
+
+def update(turns, factor_slab, rhs, blocks, name, others=()):
     depth = 2 * rhs.shape[2]
     rows = factor_slab.shape[1]
     vmem = pl.BlockSpec(memory_space=pltpu.VMEM)
+    shapes = [jax.ShapeDtypeStruct(rhs.shape, F32)]
+    if others:
+        modal, _, summed = others
+        shapes.append(jax.ShapeDtypeStruct(modal.shape, F32))
+        shapes.append(jax.ShapeDtypeStruct((summed.shape[0] * 2 // 3, summed.shape[1]), F32))
     return pl.pallas_call(
         functools.partial(update_kernel, turns),
-        out_shape=jax.ShapeDtypeStruct(rhs.shape, F32),
-        in_specs=[vmem] * (2 + len(blocks)),
-        out_specs=vmem,
+        out_shape=shapes,
+        in_specs=[vmem] * (2 + len(blocks) + len(others)),
+        out_specs=[vmem] * len(shapes),
         cost_estimate=pl.CostEstimate(
             flops=len(blocks) * 4 * rows * depth * 2 * rhs.shape[2],
             bytes_accessed=len(blocks) * 4 * rows * depth,
@@ -155,7 +173,7 @@
         ),
         compiler_params=pltpu.CompilerParams(vmem_limit_bytes=24 << 20),
         name=name,
-    )(factor_slab, rhs, *blocks)
+    )(factor_slab, rhs, *blocks, *others)
 
 
 def on_device(
@@ -166,8 +184,7 @@
     peers = diag_inverse.shape[1] // own
     outgoing = first_partials(diag_inverse, panel_rhs, modes_prev, solved_prev, peers, own)
     came = lax.all_to_all(outgoing, COL, 0, 0, tiled=True)
-    panel_solution, packed = pack(came, modes_panel.astype(F32))
-    panel_solution = panel_solution[: 2 * own].reshape(2, own, width)
+    summed, packed = pack(came, modes_panel.astype(F32))
     gathered = lax.all_to_all(packed, COL, 0, 0, tiled=True)
     block = jnp.concatenate(
         [
@@ -186,20 +203,22 @@
     modal = split(share.reshape(2 * width, width))
     sent = jnp.concatenate([block, modal], axis=0)
     came = [flipped(sent, k) for k in TURNS[1:]]
-    started = update(TURNS[:1], factor_slab, pending_rhs, [block, twin], "update_own")
+    (started,) = update(TURNS[:1], factor_slab, pending_rhs, [block, twin], "update_own")
     started, came = lax.optimization_barrier((started, came))
     depth = block.shape[0]
     twins = [swapped(c[:depth]) for c in came]
     first, third, second = (joined(c[depth:]) for c in came)
     modal = (joined(modal) + second) + (first + third)
-    modal_forces = (modal + swapped(modal)).reshape(2, width, width)
-    updated_rhs = update(
+    updated_rhs, modal_forces, panel_solution = update(
         TURNS[1:],
         factor_slab,
         started,
         [b for two in zip(came, twins) for b in two],
         "update_rest",
-    )
+        (modal, swapped(modal), summed),
+    )
+    modal_forces = modal_forces.reshape(2, width, width)
+    panel_solution = panel_solution.reshape(2, own, width)
     return (panel_solution, updated_rhs, modal_forces)
 
 

time: 66.4 us -> 65.7 us (0.989)
  waiting for transfers between devices: 15.2 us -> 16.2 us
  other arithmetic: 1.53 us -> 0.86 us
    add x1 -> x0, other arithmetic: 0.67 us -> none  [on_device(): modal_forces = (modal + swapped(modal)).reshape(2, width, width)]
    unnamed x4 -> x6, local copies, waits for them, and re-layouts: 2.19 us -> 2.2 us
  transfers between devices with their start and end apart: 9 -> 9, of which waited for: 4 -> 7; matrix products, arithmetic and copies ran while one was open for 3% -> 1% of each run, Pallas kernels for 1% -> 1%
where the time goes in v8:
time: 65.7 us; the launch traced here: 65.4 us
  starting transfers between devices  24.4 us (37%)
  waiting for transfers between devices  16.2 us (25%)
  blocking collectives  16 us (24%)
  Pallas kernels  4.75 us (7%)
  local copies, waits for them, and re-layouts  2.25 us (3%)
  other arithmetic  0.86 us (1%)
  between operations  0.75 us (1%)
    all_to_all x1, blocking collectives, on_device(): gathered = lax.all_to_all(packed, COL, 0, 0, tiled=True)  16 us
    all_to_all x1, waiting for transfers between devices, on_device(): came = lax.all_to_all(outgoing, COL, 0, 0, tiled=True)  13.1 us
    all_to_all x1, starting transfers between devices, on_device(): came = lax.all_to_all(outgoing, COL, 0, 0, tiled=True)  11.9 us
    ppermute x5, starting transfers between devices, swapped(): return lax.ppermute(value, 'core', SWAP)  8.74 us
    ppermute x3, starting transfers between devices, flipped(): return lax.ppermute(value, ('y', 'core'), pairs)  3.77 us
    pallas_call x1, Pallas kernels, first_partials(): pl.pallas_call(first_kernel, out_shape=jax.ShapeDtypeStruct((peers, 3 * o...  2.42 us
    pallas_call x2, Pallas kernels, update(): pl.pallas_call(functools.partial(update_kernel, turns), out_shape=shapes,...  2.27 us
    ppermute x5, waiting for transfers between devices, swapped(): return lax.ppermute(value, 'core', SWAP)  2.23 us
  transfers between devices with their start and end apart: 9, of which 7 were waited for; matrix products, arithmetic and copies ran while one was open for 1% of the time, Pallas kernels for 1%

profile of v8, /device:TPU:1, one launch (start us, length us, event | category | flops | bytes accessed | tf_op | source)
XLA Modules:
  0.0 65.4 jit_solution(2178868048755621865)
XLA Ops:
  0.6 0.0 copy-start.2
  0.6 2.4 %partials.1 = f32[32,24,128]{2,1,0:T(8,128)} custom-call(f32[2,64,256]{2,1,0:T(8,128)} %bitcast.26, f32[2,64,128]{2,1,0:T(8,128)} %rhs_hbm.1, bf16[256,128]{1,0:T(8,128)(2,1)} %modes_hbm.1, bf16[2,256,128]{2,1,0:T(8,128)(2,1)} %solved_hbm.1), custom_call_target="tpu_custom_call" | custom-call | tf_op jit(solution)/shard_map/partials/pallas_call | solution.py:79
  3.1 11.9 %all-to-all-start = ((f32[32,24,128]{2,1,0:T(8,128)}), f32[32,24,128]{2,1,0:T(8,128)S(1)}, u32[]{:S(2)}, u32[]{:S(2)}) async-start(f32[32,24,128]{2,1,0:T(8,128)} %partials.1), calls=%async_computation | async-start | bytes 786432 | tf_op jit(solution)/shard_map/all_to_all | solution.py:186
  15.0 0.7 %convert_element_type.39.modes_ref = f32[8,128]{1,0:T(8,128)S(1)} convert(bf16[8,128]{1,0:T(8,128)(2,1)} %param.13) | non-fusion elementwise | flops 1024 | bytes 6144 | tf_op jit(solution)/shard_map/convert_element_type | solution.py:187
  15.6 13.1 %all-to-all-done.came_ref = f32[32,24,128]{2,1,0:T(8,128)S(1)} async-done(((f32[32,24,128]{2,1,0:T(8,128)}), f32[32,24,128]{2,1,0:T(8,128)S(1)}, u32[]{:S(2)}, u32[]{:S(2)}) %all-to-all-start) | async-done | bytes 393248 | tf_op jit(solution)/shard_map/all_to_all | solution.py:186
  28.8 0.1 pack.1
  28.8 16.0 %all_to_all.10 = bf16[32,40,128]{2,1,0:T(8,128)(2,1)S(1)} all-to-all(bf16[32,40,128]{2,1,0:T(8,128)(2,1)S(1)} %get-tuple-element.12), channel_id=1, replica_groups=mesh['y'=4,'core'=2,'z'=8,'x'=4] {'z','x'}, dimensions={0} | all-to-all | bytes 655360 | tf_op jit(solution)/shard_map/all_to_all | solution.py:188
  44.9 0.2 fusion.1
  45.2 3.0 %collective-permute-start.3 = (bf16[512,256]{1,0:T(8,128)(2,1)S(1)}, bf16[512,256]{1,0:T(8,128)(2,1)S(1)}, u32[]{:S(2)}, u32[]{:S(2)}) collective-permute-start(bf16[512,256]{1,0:T(8,128)(2,1)S(1)} %maximum_maximum_fusion), channel_id=1, source_target_pairs={{0,128},{32,160},{64,192},{96,224},{128,0},{160,32},{192,64},{224,... | collective-permute-start | bytes 786440 | tf_op jit(solution)/shard_map/ppermute | solution.py:24
  48.2 0.4 collective-permute-start.2
  48.6 0.4 collective-permute-start.1
  49.0 4.7 %collective-permute-start = (bf16[256,256]{1,0:T(8,128)(2,1)S(1)}, bf16[256,256]{1,0:T(8,128)(2,1)S(1)}, u32[]{:S(2)}, u32[]{:S(2)}) collective-permute-start(bf16[256,256]{1,0:T(8,128)(2,1)S(1)} %pad_maximum_fusion.rest_0_), channel_id=1, source_target_pairs={{0,32},{32,0},{1,33},{33,1},{2,34},{34,2},{3,35},{35,3},{4,36},{36... | collective-permute-start | bytes 393224 | tf_op jit(solution)/shard_map/ppermute | solution.py:19
  53.6 1.0 %collective-permute-done.rest_1_ = bf16[256,256]{1,0:T(8,128)(2,1)S(1)} collective-permute-done((bf16[256,256]{1,0:T(8,128)(2,1)S(1)}, bf16[256,256]{1,0:T(8,128)(2,1)S(1)}, u32[]{:S(2)}, u32[]{:S(2)}) %collective-permute-start) | collective-permute-done | bytes 131104 | tf_op jit(solution)/shard_map/ppermute | solution.py:19
  54.6 0.0 copy-done.2
  54.6 0.0 copy-start
  54.6 2.2 %copy-done = bf16[2,512,2048]{2,1,0:T(8,128)(2,1)S(1)} copy-done((bf16[2,512,2048]{2,1,0:T(8,128)(2,1)S(1)}, bf16[2,512,2048]{2,1,0:T(8,128)(2,1)}, u32[]{:S(2)}) %copy-start) | copy-done | bytes 4194328
  56.8 0.0 copy-start.1
  56.8 0.5 update_own.1.rhs_ref
  57.3 0.0 collective-permute-done.3.rest_4_
  57.3 0.0 collective-permute-done.2.rest_2_
  57.3 0.9 %collective-permute-done.1.rest_0_ = bf16[512,256]{1,0:T(8,128)(2,1)S(1)} collective-permute-done((bf16[512,256]{1,0:T(8,128)(2,1)S(1)}, bf16[512,256]{1,0:T(8,128)(2,1)S(1)}, u32[]{:S(2)}, u32[]{:S(2)}) %collective-permute-start.1) | collective-permute-done | bytes 262176 | tf_op jit(solution)/shard_map/ppermute | solution.py:24
  58.2 0.1 add_add_fusion.rest_6_
  58.3 3.5 %collective-permute-start.6 = (bf16[256,256]{1,0:T(8,128)(2,1)S(1)}, bf16[256,256]{1,0:T(8,128)(2,1)S(1)}, u32[]{:S(2)}, u32[]{:S(2)}) collective-permute-start(bf16[256,256]{1,0:T(8,128)(2,1)S(1)} %slice.66), channel_id=1, source_target_pairs={{0,32},{32,0},{1,33},{33,1},{2,34},{34,2},{3,35},{35,3},{4,36},{36... | collective-permute-start | bytes 393224 | tf_op jit(solution)/shard_map/ppermute | solution.py:19
  61.8 0.1 collective-permute-start.5
  61.9 0.4 collective-permute-start.4
  62.3 0.1 collective-permute-start.7
  62.4 0.4 collective-permute-done.6.rest_5_
  62.7 0.4 collective-permute-done.5.rest_3_
  63.1 0.2 collective-permute-done.4.rest_1_
  63.3 0.3 collective-permute-done.7.rest_7_
  63.6 0.0 copy-done.1
  63.6 1.8 %update_rest.1 = (f32[2,512,128]{2,1,0:T(8,128)}, f32[256,128]{1,0:T(8,128)}, f32[16,128]{1,0:T(8,128)}) custom-call(bf16[2,512,2048]{2,1,0:T(8,128)(2,1)S(1)} %copy-done.1, f32[2,512,128]{2,1,0:T(8,128)S(1)} %update_own.1.rhs_ref, bf16[512,256]{1,0:T(8,128)(2,1)S(1)} %collective-permute-done.1.rest_0_, bf16[256,256]{1,0:T(8,128)(2,1)S(1)} %collective-permute-done.4.rest_1_, ...), custom_call_target="tpu_custom_call" | custom-call | flops 805306368 | bytes 3145728 | tf_op jit(solution)/shard_map/update_rest/pallas_call | solution.py:164
  (9 shorter events, 0.2 us)
Async XLA Ops:
  0.6 54.0 %copy-start.2 = (f32[2,512,128]{2,1,0:T(8,128)S(1)}, f32[2,512,128]{2,1,0:T(8,128)}, u32[]{:S(2)}) copy-start(f32[2,512,128]{2,1,0:T(8,128)} %rhs_ref.1) | copy-start | bytes 1572868
  3.1 25.7 %all-to-all-start = ((f32[32,24,128]{2,1,0:T(8,128)}), f32[32,24,128]{2,1,0:T(8,128)S(1)}, u32[]{:S(2)}, u32[]{:S(2)}) async-start(f32[32,24,128]{2,1,0:T(8,128)} %partials.1), calls=%async_computation | async-start | bytes 786432 | tf_op jit(solution)/shard_map/all_to_all | solution.py:186
  45.2 12.1 %collective-permute-start.3 = (bf16[512,256]{1,0:T(8,128)(2,1)S(1)}, bf16[512,256]{1,0:T(8,128)(2,1)S(1)}, u32[]{:S(2)}, u32[]{:S(2)}) collective-permute-start(bf16[512,256]{1,0:T(8,128)(2,1)S(1)} %maximum_maximum_fusion), channel_id=1, source_target_pairs={{0,128},{32,160},{64,192},{96,224},{128,0},{160,32},{192,64},{224,... | collective-permute-start | bytes 786440 | tf_op jit(solution)/shard_map/ppermute | solution.py:24
  48.2 9.1 %collective-permute-start.2 = (bf16[512,256]{1,0:T(8,128)(2,1)S(1)}, bf16[512,256]{1,0:T(8,128)(2,1)S(1)}, u32[]{:S(2)}, u32[]{:S(2)}) collective-permute-start(bf16[512,256]{1,0:T(8,128)(2,1)S(1)} %maximum_maximum_fusion), channel_id=1, source_target_pairs={{0,192},{32,96},{64,128},{96,32},{128,64},{160,224},{192,0},{224,1... | collective-permute-start | bytes 786440 | tf_op jit(solution)/shard_map/ppermute | solution.py:24
  48.6 9.6 %collective-permute-start.1 = (bf16[512,256]{1,0:T(8,128)(2,1)S(1)}, bf16[512,256]{1,0:T(8,128)(2,1)S(1)}, u32[]{:S(2)}, u32[]{:S(2)}) collective-permute-start(bf16[512,256]{1,0:T(8,128)(2,1)S(1)} %maximum_maximum_fusion), channel_id=1, source_target_pairs={{0,64},{32,224},{64,0},{96,160},{128,192},{160,96},{192,128},{224,... | collective-permute-start | bytes 786440 | tf_op jit(solution)/shard_map/ppermute | solution.py:24
  49.0 5.6 %collective-permute-start = (bf16[256,256]{1,0:T(8,128)(2,1)S(1)}, bf16[256,256]{1,0:T(8,128)(2,1)S(1)}, u32[]{:S(2)}, u32[]{:S(2)}) collective-permute-start(bf16[256,256]{1,0:T(8,128)(2,1)S(1)} %pad_maximum_fusion.rest_0_), channel_id=1, source_target_pairs={{0,32},{32,0},{1,33},{33,1},{2,34},{34,2},{3,35},{35,3},{4,36},{36... | collective-permute-start | bytes 393224 | tf_op jit(solution)/shard_map/ppermute | solution.py:19
  54.6 2.2 %copy-start = (bf16[2,512,2048]{2,1,0:T(8,128)(2,1)S(1)}, bf16[2,512,2048]{2,1,0:T(8,128)(2,1)}, u32[]{:S(2)}) copy-start(bf16[2,512,2048]{2,1,0:T(8,128)(2,1)} %factor_ref.3) | copy-start | bytes 12582916
  56.8 6.8 %copy-start.1 = (bf16[2,512,2048]{2,1,0:T(8,128)(2,1)S(1)}, bf16[2,512,2048]{2,1,0:T(8,128)(2,1)}, u32[]{:S(2)}) copy-start(bf16[2,512,2048]{2,1,0:T(8,128)(2,1)} %factor_ref.3) | copy-start | bytes 12582916
  58.3 4.5 %collective-permute-start.6 = (bf16[256,256]{1,0:T(8,128)(2,1)S(1)}, bf16[256,256]{1,0:T(8,128)(2,1)S(1)}, u32[]{:S(2)}, u32[]{:S(2)}) collective-permute-start(bf16[256,256]{1,0:T(8,128)(2,1)S(1)} %slice.66), channel_id=1, source_target_pairs={{0,32},{32,0},{1,33},{33,1},{2,34},{34,2},{3,35},{35,3},{4,36},{36... | collective-permute-start | bytes 393224 | tf_op jit(solution)/shard_map/ppermute | solution.py:19
  61.8 1.3 %collective-permute-start.5 = (bf16[256,256]{1,0:T(8,128)(2,1)S(1)}, bf16[256,256]{1,0:T(8,128)(2,1)S(1)}, u32[]{:S(2)}, u32[]{:S(2)}) collective-permute-start(bf16[256,256]{1,0:T(8,128)(2,1)S(1)} %slice.65), channel_id=1, source_target_pairs={{0,32},{32,0},{1,33},{33,1},{2,34},{34,2},{3,35},{35,3},{4,36},{36... | collective-permute-start | bytes 393224 | tf_op jit(solution)/shard_map/ppermute | solution.py:19
  61.9 1.4 %collective-permute-start.4 = (bf16[256,256]{1,0:T(8,128)(2,1)S(1)}, bf16[256,256]{1,0:T(8,128)(2,1)S(1)}, u32[]{:S(2)}, u32[]{:S(2)}) collective-permute-start(bf16[256,256]{1,0:T(8,128)(2,1)S(1)} %slice.64), channel_id=1, source_target_pairs={{0,32},{32,0},{1,33},{33,1},{2,34},{34,2},{3,35},{35,3},{4,36},{36... | collective-permute-start | bytes 393224 | tf_op jit(solution)/shard_map/ppermute | solution.py:19
  62.3 1.3 %collective-permute-start.7 = (f32[256,128]{1,0:T(8,128)S(1)}, f32[256,128]{1,0:T(8,128)S(1)}, u32[]{:S(2)}, u32[]{:S(2)}) collective-permute-start(f32[256,128]{1,0:T(8,128)S(1)} %add_add_fusion.rest_6_), channel_id=1, source_target_pairs={{0,32},{32,0},{1,33},{33,1},{2,34},{34,2},{3,35},{35,3},{4,36},{36... | collective-permute-start | bytes 393224 | tf_op jit(solution)/shard_map/ppermute | solution.py:19

commit v9 on v8

--- a/solution.py
+++ b/solution.py
@@ -12,7 +12,9 @@
 COL = ("z", "x")
 SWAP = [(0, 1), (1, 0)]
 CHUNK = 128
-TURNS = ((0, 0), (1, 3), (3, 1), (2, 2))
+OWN = ((0, 0),)
+EARLY = ((2, 2),)
+LATE = ((1, 3), (3, 1))
 
 
 def swapped(value):
@@ -202,19 +204,24 @@
     share = share.reshape(2, width, width) + jnp.stack([latest[:, :width], latest[:, width:]])
     modal = split(share.reshape(2 * width, width))
     sent = jnp.concatenate([block, modal], axis=0)
-    came = [flipped(sent, k) for k in TURNS[1:]]
-    (started,) = update(TURNS[:1], factor_slab, pending_rhs, [block, twin], "update_own")
-    started, came = lax.optimization_barrier((started, came))
+    head = flipped(sent, EARLY[0])
+    tail = [flipped(sent, turn) for turn in LATE]
     depth = block.shape[0]
-    twins = [swapped(c[:depth]) for c in came]
-    first, third, second = (joined(c[depth:]) for c in came)
+    (started,) = update(OWN, factor_slab, pending_rhs, [block, twin], "update_own")
+    started, head = lax.optimization_barrier((started, head))
+    (started,) = update(
+        EARLY, factor_slab, started, [head, swapped(head[:depth])], "update_early"
+    )
+    started, tail = lax.optimization_barrier((started, tail))
+    twins = [swapped(c[:depth]) for c in tail]
+    first, third, second = (joined(c[depth:]) for c in (*tail, head))
     modal = (joined(modal) + second) + (first + third)
     updated_rhs, modal_forces, panel_solution = update(
-        TURNS[1:],
+        LATE,
         factor_slab,
         started,
-        [b for two in zip(came, twins) for b in two],
-        "update_rest",
+        [b for two in zip(tail, twins) for b in two],
+        "update_late",
         (modal, swapped(modal), summed),
     )
     modal_forces = modal_forces.reshape(2, width, width)

time: 65.7 us -> 66.9 us (1.018)
  waiting for transfers between devices: 16.2 us -> 17.8 us
    ppermute x3, waiting for transfers between devices: 0.87 us -> 2.44 us  [flipped(): return lax.ppermute(value, ('y', 'core'), pairs)]
    pallas_call x2 -> x3, Pallas kernels: 2.27 us -> 2.46 us  [update(): pl.pallas_call(functools.partial(update_kernel, turns), out_shape=shapes,...]
  transfers between devices with their start and end apart: 9 -> 9, of which waited for: 7 -> 8; matrix products, arithmetic and copies ran while one was open for 1% -> 1% of each run, Pallas kernels for 1% -> 1%
where the time goes in v9:
time: 66.9 us; the launch traced here: 66.6 us
  starting transfers between devices  23.8 us (36%)
  waiting for transfers between devices  17.8 us (27%)
  blocking collectives  16 us (24%)
  Pallas kernels  4.93 us (7%)
  local copies, waits for them, and re-layouts  2.25 us (3%)
  other arithmetic  0.86 us (1%)
  between operations  0.76 us (1%)
    all_to_all x1, blocking collectives, on_device(): gathered = lax.all_to_all(packed, COL, 0, 0, tiled=True)  16 us
    all_to_all x1, waiting for transfers between devices, on_device(): came = lax.all_to_all(outgoing, COL, 0, 0, tiled=True)  13.1 us
    all_to_all x1, starting transfers between devices, on_device(): came = lax.all_to_all(outgoing, COL, 0, 0, tiled=True)  11.9 us
    ppermute x5, starting transfers between devices, swapped(): return lax.ppermute(value, 'core', SWAP)  8.14 us
    ppermute x3, starting transfers between devices, flipped(): return lax.ppermute(value, ('y', 'core'), pairs)  3.79 us
    pallas_call x3, Pallas kernels, update(): pl.pallas_call(functools.partial(update_kernel, turns), out_shape=shapes,...  2.46 us
    ppermute x3, waiting for transfers between devices, flipped(): return lax.ppermute(value, ('y', 'core'), pairs)  2.44 us
    pallas_call x1, Pallas kernels, first_partials(): pl.pallas_call(first_kernel, out_shape=jax.ShapeDtypeStruct((peers, 3 * o...  2.42 us
  transfers between devices with their start and end apart: 9, of which 8 were waited for; matrix products, arithmetic and copies ran while one was open for 1% of the time, Pallas kernels for 1%

profile of v9, /device:TPU:1, one launch (start us, length us, event | category | flops | bytes accessed | tf_op | source)
XLA Modules:
  0.0 66.6 jit_solution(804477902493443460)
XLA Ops:
  0.6 0.0 copy-start.2
  0.6 2.4 %partials.1 = f32[32,24,128]{2,1,0:T(8,128)} custom-call(f32[2,64,256]{2,1,0:T(8,128)} %bitcast.26, f32[2,64,128]{2,1,0:T(8,128)} %rhs_hbm.1, bf16[256,128]{1,0:T(8,128)(2,1)} %modes_hbm.1, bf16[2,256,128]{2,1,0:T(8,128)(2,1)} %solved_hbm.1), custom_call_target="tpu_custom_call" | custom-call | tf_op jit(solution)/shard_map/partials/pallas_call | solution.py:81
  3.1 11.9 %all-to-all-start = ((f32[32,24,128]{2,1,0:T(8,128)}), f32[32,24,128]{2,1,0:T(8,128)S(1)}, u32[]{:S(2)}, u32[]{:S(2)}) async-start(f32[32,24,128]{2,1,0:T(8,128)} %partials.1), calls=%async_computation | async-start | bytes 786432 | tf_op jit(solution)/shard_map/all_to_all | solution.py:188
  15.0 0.7 %convert_element_type.39.modes_ref = f32[8,128]{1,0:T(8,128)S(1)} convert(bf16[8,128]{1,0:T(8,128)(2,1)} %param.13) | non-fusion elementwise | flops 1024 | bytes 6144 | tf_op jit(solution)/shard_map/convert_element_type | solution.py:189
  15.6 13.1 %all-to-all-done.came_ref = f32[32,24,128]{2,1,0:T(8,128)S(1)} async-done(((f32[32,24,128]{2,1,0:T(8,128)}), f32[32,24,128]{2,1,0:T(8,128)S(1)}, u32[]{:S(2)}, u32[]{:S(2)}) %all-to-all-start) | async-done | bytes 393248 | tf_op jit(solution)/shard_map/all_to_all | solution.py:188
  28.8 0.1 pack.1
  28.8 16.0 %all_to_all.10 = bf16[32,40,128]{2,1,0:T(8,128)(2,1)S(1)} all-to-all(bf16[32,40,128]{2,1,0:T(8,128)(2,1)S(1)} %get-tuple-element.13), channel_id=1, replica_groups=mesh['y'=4,'core'=2,'z'=8,'x'=4] {'z','x'}, dimensions={0} | all-to-all | bytes 655360 | tf_op jit(solution)/shard_map/all_to_all | solution.py:190
  44.9 0.2 fusion.1
  45.2 3.0 %collective-permute-start.1 = (bf16[512,256]{1,0:T(8,128)(2,1)S(1)}, bf16[512,256]{1,0:T(8,128)(2,1)S(1)}, u32[]{:S(2)}, u32[]{:S(2)}) collective-permute-start(bf16[512,256]{1,0:T(8,128)(2,1)S(1)} %maximum_maximum_fusion), channel_id=1, source_target_pairs={{0,128},{32,160},{64,192},{96,224},{128,0},{160,32},{192,64},{224,... | collective-permute-start | bytes 786440 | tf_op jit(solution)/shard_map/ppermute | solution.py:26
  48.2 4.4 %collective-permute-start = (bf16[256,256]{1,0:T(8,128)(2,1)S(1)}, bf16[256,256]{1,0:T(8,128)(2,1)S(1)}, u32[]{:S(2)}, u32[]{:S(2)}) collective-permute-start(bf16[256,256]{1,0:T(8,128)(2,1)S(1)} %pad_maximum_fusion.rest_0_), channel_id=1, source_target_pairs={{0,32},{32,0},{1,33},{33,1},{2,34},{34,2},{3,35},{35,3},{4,36},{36... | collective-permute-start | bytes 393224 | tf_op jit(solution)/shard_map/ppermute | solution.py:21
  52.6 0.4 collective-permute-start.4
  53.0 0.4 collective-permute-start.3
  53.4 0.2 collective-permute-done.rest_1_
  53.6 0.0 copy-done.2
  53.6 0.0 copy-start
  53.6 2.2 %copy-done = bf16[2,512,2048]{2,1,0:T(8,128)(2,1)S(1)} copy-done((bf16[2,512,2048]{2,1,0:T(8,128)(2,1)S(1)}, bf16[2,512,2048]{2,1,0:T(8,128)(2,1)}, u32[]{:S(2)}) %copy-start) | copy-done | bytes 4194328
  55.8 0.5 update_own.1.rhs_ref
  56.2 0.0 copy-start.1
  56.2 0.0 collective-permute-done.1.rest_0_
  56.3 2.7 %collective-permute-start.2 = (bf16[256,256]{1,0:T(8,128)(2,1)S(1)}, bf16[256,256]{1,0:T(8,128)(2,1)S(1)}, u32[]{:S(2)}, u32[]{:S(2)}) collective-permute-start(bf16[256,256]{1,0:T(8,128)(2,1)S(1)} %slice.64), channel_id=1, source_target_pairs={{0,32},{32,0},{1,33},{33,1},{2,34},{34,2},{3,35},{35,3},{4,36},{36... | collective-permute-start | bytes 393224 | tf_op jit(solution)/shard_map/ppermute | solution.py:21
  59.0 1.0 %collective-permute-done.2.rest_1_ = bf16[256,256]{1,0:T(8,128)(2,1)S(1)} collective-permute-done((bf16[256,256]{1,0:T(8,128)(2,1)S(1)}, bf16[256,256]{1,0:T(8,128)(2,1)S(1)}, u32[]{:S(2)}, u32[]{:S(2)}) %collective-permute-start.2) | collective-permute-done | bytes 131104 | tf_op jit(solution)/shard_map/ppermute | solution.py:21
  59.9 0.5 update_early.1.rhs_ref
  60.4 0.5 collective-permute-done.4.rest_2_
  60.9 1.9 %collective-permute-done.3.rest_0_ = bf16[512,256]{1,0:T(8,128)(2,1)S(1)} collective-permute-done((bf16[512,256]{1,0:T(8,128)(2,1)S(1)}, bf16[512,256]{1,0:T(8,128)(2,1)S(1)}, u32[]{:S(2)}, u32[]{:S(2)}) %collective-permute-start.3) | collective-permute-done | bytes 262176 | tf_op jit(solution)/shard_map/ppermute | solution.py:26
  62.8 0.1 add_add_fusion.rest_4_
  62.9 0.6 collective-permute-start.6
  63.5 0.1 collective-permute-start.5
  63.6 0.4 collective-permute-start.7
  64.0 0.5 collective-permute-done.6.rest_3_
  64.5 0.4 collective-permute-done.5.rest_1_
  64.9 0.2 collective-permute-done.7.rest_5_
  65.0 0.0 copy-done.1
  65.0 1.5 %update_late.1 = (f32[2,512,128]{2,1,0:T(8,128)}, f32[256,128]{1,0:T(8,128)}, f32[16,128]{1,0:T(8,128)}) custom-call(bf16[2,512,2048]{2,1,0:T(8,128)(2,1)S(1)} %copy-done.1, f32[2,512,128]{2,1,0:T(8,128)S(1)} %update_early.1.rhs_ref, bf16[512,256]{1,0:T(8,128)(2,1)S(1)} %collective-permute-done.3.rest_0_, ...), custom_call_target="tpu_custom_call" | custom-call | flops 536870912 | bytes 2097152 | tf_op jit(solution)/shard_map/update_late/pallas_call | solution.py:166
  (9 shorter events, 0.2 us)
Async XLA Ops:
  0.6 52.9 %copy-start.2 = (f32[2,512,128]{2,1,0:T(8,128)S(1)}, f32[2,512,128]{2,1,0:T(8,128)}, u32[]{:S(2)}) copy-start(f32[2,512,128]{2,1,0:T(8,128)} %rhs_ref.1) | copy-start | bytes 1572868
  3.1 25.7 %all-to-all-start = ((f32[32,24,128]{2,1,0:T(8,128)}), f32[32,24,128]{2,1,0:T(8,128)S(1)}, u32[]{:S(2)}, u32[]{:S(2)}) async-start(f32[32,24,128]{2,1,0:T(8,128)} %partials.1), calls=%async_computation | async-start | bytes 786432 | tf_op jit(solution)/shard_map/all_to_all | solution.py:188
  45.2 11.0 %collective-permute-start.1 = (bf16[512,256]{1,0:T(8,128)(2,1)S(1)}, bf16[512,256]{1,0:T(8,128)(2,1)S(1)}, u32[]{:S(2)}, u32[]{:S(2)}) collective-permute-start(bf16[512,256]{1,0:T(8,128)(2,1)S(1)} %maximum_maximum_fusion), channel_id=1, source_target_pairs={{0,128},{32,160},{64,192},{96,224},{128,0},{160,32},{192,64},{224,... | collective-permute-start | bytes 786440 | tf_op jit(solution)/shard_map/ppermute | solution.py:26
  48.2 5.4 %collective-permute-start = (bf16[256,256]{1,0:T(8,128)(2,1)S(1)}, bf16[256,256]{1,0:T(8,128)(2,1)S(1)}, u32[]{:S(2)}, u32[]{:S(2)}) collective-permute-start(bf16[256,256]{1,0:T(8,128)(2,1)S(1)} %pad_maximum_fusion.rest_0_), channel_id=1, source_target_pairs={{0,32},{32,0},{1,33},{33,1},{2,34},{34,2},{3,35},{35,3},{4,36},{36... | collective-permute-start | bytes 393224 | tf_op jit(solution)/shard_map/ppermute | solution.py:21
  52.6 8.3 %collective-permute-start.4 = (bf16[512,256]{1,0:T(8,128)(2,1)S(1)}, bf16[512,256]{1,0:T(8,128)(2,1)S(1)}, u32[]{:S(2)}, u32[]{:S(2)}) collective-permute-start(bf16[512,256]{1,0:T(8,128)(2,1)S(1)} %maximum_maximum_fusion), channel_id=1, source_target_pairs={{0,192},{32,96},{64,128},{96,32},{128,64},{160,224},{192,0},{224,1... | collective-permute-start | bytes 786440 | tf_op jit(solution)/shard_map/ppermute | solution.py:26
  53.0 9.8 %collective-permute-start.3 = (bf16[512,256]{1,0:T(8,128)(2,1)S(1)}, bf16[512,256]{1,0:T(8,128)(2,1)S(1)}, u32[]{:S(2)}, u32[]{:S(2)}) collective-permute-start(bf16[512,256]{1,0:T(8,128)(2,1)S(1)} %maximum_maximum_fusion), channel_id=1, source_target_pairs={{0,64},{32,224},{64,0},{96,160},{128,192},{160,96},{192,128},{224,... | collective-permute-start | bytes 786440 | tf_op jit(solution)/shard_map/ppermute | solution.py:26
  53.6 2.2 %copy-start = (bf16[2,512,2048]{2,1,0:T(8,128)(2,1)S(1)}, bf16[2,512,2048]{2,1,0:T(8,128)(2,1)}, u32[]{:S(2)}) copy-start(bf16[2,512,2048]{2,1,0:T(8,128)(2,1)} %factor_ref.5) | copy-start | bytes 12582916
  56.2 8.8 %copy-start.1 = (bf16[2,512,2048]{2,1,0:T(8,128)(2,1)S(1)}, bf16[2,512,2048]{2,1,0:T(8,128)(2,1)}, u32[]{:S(2)}) copy-start(bf16[2,512,2048]{2,1,0:T(8,128)(2,1)} %factor_ref.5) | copy-start | bytes 12582916
  56.3 3.7 %collective-permute-start.2 = (bf16[256,256]{1,0:T(8,128)(2,1)S(1)}, bf16[256,256]{1,0:T(8,128)(2,1)S(1)}, u32[]{:S(2)}, u32[]{:S(2)}) collective-permute-start(bf16[256,256]{1,0:T(8,128)(2,1)S(1)} %slice.64), channel_id=1, source_target_pairs={{0,32},{32,0},{1,33},{33,1},{2,34},{34,2},{3,35},{35,3},{4,36},{36... | collective-permute-start | bytes 393224 | tf_op jit(solution)/shard_map/ppermute | solution.py:21
  62.9 1.6 %collective-permute-start.6 = (bf16[256,256]{1,0:T(8,128)(2,1)S(1)}, bf16[256,256]{1,0:T(8,128)(2,1)S(1)}, u32[]{:S(2)}, u32[]{:S(2)}) collective-permute-start(bf16[256,256]{1,0:T(8,128)(2,1)S(1)} %slice.66), channel_id=1, source_target_pairs={{0,32},{32,0},{1,33},{33,1},{2,34},{34,2},{3,35},{35,3},{4,36},{36... | collective-permute-start | bytes 393224 | tf_op jit(solution)/shard_map/ppermute | solution.py:21
  63.5 1.3 %collective-permute-start.5 = (bf16[256,256]{1,0:T(8,128)(2,1)S(1)}, bf16[256,256]{1,0:T(8,128)(2,1)S(1)}, u32[]{:S(2)}, u32[]{:S(2)}) collective-permute-start(bf16[256,256]{1,0:T(8,128)(2,1)S(1)} %slice.65), channel_id=1, source_target_pairs={{0,32},{32,0},{1,33},{33,1},{2,34},{34,2},{3,35},{35,3},{4,36},{36... | collective-permute-start | bytes 393224 | tf_op jit(solution)/shard_map/ppermute | solution.py:21
  63.6 1.4 %collective-permute-start.7 = (f32[256,128]{1,0:T(8,128)S(1)}, f32[256,128]{1,0:T(8,128)S(1)}, u32[]{:S(2)}, u32[]{:S(2)}) collective-permute-start(f32[256,128]{1,0:T(8,128)S(1)} %add_add_fusion.rest_4_), channel_id=1, source_target_pairs={{0,32},{32,0},{1,33},{33,1},{2,34},{34,2},{3,35},{35,3},{4,36},{36... | collective-permute-start | bytes 393224 | tf_op jit(solution)/shard_map/ppermute | solution.py:21

commit v10 on v8

--- a/solution.py
+++ b/solution.py
@@ -1,5 +1,3 @@
-import functools
-
 import jax
 import jax.numpy as jnp
 from jax import lax
@@ -119,18 +117,7 @@
     )(came, modes_panel)
 
 
-def update_kernel(turns, factor_ref, rhs_ref, *rest):
-    count = 2 * len(turns)
-    blocks, rest = rest[:count], rest[count:]
-    if len(rest) == 1:
-        (out_ref,) = rest
-    else:
-        modal_ref, back_ref, summed_ref, out_ref, forces_ref, panel_ref = rest
-        forces_ref[...] = modal_ref[...] + back_ref[...]
-        panel_ref[...] = summed_ref[: panel_ref.shape[0], :]
-    width = out_ref.shape[2]
-    depth = 2 * width
-    rows = factor_ref.shape[1]
+def block_pieces(turns, blocks, depth):
     y = lax.axis_index("y")
     core = lax.axis_index("core")
     pieces = []
@@ -140,40 +127,89 @@
         place = jnp.bitwise_xor(y, low + (high - low) * source) * 2 + source
         columns = pl.ds(pl.multiple_of(place * depth, depth), depth)
         straight = block_ref[:depth, :]
-        crossed = jnp.concatenate([-straight[:, width:], straight[:, :width]], axis=1)
+        half = depth // 2
+        crossed = jnp.concatenate([-straight[:, half:], straight[:, :half]], axis=1)
         pieces.append((columns, straight, crossed))
-    for at in range(0, rows, CHUNK):
-        span = slice(at, at + CHUNK)
-        product = jnp.zeros((CHUNK, depth), F32)
-        for columns, straight, crossed in pieces:
-            product += jnp.dot(factor_ref[0, span, columns], straight, preferred_element_type=F32)
-            product += jnp.dot(factor_ref[1, span, columns], crossed, preferred_element_type=F32)
-        out_ref[0, span, :] = rhs_ref[0, span, :] - product[:, :width]
-        out_ref[1, span, :] = rhs_ref[1, span, :] - product[:, width:]
-
-
-def update(turns, factor_slab, rhs, blocks, name, others=()):
-    depth = 2 * rhs.shape[2]
-    rows = factor_slab.shape[1]
+    return pieces
+
+
+def subtract(factor_ref, rhs_ref, out_ref, pieces, span):
+    width = out_ref.shape[2]
+    product = jnp.zeros((CHUNK, 2 * width), F32)
+    for columns, straight, crossed in pieces:
+        product += jnp.dot(factor_ref[0, span, columns], straight, preferred_element_type=F32)
+        product += jnp.dot(factor_ref[1, span, columns], crossed, preferred_element_type=F32)
+    out_ref[0, span, :] = rhs_ref[0, span, :] - product[:, :width]
+    out_ref[1, span, :] = rhs_ref[1, span, :] - product[:, width:]
+
+
+def own_kernel(factor_ref, rhs_ref, block_ref, twin_ref, out_ref):
+    pieces = block_pieces(TURNS[:1], (block_ref, twin_ref), 2 * out_ref.shape[2])
+    for at in range(0, out_ref.shape[1], CHUNK):
+        subtract(factor_ref, rhs_ref, out_ref, pieces, slice(at, at + CHUNK))
+
+
+def update_own(factor_slab, rhs, block, twin):
     vmem = pl.BlockSpec(memory_space=pltpu.VMEM)
-    shapes = [jax.ShapeDtypeStruct(rhs.shape, F32)]
-    if others:
-        modal, _, summed = others
-        shapes.append(jax.ShapeDtypeStruct(modal.shape, F32))
-        shapes.append(jax.ShapeDtypeStruct((summed.shape[0] * 2 // 3, summed.shape[1]), F32))
-    return pl.pallas_call(
-        functools.partial(update_kernel, turns),
-        out_shape=shapes,
-        in_specs=[vmem] * (2 + len(blocks) + len(others)),
-        out_specs=[vmem] * len(shapes),
-        cost_estimate=pl.CostEstimate(
-            flops=len(blocks) * 4 * rows * depth * 2 * rhs.shape[2],
-            bytes_accessed=len(blocks) * 4 * rows * depth,
-            transcendentals=0,
-        ),
+    return pl.pallas_call(
+        own_kernel,
+        out_shape=jax.ShapeDtypeStruct(rhs.shape, F32),
+        in_specs=[vmem] * 4,
+        out_specs=vmem,
+        cost_estimate=update_cost(factor_slab, rhs, 2),
         compiler_params=pltpu.CompilerParams(vmem_limit_bytes=24 << 20),
-        name=name,
-    )(factor_slab, rhs, *blocks, *others)
+        name="update_own",
+    )(factor_slab, rhs, block, twin)
+
+
+def rest_kernel(factor_ref, rhs_ref, pair_ref, summed_ref, *rest):
+    count = 2 * len(TURNS[1:])
+    blocks = rest[:count]
+    out_hbm, forces_hbm, panel_hbm, out_ref, forces_ref, panel_ref, sems = rest[count:]
+    depth = 2 * out_ref.shape[2]
+    forces_ref[...] = joined(pair_ref[...]) + joined(blocks[-1][depth:, :])
+    panel_ref[...] = summed_ref[: panel_ref.shape[0], :]
+    moves = [
+        pltpu.make_async_copy(forces_ref, forces_hbm, sems.at[0]),
+        pltpu.make_async_copy(panel_ref, panel_hbm, sems.at[1]),
+    ]
+    for move in moves:
+        move.start()
+    pieces = block_pieces(TURNS[1:], blocks, depth)
+    for at in range(0, out_ref.shape[1], CHUNK):
+        subtract(factor_ref, rhs_ref, out_ref, pieces, slice(at, at + CHUNK))
+        rows = pl.ds(at, CHUNK)
+        move = pltpu.make_async_copy(
+            out_ref.at[:, rows, :], out_hbm.at[:, rows, :], sems.at[2 + at // CHUNK]
+        )
+        move.start()
+        moves.append(move)
+    for move in moves:
+        move.wait()
+
+
+def update_rest(factor_slab, rhs, blocks, pair, summed):
+    width = rhs.shape[2]
+    vmem = pl.BlockSpec(memory_space=pltpu.VMEM)
+    shapes = [rhs.shape, (pair.shape[0], width), (summed.shape[0] * 2 // 3, width)]
+    return pl.pallas_call(
+        rest_kernel,
+        out_shape=[jax.ShapeDtypeStruct(shape, F32) for shape in shapes],
+        in_specs=[vmem] * (4 + len(blocks)),
+        out_specs=[pl.BlockSpec(memory_space=pl.ANY)] * len(shapes),
+        scratch_shapes=[pltpu.VMEM(shape, F32) for shape in shapes]
+        + [pltpu.SemaphoreType.DMA((2 + rhs.shape[1] // CHUNK,))],
+        cost_estimate=update_cost(factor_slab, rhs, len(blocks)),
+        compiler_params=pltpu.CompilerParams(vmem_limit_bytes=24 << 20),
+        name="update_rest",
+    )(factor_slab, rhs, pair, summed, *blocks)
+
+
+def update_cost(factor_slab, rhs, count):
+    elements = count * 2 * factor_slab.shape[1] * 2 * rhs.shape[2]
+    return pl.CostEstimate(
+        flops=elements * 4 * rhs.shape[2], bytes_accessed=2 * elements, transcendentals=0
+    )
 
 
 def on_device(
@@ -203,19 +239,15 @@
     modal = split(share.reshape(2 * width, width))
     sent = jnp.concatenate([block, modal], axis=0)
     came = [flipped(sent, k) for k in TURNS[1:]]
-    (started,) = update(TURNS[:1], factor_slab, pending_rhs, [block, twin], "update_own")
+    started = update_own(factor_slab, pending_rhs, block, twin)
     started, came = lax.optimization_barrier((started, came))
     depth = block.shape[0]
-    twins = [swapped(c[:depth]) for c in came]
     first, third, second = (joined(c[depth:]) for c in came)
-    modal = (joined(modal) + second) + (first + third)
-    updated_rhs, modal_forces, panel_solution = update(
-        TURNS[1:],
-        factor_slab,
-        started,
-        [b for two in zip(came, twins) for b in two],
-        "update_rest",
-        (modal, swapped(modal), summed),
+    pair = split((joined(modal) + second) + (first + third))
+    twins = [swapped(c[:depth]) for c in came[:-1]]
+    twins.append(swapped(jnp.concatenate([came[-1][:depth], pair], axis=0)))
+    updated_rhs, modal_forces, panel_solution = update_rest(
+        factor_slab, started, [b for two in zip(came, twins) for b in two], pair, summed
     )
     modal_forces = modal_forces.reshape(2, width, width)
     panel_solution = panel_solution.reshape(2, own, width)

time: 65.7 us -> 65.5 us (level)
    ppermute x5 -> x4, waiting for transfers between devices: 2.23 us -> 1.99 us  [swapped(): return lax.ppermute(value, 'core', SWAP)]
    ppermute x5 -> x4, starting transfers between devices: 8.74 us -> 8.72 us  [swapped(): return lax.ppermute(value, 'core', SWAP)]
  transfers between devices with their start and end apart: 9 -> 8, of which waited for: 7 -> 5; matrix products, arithmetic and copies ran while one was open for 1% -> 1% of each run, Pallas kernels for 1% -> 1%
where the time goes in v10:
time: 65.5 us; the launch traced here: 65.3 us
  starting transfers between devices  24.4 us (37%)
  waiting for transfers between devices  16 us (24%)
  blocking collectives  16 us (24%)
  Pallas kernels  4.74 us (7%)
  local copies, waits for them, and re-layouts  2.25 us (3%)
  other arithmetic  0.93 us (1%)
  between operations  0.76 us (1%)
    all_to_all x1, blocking collectives, on_device(): gathered = lax.all_to_all(packed, COL, 0, 0, tiled=True)  16 us
    all_to_all x1, waiting for transfers between devices, on_device(): came = lax.all_to_all(outgoing, COL, 0, 0, tiled=True)  13.1 us
    all_to_all x1, starting transfers between devices, on_device(): came = lax.all_to_all(outgoing, COL, 0, 0, tiled=True)  11.9 us
    ppermute x4, starting transfers between devices, swapped(): return lax.ppermute(value, 'core', SWAP)  8.72 us
    ppermute x3, starting transfers between devices, flipped(): return lax.ppermute(value, ('y', 'core'), pairs)  3.77 us
    pallas_call x1, Pallas kernels, first_partials(): pl.pallas_call(first_kernel, out_shape=jax.ShapeDtypeStruct((peers, 3 * o...  2.42 us
    unnamed x6, local copies, waits for them, and re-layouts  2.2 us
    ppermute x4, waiting for transfers between devices, swapped(): return lax.ppermute(value, 'core', SWAP)  1.99 us
  transfers between devices with their start and end apart: 8, of which 5 were waited for; matrix products, arithmetic and copies ran while one was open for 1% of the time, Pallas kernels for 1%

profile of v10, /device:TPU:1, one launch (start us, length us, event | category | flops | bytes accessed | tf_op | source)
XLA Modules:
  0.0 65.3 jit_solution(11864810214742262194)
XLA Ops:
  0.6 0.0 copy-start.2
  0.6 2.4 %partials.1 = f32[32,24,128]{2,1,0:T(8,128)} custom-call(f32[2,64,256]{2,1,0:T(8,128)} %bitcast.26, f32[2,64,128]{2,1,0:T(8,128)} %rhs_hbm.1, bf16[256,128]{1,0:T(8,128)(2,1)} %modes_hbm.1, bf16[2,256,128]{2,1,0:T(8,128)(2,1)} %solved_hbm.1), custom_call_target="tpu_custom_call" | custom-call | tf_op jit(solution)/shard_map/partials/pallas_call | solution.py:77
  3.1 11.9 %all-to-all-start = ((f32[32,24,128]{2,1,0:T(8,128)}), f32[32,24,128]{2,1,0:T(8,128)S(1)}, u32[]{:S(2)}, u32[]{:S(2)}) async-start(f32[32,24,128]{2,1,0:T(8,128)} %partials.1), calls=%async_computation | async-start | bytes 786432 | tf_op jit(solution)/shard_map/all_to_all | solution.py:222
  15.0 0.7 %convert_element_type.45.modes_ref = f32[8,128]{1,0:T(8,128)S(1)} convert(bf16[8,128]{1,0:T(8,128)(2,1)} %param.13) | non-fusion elementwise | flops 1024 | bytes 6144 | tf_op jit(solution)/shard_map/convert_element_type | solution.py:223
  15.6 13.1 %all-to-all-done.came_ref = f32[32,24,128]{2,1,0:T(8,128)S(1)} async-done(((f32[32,24,128]{2,1,0:T(8,128)}), f32[32,24,128]{2,1,0:T(8,128)S(1)}, u32[]{:S(2)}, u32[]{:S(2)}) %all-to-all-start) | async-done | bytes 393248 | tf_op jit(solution)/shard_map/all_to_all | solution.py:222
  28.8 0.1 pack.1
  28.8 16.0 %all_to_all.10 = bf16[32,40,128]{2,1,0:T(8,128)(2,1)S(1)} all-to-all(bf16[32,40,128]{2,1,0:T(8,128)(2,1)S(1)} %get-tuple-element.12), channel_id=1, replica_groups=mesh['y'=4,'core'=2,'z'=8,'x'=4] {'z','x'}, dimensions={0} | all-to-all | bytes 655360 | tf_op jit(solution)/shard_map/all_to_all | solution.py:224
  44.9 0.2 fusion.2
  45.2 3.0 %collective-permute-start.3 = (bf16[512,256]{1,0:T(8,128)(2,1)S(1)}, bf16[512,256]{1,0:T(8,128)(2,1)S(1)}, u32[]{:S(2)}, u32[]{:S(2)}) collective-permute-start(bf16[512,256]{1,0:T(8,128)(2,1)S(1)} %maximum_maximum_fusion), channel_id=1, source_target_pairs={{0,128},{32,160},{64,192},{96,224},{128,0},{160,32},{192,64},{224,... | collective-permute-start | bytes 786440 | tf_op jit(solution)/shard_map/ppermute | solution.py:22
  48.2 0.4 collective-permute-start.2
  48.6 0.4 collective-permute-start.1
  49.0 4.7 %collective-permute-start = (bf16[256,256]{1,0:T(8,128)(2,1)S(1)}, bf16[256,256]{1,0:T(8,128)(2,1)S(1)}, u32[]{:S(2)}, u32[]{:S(2)}) collective-permute-start(bf16[256,256]{1,0:T(8,128)(2,1)S(1)} %pad_maximum_fusion.block_ref), channel_id=1, source_target_pairs={{0,32},{32,0},{1,33},{33,1},{2,34},{34,2},{3,35},{35,3},{4,36},{36... | collective-permute-start | bytes 393224 | tf_op jit(solution)/shard_map/ppermute | solution.py:17
  53.6 1.0 %collective-permute-done.twin_ref = bf16[256,256]{1,0:T(8,128)(2,1)S(1)} collective-permute-done((bf16[256,256]{1,0:T(8,128)(2,1)S(1)}, bf16[256,256]{1,0:T(8,128)(2,1)S(1)}, u32[]{:S(2)}, u32[]{:S(2)}) %collective-permute-start) | collective-permute-done | bytes 131104 | tf_op jit(solution)/shard_map/ppermute | solution.py:17
  54.6 0.0 copy-done.2
  54.6 0.0 copy-start
  54.6 2.2 %copy-done = bf16[2,512,2048]{2,1,0:T(8,128)(2,1)S(1)} copy-done((bf16[2,512,2048]{2,1,0:T(8,128)(2,1)S(1)}, bf16[2,512,2048]{2,1,0:T(8,128)(2,1)}, u32[]{:S(2)}) %copy-start) | copy-done | bytes 4194328
  56.8 0.0 copy-start.1
  56.8 0.5 update_own.1.rhs_ref
  57.3 0.0 collective-permute-done.3.rest_4_
  57.3 0.0 collective-permute-done.2.rest_2_
  57.3 0.9 %collective-permute-done.1.rest_0_ = bf16[512,256]{1,0:T(8,128)(2,1)S(1)} collective-permute-done((bf16[512,256]{1,0:T(8,128)(2,1)S(1)}, bf16[512,256]{1,0:T(8,128)(2,1)S(1)}, u32[]{:S(2)}, u32[]{:S(2)}) %collective-permute-start.1) | collective-permute-done | bytes 262176 | tf_op jit(solution)/shard_map/ppermute | solution.py:22
  58.2 0.1 reduce-precision_convert_fusion
  58.3 3.5 %collective-permute-start.6 = (bf16[512,256]{1,0:T(8,128)(2,1)S(1)}, bf16[512,256]{1,0:T(8,128)(2,1)S(1)}, u32[]{:S(2)}, u32[]{:S(2)}) collective-permute-start(bf16[512,256]{1,0:T(8,128)(2,1)S(1)} %maximum_maximum_fusion.1), channel_id=1, source_target_pairs={{0,32},{32,0},{1,33},{33,1},{2,34},{34,2},{3,35},{35,3},{4,36},{36... | collective-permute-start | bytes 786440 | tf_op jit(solution)/shard_map/ppermute | solution.py:17
  61.8 0.1 collective-permute-start.5
  61.9 0.5 collective-permute-start.4
  62.4 0.8 %collective-permute-done.5.rest_3_ = bf16[256,256]{1,0:T(8,128)(2,1)S(1)} collective-permute-done((bf16[256,256]{1,0:T(8,128)(2,1)S(1)}, bf16[256,256]{1,0:T(8,128)(2,1)S(1)}, u32[]{:S(2)}, u32[]{:S(2)}) %collective-permute-start.5) | collective-permute-done | bytes 131104 | tf_op jit(solution)/shard_map/ppermute | solution.py:17
  63.3 0.2 collective-permute-done.4.rest_1_
  63.4 0.0 collective-permute-done.6.rest_5_
  63.4 0.0 copy-done.1
  63.5 1.8 %update_rest.1 = (f32[2,512,128]{2,1,0:T(8,128)}, f32[256,128]{1,0:T(8,128)}, f32[16,128]{1,0:T(8,128)}) custom-call(bf16[2,512,2048]{2,1,0:T(8,128)(2,1)S(1)} %copy-done.1, f32[2,512,128]{2,1,0:T(8,128)S(1)} %update_own.1.rhs_ref, bf16[256,256]{1,0:T(8,128)(2,1)S(1)} %pad_maximum_fusion.2.pair_ref, f32[24,128]{1,0:T(8,128)S(1)} %get-tuple-element.17.summed_ref, ...), custom_call_target="tpu_custom_call" | custom-call | flops 805306368 | bytes 3145728 | tf_op jit(solution)/shard_map/update_rest/pallas_call | solution.py:195
  (12 shorter events, 0.2 us)
Async XLA Ops:
  0.6 54.0 %copy-start.2 = (f32[2,512,128]{2,1,0:T(8,128)S(1)}, f32[2,512,128]{2,1,0:T(8,128)}, u32[]{:S(2)}) copy-start(f32[2,512,128]{2,1,0:T(8,128)} %rhs_ref.1) | copy-start | bytes 1572868
  3.1 25.7 %all-to-all-start = ((f32[32,24,128]{2,1,0:T(8,128)}), f32[32,24,128]{2,1,0:T(8,128)S(1)}, u32[]{:S(2)}, u32[]{:S(2)}) async-start(f32[32,24,128]{2,1,0:T(8,128)} %partials.1), calls=%async_computation | async-start | bytes 786432 | tf_op jit(solution)/shard_map/all_to_all | solution.py:222
  45.2 12.1 %collective-permute-start.3 = (bf16[512,256]{1,0:T(8,128)(2,1)S(1)}, bf16[512,256]{1,0:T(8,128)(2,1)S(1)}, u32[]{:S(2)}, u32[]{:S(2)}) collective-permute-start(bf16[512,256]{1,0:T(8,128)(2,1)S(1)} %maximum_maximum_fusion), channel_id=1, source_target_pairs={{0,128},{32,160},{64,192},{96,224},{128,0},{160,32},{192,64},{224,... | collective-permute-start | bytes 786440 | tf_op jit(solution)/shard_map/ppermute | solution.py:22
  48.2 9.1 %collective-permute-start.2 = (bf16[512,256]{1,0:T(8,128)(2,1)S(1)}, bf16[512,256]{1,0:T(8,128)(2,1)S(1)}, u32[]{:S(2)}, u32[]{:S(2)}) collective-permute-start(bf16[512,256]{1,0:T(8,128)(2,1)S(1)} %maximum_maximum_fusion), channel_id=1, source_target_pairs={{0,192},{32,96},{64,128},{96,32},{128,64},{160,224},{192,0},{224,1... | collective-permute-start | bytes 786440 | tf_op jit(solution)/shard_map/ppermute | solution.py:22
  48.6 9.6 %collective-permute-start.1 = (bf16[512,256]{1,0:T(8,128)(2,1)S(1)}, bf16[512,256]{1,0:T(8,128)(2,1)S(1)}, u32[]{:S(2)}, u32[]{:S(2)}) collective-permute-start(bf16[512,256]{1,0:T(8,128)(2,1)S(1)} %maximum_maximum_fusion), channel_id=1, source_target_pairs={{0,64},{32,224},{64,0},{96,160},{128,192},{160,96},{192,128},{224,... | collective-permute-start | bytes 786440 | tf_op jit(solution)/shard_map/ppermute | solution.py:22
  49.0 5.6 %collective-permute-start = (bf16[256,256]{1,0:T(8,128)(2,1)S(1)}, bf16[256,256]{1,0:T(8,128)(2,1)S(1)}, u32[]{:S(2)}, u32[]{:S(2)}) collective-permute-start(bf16[256,256]{1,0:T(8,128)(2,1)S(1)} %pad_maximum_fusion.block_ref), channel_id=1, source_target_pairs={{0,32},{32,0},{1,33},{33,1},{2,34},{34,2},{3,35},{35,3},{4,36},{36... | collective-permute-start | bytes 393224 | tf_op jit(solution)/shard_map/ppermute | solution.py:17
  54.6 2.2 %copy-start = (bf16[2,512,2048]{2,1,0:T(8,128)(2,1)S(1)}, bf16[2,512,2048]{2,1,0:T(8,128)(2,1)}, u32[]{:S(2)}) copy-start(bf16[2,512,2048]{2,1,0:T(8,128)(2,1)} %factor_ref.3) | copy-start | bytes 12582916
  56.8 6.6 %copy-start.1 = (bf16[2,512,2048]{2,1,0:T(8,128)(2,1)S(1)}, bf16[2,512,2048]{2,1,0:T(8,128)(2,1)}, u32[]{:S(2)}) copy-start(bf16[2,512,2048]{2,1,0:T(8,128)(2,1)} %factor_ref.3) | copy-start | bytes 12582916
  58.3 5.1 %collective-permute-start.6 = (bf16[512,256]{1,0:T(8,128)(2,1)S(1)}, bf16[512,256]{1,0:T(8,128)(2,1)S(1)}, u32[]{:S(2)}, u32[]{:S(2)}) collective-permute-start(bf16[512,256]{1,0:T(8,128)(2,1)S(1)} %maximum_maximum_fusion.1), channel_id=1, source_target_pairs={{0,32},{32,0},{1,33},{33,1},{2,34},{34,2},{3,35},{35,3},{4,36},{36... | collective-permute-start | bytes 786440 | tf_op jit(solution)/shard_map/ppermute | solution.py:17
  61.8 1.4 %collective-permute-start.5 = (bf16[256,256]{1,0:T(8,128)(2,1)S(1)}, bf16[256,256]{1,0:T(8,128)(2,1)S(1)}, u32[]{:S(2)}, u32[]{:S(2)}) collective-permute-start(bf16[256,256]{1,0:T(8,128)(2,1)S(1)} %slice.71), channel_id=1, source_target_pairs={{0,32},{32,0},{1,33},{33,1},{2,34},{34,2},{3,35},{35,3},{4,36},{36... | collective-permute-start | bytes 393224 | tf_op jit(solution)/shard_map/ppermute | solution.py:17
  61.9 1.5 %collective-permute-start.4 = (bf16[256,256]{1,0:T(8,128)(2,1)S(1)}, bf16[256,256]{1,0:T(8,128)(2,1)S(1)}, u32[]{:S(2)}, u32[]{:S(2)}) collective-permute-start(bf16[256,256]{1,0:T(8,128)(2,1)S(1)} %slice.70), channel_id=1, source_target_pairs={{0,32},{32,0},{1,33},{33,1},{2,34},{34,2},{3,35},{35,3},{4,36},{36... | collective-permute-start | bytes 393224 | tf_op jit(solution)/shard_map/ppermute | solution.py:17

commit v11 on v9

--- a/solution.py
+++ b/solution.py
@@ -208,7 +208,6 @@
     tail = [flipped(sent, turn) for turn in LATE]
     depth = block.shape[0]
     (started,) = update(OWN, factor_slab, pending_rhs, [block, twin], "update_own")
-    started, head = lax.optimization_barrier((started, head))
     (started,) = update(
         EARLY, factor_slab, started, [head, swapped(head[:depth])], "update_early"
     )

time: 66.9 us -> 65.7 us (0.982)
  waiting for transfers between devices: 17.8 us -> 14.4 us
  starting transfers between devices: 23.8 us -> 26 us
    ppermute x3, waiting for transfers between devices: 2.44 us -> 0.01 us  [flipped(): return lax.ppermute(value, ('y', 'core'), pairs)]
    ppermute x5, starting transfers between devices: 8.14 us -> 10.3 us  [swapped(): return lax.ppermute(value, 'core', SWAP)]
    ppermute x5, waiting for transfers between devices: 2.2 us -> 1.25 us  [swapped(): return lax.ppermute(value, 'core', SWAP)]
  transfers between devices with their start and end apart: 9 -> 9, of which waited for: 8 -> 4; matrix products, arithmetic and copies ran while one was open for 1% -> 1% of each run, Pallas kernels for 1% -> 1%
where the time goes in v11:
time: 65.7 us; the launch traced here: 65.4 us
  starting transfers between devices  26 us (40%)
  blocking collectives  16 us (24%)
  waiting for transfers between devices  14.4 us (22%)
  Pallas kernels  4.94 us (8%)
  local copies, waits for them, and re-layouts  2.26 us (3%)
  other arithmetic  0.85 us (1%)
  between operations  0.77 us (1%)
    all_to_all x1, blocking collectives, on_device(): gathered = lax.all_to_all(packed, COL, 0, 0, tiled=True)  16 us
    all_to_all x1, waiting for transfers between devices, on_device(): came = lax.all_to_all(outgoing, COL, 0, 0, tiled=True)  13.1 us
    all_to_all x1, starting transfers between devices, on_device(): came = lax.all_to_all(outgoing, COL, 0, 0, tiled=True)  11.9 us
    ppermute x5, starting transfers between devices, swapped(): return lax.ppermute(value, 'core', SWAP)  10.3 us
    ppermute x3, starting transfers between devices, flipped(): return lax.ppermute(value, ('y', 'core'), pairs)  3.77 us
    pallas_call x3, Pallas kernels, update(): pl.pallas_call(functools.partial(update_kernel, turns), out_shape=shapes,...  2.46 us
    pallas_call x1, Pallas kernels, first_partials(): pl.pallas_call(first_kernel, out_shape=jax.ShapeDtypeStruct((peers, 3 * o...  2.42 us
    unnamed x6, local copies, waits for them, and re-layouts  2.2 us
  transfers between devices with their start and end apart: 9, of which 4 were waited for; matrix products, arithmetic and copies ran while one was open for 1% of the time, Pallas kernels for 1%

profile of v11, /device:TPU:1, one launch (start us, length us, event | category | flops | bytes accessed | tf_op | source)
XLA Modules:
  0.0 65.4 jit_solution(2750359923232281208)
XLA Ops:
  0.6 0.0 copy-start.2
  0.6 2.4 %partials.1 = f32[32,24,128]{2,1,0:T(8,128)} custom-call(f32[2,64,256]{2,1,0:T(8,128)} %bitcast.26, f32[2,64,128]{2,1,0:T(8,128)} %rhs_hbm.1, bf16[256,128]{1,0:T(8,128)(2,1)} %modes_hbm.1, bf16[2,256,128]{2,1,0:T(8,128)(2,1)} %solved_hbm.1), custom_call_target="tpu_custom_call" | custom-call | tf_op jit(solution)/shard_map/partials/pallas_call | solution.py:81
  3.1 11.9 %all-to-all-start = ((f32[32,24,128]{2,1,0:T(8,128)}), f32[32,24,128]{2,1,0:T(8,128)S(1)}, u32[]{:S(2)}, u32[]{:S(2)}) async-start(f32[32,24,128]{2,1,0:T(8,128)} %partials.1), calls=%async_computation | async-start | bytes 786432 | tf_op jit(solution)/shard_map/all_to_all | solution.py:188
  15.0 0.7 %convert_element_type.39.modes_ref = f32[8,128]{1,0:T(8,128)S(1)} convert(bf16[8,128]{1,0:T(8,128)(2,1)} %param.13) | non-fusion elementwise | flops 1024 | bytes 6144 | tf_op jit(solution)/shard_map/convert_element_type | solution.py:189
  15.6 13.1 %all-to-all-done.came_ref = f32[32,24,128]{2,1,0:T(8,128)S(1)} async-done(((f32[32,24,128]{2,1,0:T(8,128)}), f32[32,24,128]{2,1,0:T(8,128)S(1)}, u32[]{:S(2)}, u32[]{:S(2)}) %all-to-all-start) | async-done | bytes 393248 | tf_op jit(solution)/shard_map/all_to_all | solution.py:188
  28.8 0.1 pack.1
  28.8 16.0 %all_to_all.10 = bf16[32,40,128]{2,1,0:T(8,128)(2,1)S(1)} all-to-all(bf16[32,40,128]{2,1,0:T(8,128)(2,1)S(1)} %get-tuple-element.11), channel_id=1, replica_groups=mesh['y'=4,'core'=2,'z'=8,'x'=4] {'z','x'}, dimensions={0} | all-to-all | bytes 655360 | tf_op jit(solution)/shard_map/all_to_all | solution.py:190
  44.9 0.2 fusion.1
  45.2 3.0 %collective-permute-start.1 = (bf16[512,256]{1,0:T(8,128)(2,1)S(1)}, bf16[512,256]{1,0:T(8,128)(2,1)S(1)}, u32[]{:S(2)}, u32[]{:S(2)}) collective-permute-start(bf16[512,256]{1,0:T(8,128)(2,1)S(1)} %maximum_maximum_fusion), channel_id=1, source_target_pairs={{0,128},{32,160},{64,192},{96,224},{128,0},{160,32},{192,64},{224,... | collective-permute-start | bytes 786440 | tf_op jit(solution)/shard_map/ppermute | solution.py:26
  48.2 0.4 collective-permute-start.4
  48.6 0.4 collective-permute-start.3
  49.0 4.7 %collective-permute-start = (bf16[256,256]{1,0:T(8,128)(2,1)S(1)}, bf16[256,256]{1,0:T(8,128)(2,1)S(1)}, u32[]{:S(2)}, u32[]{:S(2)}) collective-permute-start(bf16[256,256]{1,0:T(8,128)(2,1)S(1)} %pad_maximum_fusion.rest_0_), channel_id=1, source_target_pairs={{0,32},{32,0},{1,33},{33,1},{2,34},{34,2},{3,35},{35,3},{4,36},{36... | collective-permute-start | bytes 393224 | tf_op jit(solution)/shard_map/ppermute | solution.py:21
  53.6 0.0 collective-permute-done.1.rest_0_
  53.7 4.9 %collective-permute-start.2 = (bf16[256,256]{1,0:T(8,128)(2,1)S(1)}, bf16[256,256]{1,0:T(8,128)(2,1)S(1)}, u32[]{:S(2)}, u32[]{:S(2)}) collective-permute-start(bf16[256,256]{1,0:T(8,128)(2,1)S(1)} %slice.80), channel_id=1, source_target_pairs={{0,32},{32,0},{1,33},{33,1},{2,34},{34,2},{3,35},{35,3},{4,36},{36... | collective-permute-start | bytes 393224 | tf_op jit(solution)/shard_map/ppermute | solution.py:21
  58.5 0.0 collective-permute-done.rest_1_
  58.5 0.0 copy-done.2
  58.5 0.0 copy-start
  58.5 2.2 %copy-done = bf16[2,512,2048]{2,1,0:T(8,128)(2,1)S(1)} copy-done((bf16[2,512,2048]{2,1,0:T(8,128)(2,1)S(1)}, bf16[2,512,2048]{2,1,0:T(8,128)(2,1)}, u32[]{:S(2)}) %copy-start) | copy-done | bytes 4194328
  60.7 0.5 update_own.1.rhs_ref
  61.2 0.0 copy-start.1
  61.2 0.0 collective-permute-done.2.rest_1_
  61.2 0.5 update_early.1.rhs_ref
  61.7 0.0 collective-permute-done.4.rest_2_
  61.7 0.0 collective-permute-done.3.rest_0_
  61.7 0.1 collective-permute-start.6
  61.8 0.5 collective-permute-start.5
  62.3 0.1 add_add_fusion.rest_4_
  62.4 0.2 collective-permute-start.7
  62.6 0.6 collective-permute-done.6.rest_3_
  63.2 0.2 collective-permute-done.5.rest_1_
  63.4 0.5 collective-permute-done.7.rest_5_
  63.8 0.0 copy-done.1
  63.8 1.5 %update_late.1 = (f32[2,512,128]{2,1,0:T(8,128)}, f32[256,128]{1,0:T(8,128)}, f32[16,128]{1,0:T(8,128)}) custom-call(bf16[2,512,2048]{2,1,0:T(8,128)(2,1)S(1)} %copy-done.1, f32[2,512,128]{2,1,0:T(8,128)S(1)} %update_early.1.rhs_ref, bf16[512,256]{1,0:T(8,128)(2,1)S(1)} %collective-permute-done.3.rest_0_, ...), custom_call_target="tpu_custom_call" | custom-call | flops 536870912 | bytes 2097152 | tf_op jit(solution)/shard_map/update_late/pallas_call | solution.py:166
  (9 shorter events, 0.2 us)
Async XLA Ops:
  0.6 57.9 %copy-start.2 = (f32[2,512,128]{2,1,0:T(8,128)S(1)}, f32[2,512,128]{2,1,0:T(8,128)}, u32[]{:S(2)}) copy-start(f32[2,512,128]{2,1,0:T(8,128)} %rhs_ref.1) | copy-start | bytes 1572868
  3.1 25.7 %all-to-all-start = ((f32[32,24,128]{2,1,0:T(8,128)}), f32[32,24,128]{2,1,0:T(8,128)S(1)}, u32[]{:S(2)}, u32[]{:S(2)}) async-start(f32[32,24,128]{2,1,0:T(8,128)} %partials.1), calls=%async_computation | async-start | bytes 786432 | tf_op jit(solution)/shard_map/all_to_all | solution.py:188
  45.2 8.5 %collective-permute-start.1 = (bf16[512,256]{1,0:T(8,128)(2,1)S(1)}, bf16[512,256]{1,0:T(8,128)(2,1)S(1)}, u32[]{:S(2)}, u32[]{:S(2)}) collective-permute-start(bf16[512,256]{1,0:T(8,128)(2,1)S(1)} %maximum_maximum_fusion), channel_id=1, source_target_pairs={{0,128},{32,160},{64,192},{96,224},{128,0},{160,32},{192,64},{224,... | collective-permute-start | bytes 786440 | tf_op jit(solution)/shard_map/ppermute | solution.py:26
  48.2 13.5 %collective-permute-start.4 = (bf16[512,256]{1,0:T(8,128)(2,1)S(1)}, bf16[512,256]{1,0:T(8,128)(2,1)S(1)}, u32[]{:S(2)}, u32[]{:S(2)}) collective-permute-start(bf16[512,256]{1,0:T(8,128)(2,1)S(1)} %maximum_maximum_fusion), channel_id=1, source_target_pairs={{0,192},{32,96},{64,128},{96,32},{128,64},{160,224},{192,0},{224,1... | collective-permute-start | bytes 786440 | tf_op jit(solution)/shard_map/ppermute | solution.py:26
  48.6 13.1 %collective-permute-start.3 = (bf16[512,256]{1,0:T(8,128)(2,1)S(1)}, bf16[512,256]{1,0:T(8,128)(2,1)S(1)}, u32[]{:S(2)}, u32[]{:S(2)}) collective-permute-start(bf16[512,256]{1,0:T(8,128)(2,1)S(1)} %maximum_maximum_fusion), channel_id=1, source_target_pairs={{0,64},{32,224},{64,0},{96,160},{128,192},{160,96},{192,128},{224,... | collective-permute-start | bytes 786440 | tf_op jit(solution)/shard_map/ppermute | solution.py:26
  49.0 9.5 %collective-permute-start = (bf16[256,256]{1,0:T(8,128)(2,1)S(1)}, bf16[256,256]{1,0:T(8,128)(2,1)S(1)}, u32[]{:S(2)}, u32[]{:S(2)}) collective-permute-start(bf16[256,256]{1,0:T(8,128)(2,1)S(1)} %pad_maximum_fusion.rest_0_), channel_id=1, source_target_pairs={{0,32},{32,0},{1,33},{33,1},{2,34},{34,2},{3,35},{35,3},{4,36},{36... | collective-permute-start | bytes 393224 | tf_op jit(solution)/shard_map/ppermute | solution.py:21
  53.7 7.5 %collective-permute-start.2 = (bf16[256,256]{1,0:T(8,128)(2,1)S(1)}, bf16[256,256]{1,0:T(8,128)(2,1)S(1)}, u32[]{:S(2)}, u32[]{:S(2)}) collective-permute-start(bf16[256,256]{1,0:T(8,128)(2,1)S(1)} %slice.80), channel_id=1, source_target_pairs={{0,32},{32,0},{1,33},{33,1},{2,34},{34,2},{3,35},{35,3},{4,36},{36... | collective-permute-start | bytes 393224 | tf_op jit(solution)/shard_map/ppermute | solution.py:21
  58.5 2.2 %copy-start = (bf16[2,512,2048]{2,1,0:T(8,128)(2,1)S(1)}, bf16[2,512,2048]{2,1,0:T(8,128)(2,1)}, u32[]{:S(2)}) copy-start(bf16[2,512,2048]{2,1,0:T(8,128)(2,1)} %factor_ref.5) | copy-start | bytes 12582916
  61.2 2.7 %copy-start.1 = (bf16[2,512,2048]{2,1,0:T(8,128)(2,1)S(1)}, bf16[2,512,2048]{2,1,0:T(8,128)(2,1)}, u32[]{:S(2)}) copy-start(bf16[2,512,2048]{2,1,0:T(8,128)(2,1)} %factor_ref.5) | copy-start | bytes 12582916
  61.7 1.4 %collective-permute-start.6 = (bf16[256,256]{1,0:T(8,128)(2,1)S(1)}, bf16[256,256]{1,0:T(8,128)(2,1)S(1)}, u32[]{:S(2)}, u32[]{:S(2)}) collective-permute-start(bf16[256,256]{1,0:T(8,128)(2,1)S(1)} %slice.66), channel_id=1, source_target_pairs={{0,32},{32,0},{1,33},{33,1},{2,34},{34,2},{3,35},{35,3},{4,36},{36... | collective-permute-start | bytes 393224 | tf_op jit(solution)/shard_map/ppermute | solution.py:21
  61.8 1.5 %collective-permute-start.5 = (bf16[256,256]{1,0:T(8,128)(2,1)S(1)}, bf16[256,256]{1,0:T(8,128)(2,1)S(1)}, u32[]{:S(2)}, u32[]{:S(2)}) collective-permute-start(bf16[256,256]{1,0:T(8,128)(2,1)S(1)} %slice.65), channel_id=1, source_target_pairs={{0,32},{32,0},{1,33},{33,1},{2,34},{34,2},{3,35},{35,3},{4,36},{36... | collective-permute-start | bytes 393224 | tf_op jit(solution)/shard_map/ppermute | solution.py:21
  62.4 1.4 %collective-permute-start.7 = (f32[256,128]{1,0:T(8,128)S(1)}, f32[256,128]{1,0:T(8,128)S(1)}, u32[]{:S(2)}, u32[]{:S(2)}) collective-permute-start(f32[256,128]{1,0:T(8,128)S(1)} %add_add_fusion.rest_4_), channel_id=1, source_target_pairs={{0,32},{32,0},{1,33},{33,1},{2,34},{34,2},{3,35},{35,3},{4,36},{36... | collective-permute-start | bytes 393224 | tf_op jit(solution)/shard_map/ppermute | solution.py:21

commit v12 on v9

--- a/solution.py
+++ b/solution.py
@@ -12,9 +12,9 @@
 COL = ("z", "x")
 SWAP = [(0, 1), (1, 0)]
 CHUNK = 128
-OWN = ((0, 0),)
-EARLY = ((2, 2),)
-LATE = ((1, 3), (3, 1))
+OWN = (((0, 0), 0),)
+EARLY = (((0, 0), 1), ((2, 2), 0), ((2, 2), 1))
+LATE = (((1, 3), 0), ((1, 3), 1), ((3, 1), 0), ((3, 1), 1))
 
 
 def swapped(value):
@@ -122,7 +122,7 @@
 
 
 def update_kernel(turns, factor_ref, rhs_ref, *rest):
-    count = 2 * len(turns)
+    count = len(turns)
     blocks, rest = rest[:count], rest[count:]
     if len(rest) == 1:
         (out_ref,) = rest
@@ -137,8 +137,8 @@
     core = lax.axis_index("core")
     pieces = []
     for j, block_ref in enumerate(blocks):
-        source = core if j % 2 == 0 else 1 - core
-        low, high = turns[j // 2]
+        (low, high), other = turns[j]
+        source = 1 - core if other else core
         place = jnp.bitwise_xor(y, low + (high - low) * source) * 2 + source
         columns = pl.ds(pl.multiple_of(place * depth, depth), depth)
         straight = block_ref[:depth, :]
@@ -204,13 +204,13 @@
     share = share.reshape(2, width, width) + jnp.stack([latest[:, :width], latest[:, width:]])
     modal = split(share.reshape(2 * width, width))
     sent = jnp.concatenate([block, modal], axis=0)
-    head = flipped(sent, EARLY[0])
-    tail = [flipped(sent, turn) for turn in LATE]
+    head = flipped(sent, EARLY[1][0])
+    tail = [flipped(sent, turn) for turn, other in LATE if not other]
     depth = block.shape[0]
-    (started,) = update(OWN, factor_slab, pending_rhs, [block, twin], "update_own")
+    (started,) = update(OWN, factor_slab, pending_rhs, [block], "update_own")
     started, head = lax.optimization_barrier((started, head))
     (started,) = update(
-        EARLY, factor_slab, started, [head, swapped(head[:depth])], "update_early"
+        EARLY, factor_slab, started, [twin, head, swapped(head[:depth])], "update_early"
     )
     started, tail = lax.optimization_barrier((started, tail))
     twins = [swapped(c[:depth]) for c in tail]

time: 66.9 us -> 65.1 us (0.973)
  waiting for transfers between devices: 17.8 us -> 15.1 us
  starting transfers between devices: 23.8 us -> 24.6 us
    ppermute x3, waiting for transfers between devices: 2.44 us -> 0.01 us  [flipped(): return lax.ppermute(value, ('y', 'core'), pairs)]
    ppermute x5, starting transfers between devices: 8.14 us -> 8.99 us  [swapped(): return lax.ppermute(value, 'core', SWAP)]
  transfers between devices with their start and end apart: 9 -> 9, of which waited for: 8 -> 5; matrix products, arithmetic and copies ran while one was open for 1% -> 1% of each run, Pallas kernels for 1% -> 1%
where the time goes in v12:
time: 65.1 us; the launch traced here: 64.8 us
  starting transfers between devices  24.6 us (38%)
  blocking collectives  16 us (25%)
  waiting for transfers between devices  15.1 us (23%)
  Pallas kernels  4.93 us (8%)
  local copies, waits for them, and re-layouts  2.26 us (3%)
  other arithmetic  0.86 us (1%)
  between operations  0.78 us (1%)
    all_to_all x1, blocking collectives, on_device(): gathered = lax.all_to_all(packed, COL, 0, 0, tiled=True)  16 us
    all_to_all x1, waiting for transfers between devices, on_device(): came = lax.all_to_all(outgoing, COL, 0, 0, tiled=True)  13.1 us
    all_to_all x1, starting transfers between devices, on_device(): came = lax.all_to_all(outgoing, COL, 0, 0, tiled=True)  11.9 us
    ppermute x5, starting transfers between devices, swapped(): return lax.ppermute(value, 'core', SWAP)  8.99 us
    ppermute x3, starting transfers between devices, flipped(): return lax.ppermute(value, ('y', 'core'), pairs)  3.77 us
    pallas_call x3, Pallas kernels, update(): pl.pallas_call(functools.partial(update_kernel, turns), out_shape=shapes,...  2.45 us
    pallas_call x1, Pallas kernels, first_partials(): pl.pallas_call(first_kernel, out_shape=jax.ShapeDtypeStruct((peers, 3 * o...  2.42 us
    unnamed x6, local copies, waits for them, and re-layouts  2.2 us
  transfers between devices with their start and end apart: 9, of which 5 were waited for; matrix products, arithmetic and copies ran while one was open for 1% of the time, Pallas kernels for 1%

profile of v12, /device:TPU:1, one launch (start us, length us, event | category | flops | bytes accessed | tf_op | source)
XLA Modules:
  0.0 64.8 jit_solution(8316745211200843263)
XLA Ops:
  0.6 0.0 copy-start.2
  0.6 2.4 %partials.1 = f32[32,24,128]{2,1,0:T(8,128)} custom-call(f32[2,64,256]{2,1,0:T(8,128)} %bitcast.26, f32[2,64,128]{2,1,0:T(8,128)} %rhs_hbm.1, bf16[256,128]{1,0:T(8,128)(2,1)} %modes_hbm.1, bf16[2,256,128]{2,1,0:T(8,128)(2,1)} %solved_hbm.1), custom_call_target="tpu_custom_call" | custom-call | tf_op jit(solution)/shard_map/partials/pallas_call | solution.py:81
  3.1 11.9 %all-to-all-start = ((f32[32,24,128]{2,1,0:T(8,128)}), f32[32,24,128]{2,1,0:T(8,128)S(1)}, u32[]{:S(2)}, u32[]{:S(2)}) async-start(f32[32,24,128]{2,1,0:T(8,128)} %partials.1), calls=%async_computation | async-start | bytes 786432 | tf_op jit(solution)/shard_map/all_to_all | solution.py:188
  15.0 0.7 %convert_element_type.39.modes_ref = f32[8,128]{1,0:T(8,128)S(1)} convert(bf16[8,128]{1,0:T(8,128)(2,1)} %param.13) | non-fusion elementwise | flops 1024 | bytes 6144 | tf_op jit(solution)/shard_map/convert_element_type | solution.py:189
  15.6 13.1 %all-to-all-done.came_ref = f32[32,24,128]{2,1,0:T(8,128)S(1)} async-done(((f32[32,24,128]{2,1,0:T(8,128)}), f32[32,24,128]{2,1,0:T(8,128)S(1)}, u32[]{:S(2)}, u32[]{:S(2)}) %all-to-all-start) | async-done | bytes 393248 | tf_op jit(solution)/shard_map/all_to_all | solution.py:188
  28.8 0.1 pack.1
  28.8 16.0 %all_to_all.10 = bf16[32,40,128]{2,1,0:T(8,128)(2,1)S(1)} all-to-all(bf16[32,40,128]{2,1,0:T(8,128)(2,1)S(1)} %get-tuple-element.13), channel_id=1, replica_groups=mesh['y'=4,'core'=2,'z'=8,'x'=4] {'z','x'}, dimensions={0} | all-to-all | bytes 655360 | tf_op jit(solution)/shard_map/all_to_all | solution.py:190
  44.9 0.2 fusion.1
  45.2 3.0 %collective-permute-start = (bf16[512,256]{1,0:T(8,128)(2,1)S(1)}, bf16[512,256]{1,0:T(8,128)(2,1)S(1)}, u32[]{:S(2)}, u32[]{:S(2)}) collective-permute-start(bf16[512,256]{1,0:T(8,128)(2,1)S(1)} %maximum_maximum_fusion), channel_id=1, source_target_pairs={{0,128},{32,160},{64,192},{96,224},{128,0},{160,32},{192,64},{224,... | collective-permute-start | bytes 786440 | tf_op jit(solution)/shard_map/ppermute | solution.py:26
  48.2 0.4 collective-permute-start.4
  48.6 0.4 collective-permute-start.3
  49.0 4.7 %collective-permute-start.1 = (bf16[256,256]{1,0:T(8,128)(2,1)S(1)}, bf16[256,256]{1,0:T(8,128)(2,1)S(1)}, u32[]{:S(2)}, u32[]{:S(2)}) collective-permute-start(bf16[256,256]{1,0:T(8,128)(2,1)S(1)} %pad_maximum_fusion.rest_0_), channel_id=1, source_target_pairs={{0,32},{32,0},{1,33},{33,1},{2,34},{34,2},{3,35},{35,3},{4,36},{36... | collective-permute-start | bytes 393224 | tf_op jit(solution)/shard_map/ppermute | solution.py:21
  53.6 0.0 copy-done.2
  53.6 0.0 copy-start
  53.6 2.2 %copy-done = bf16[2,512,2048]{2,1,0:T(8,128)(2,1)S(1)} copy-done((bf16[2,512,2048]{2,1,0:T(8,128)(2,1)S(1)}, bf16[2,512,2048]{2,1,0:T(8,128)(2,1)}, u32[]{:S(2)}) %copy-start) | copy-done | bytes 4194328
  55.8 0.3 update_own.1.rhs_ref
  56.1 0.0 copy-start.1
  56.2 0.0 collective-permute-done.rest_1_
  56.2 2.3 %collective-permute-start.2 = (bf16[256,256]{1,0:T(8,128)(2,1)S(1)}, bf16[256,256]{1,0:T(8,128)(2,1)S(1)}, u32[]{:S(2)}, u32[]{:S(2)}) collective-permute-start(bf16[256,256]{1,0:T(8,128)(2,1)S(1)} %slice.64), channel_id=1, source_target_pairs={{0,32},{32,0},{1,33},{33,1},{2,34},{34,2},{3,35},{35,3},{4,36},{36... | collective-permute-start | bytes 393224 | tf_op jit(solution)/shard_map/ppermute | solution.py:21
  58.5 0.0 collective-permute-done.1.rest_0_
  58.5 1.0 %collective-permute-done.2.rest_2_ = bf16[256,256]{1,0:T(8,128)(2,1)S(1)} collective-permute-done((bf16[256,256]{1,0:T(8,128)(2,1)S(1)}, bf16[256,256]{1,0:T(8,128)(2,1)S(1)}, u32[]{:S(2)}, u32[]{:S(2)}) %collective-permute-start.2) | collective-permute-done | bytes 131104 | tf_op jit(solution)/shard_map/ppermute | solution.py:21
  59.5 0.6 update_early.1.rhs_ref
  60.1 0.0 collective-permute-done.4.rest_2_
  60.1 0.0 collective-permute-done.3.rest_0_
  60.2 0.1 add_add_fusion.rest_4_
  60.3 1.5 %collective-permute-start.6 = (bf16[256,256]{1,0:T(8,128)(2,1)S(1)}, bf16[256,256]{1,0:T(8,128)(2,1)S(1)}, u32[]{:S(2)}, u32[]{:S(2)}) collective-permute-start(bf16[256,256]{1,0:T(8,128)(2,1)S(1)} %slice.66), channel_id=1, source_target_pairs={{0,32},{32,0},{1,33},{33,1},{2,34},{34,2},{3,35},{35,3},{4,36},{36... | collective-permute-start | bytes 393224 | tf_op jit(solution)/shard_map/ppermute | solution.py:21
  61.7 0.1 collective-permute-start.5
  61.8 0.4 collective-permute-start.7
  62.3 0.5 collective-permute-done.6.rest_3_
  62.7 0.4 collective-permute-done.5.rest_1_
  63.1 0.2 collective-permute-done.7.rest_5_
  63.3 0.0 copy-done.1
  63.3 1.5 %update_late.1 = (f32[2,512,128]{2,1,0:T(8,128)}, f32[256,128]{1,0:T(8,128)}, f32[16,128]{1,0:T(8,128)}) custom-call(bf16[2,512,2048]{2,1,0:T(8,128)(2,1)S(1)} %copy-done.1, f32[2,512,128]{2,1,0:T(8,128)S(1)} %update_early.1.rhs_ref, bf16[512,256]{1,0:T(8,128)(2,1)S(1)} %collective-permute-done.3.rest_0_, ...), custom_call_target="tpu_custom_call" | custom-call | flops 536870912 | bytes 2097152 | tf_op jit(solution)/shard_map/update_late/pallas_call | solution.py:166
  (9 shorter events, 0.2 us)
Async XLA Ops:
  0.6 53.0 %copy-start.2 = (f32[2,512,128]{2,1,0:T(8,128)S(1)}, f32[2,512,128]{2,1,0:T(8,128)}, u32[]{:S(2)}) copy-start(f32[2,512,128]{2,1,0:T(8,128)} %rhs_ref.1) | copy-start | bytes 1572868
  3.1 25.7 %all-to-all-start = ((f32[32,24,128]{2,1,0:T(8,128)}), f32[32,24,128]{2,1,0:T(8,128)S(1)}, u32[]{:S(2)}, u32[]{:S(2)}) async-start(f32[32,24,128]{2,1,0:T(8,128)} %partials.1), calls=%async_computation | async-start | bytes 786432 | tf_op jit(solution)/shard_map/all_to_all | solution.py:188
  45.2 11.0 %collective-permute-start = (bf16[512,256]{1,0:T(8,128)(2,1)S(1)}, bf16[512,256]{1,0:T(8,128)(2,1)S(1)}, u32[]{:S(2)}, u32[]{:S(2)}) collective-permute-start(bf16[512,256]{1,0:T(8,128)(2,1)S(1)} %maximum_maximum_fusion), channel_id=1, source_target_pairs={{0,128},{32,160},{64,192},{96,224},{128,0},{160,32},{192,64},{224,... | collective-permute-start | bytes 786440 | tf_op jit(solution)/shard_map/ppermute | solution.py:26
  48.2 11.9 %collective-permute-start.4 = (bf16[512,256]{1,0:T(8,128)(2,1)S(1)}, bf16[512,256]{1,0:T(8,128)(2,1)S(1)}, u32[]{:S(2)}, u32[]{:S(2)}) collective-permute-start(bf16[512,256]{1,0:T(8,128)(2,1)S(1)} %maximum_maximum_fusion), channel_id=1, source_target_pairs={{0,192},{32,96},{64,128},{96,32},{128,64},{160,224},{192,0},{224,1... | collective-permute-start | bytes 786440 | tf_op jit(solution)/shard_map/ppermute | solution.py:26
  48.6 11.5 %collective-permute-start.3 = (bf16[512,256]{1,0:T(8,128)(2,1)S(1)}, bf16[512,256]{1,0:T(8,128)(2,1)S(1)}, u32[]{:S(2)}, u32[]{:S(2)}) collective-permute-start(bf16[512,256]{1,0:T(8,128)(2,1)S(1)} %maximum_maximum_fusion), channel_id=1, source_target_pairs={{0,64},{32,224},{64,0},{96,160},{128,192},{160,96},{192,128},{224,... | collective-permute-start | bytes 786440 | tf_op jit(solution)/shard_map/ppermute | solution.py:26
  49.0 9.5 %collective-permute-start.1 = (bf16[256,256]{1,0:T(8,128)(2,1)S(1)}, bf16[256,256]{1,0:T(8,128)(2,1)S(1)}, u32[]{:S(2)}, u32[]{:S(2)}) collective-permute-start(bf16[256,256]{1,0:T(8,128)(2,1)S(1)} %pad_maximum_fusion.rest_0_), channel_id=1, source_target_pairs={{0,32},{32,0},{1,33},{33,1},{2,34},{34,2},{3,35},{35,3},{4,36},{36... | collective-permute-start | bytes 393224 | tf_op jit(solution)/shard_map/ppermute | solution.py:21
  53.6 2.2 %copy-start = (bf16[2,512,2048]{2,1,0:T(8,128)(2,1)S(1)}, bf16[2,512,2048]{2,1,0:T(8,128)(2,1)}, u32[]{:S(2)}) copy-start(bf16[2,512,2048]{2,1,0:T(8,128)(2,1)} %factor_ref.5) | copy-start | bytes 12582916
  56.1 7.1 %copy-start.1 = (bf16[2,512,2048]{2,1,0:T(8,128)(2,1)S(1)}, bf16[2,512,2048]{2,1,0:T(8,128)(2,1)}, u32[]{:S(2)}) copy-start(bf16[2,512,2048]{2,1,0:T(8,128)(2,1)} %factor_ref.5) | copy-start | bytes 12582916
  56.2 3.3 %collective-permute-start.2 = (bf16[256,256]{1,0:T(8,128)(2,1)S(1)}, bf16[256,256]{1,0:T(8,128)(2,1)S(1)}, u32[]{:S(2)}, u32[]{:S(2)}) collective-permute-start(bf16[256,256]{1,0:T(8,128)(2,1)S(1)} %slice.64), channel_id=1, source_target_pairs={{0,32},{32,0},{1,33},{33,1},{2,34},{34,2},{3,35},{35,3},{4,36},{36... | collective-permute-start | bytes 393224 | tf_op jit(solution)/shard_map/ppermute | solution.py:21
  60.3 2.5 %collective-permute-start.6 = (bf16[256,256]{1,0:T(8,128)(2,1)S(1)}, bf16[256,256]{1,0:T(8,128)(2,1)S(1)}, u32[]{:S(2)}, u32[]{:S(2)}) collective-permute-start(bf16[256,256]{1,0:T(8,128)(2,1)S(1)} %slice.66), channel_id=1, source_target_pairs={{0,32},{32,0},{1,33},{33,1},{2,34},{34,2},{3,35},{35,3},{4,36},{36... | collective-permute-start | bytes 393224 | tf_op jit(solution)/shard_map/ppermute | solution.py:21
  61.7 1.3 %collective-permute-start.5 = (bf16[256,256]{1,0:T(8,128)(2,1)S(1)}, bf16[256,256]{1,0:T(8,128)(2,1)S(1)}, u32[]{:S(2)}, u32[]{:S(2)}) collective-permute-start(bf16[256,256]{1,0:T(8,128)(2,1)S(1)} %slice.65), channel_id=1, source_target_pairs={{0,32},{32,0},{1,33},{33,1},{2,34},{34,2},{3,35},{35,3},{4,36},{36... | collective-permute-start | bytes 393224 | tf_op jit(solution)/shard_map/ppermute | solution.py:21
  61.8 1.4 %collective-permute-start.7 = (f32[256,128]{1,0:T(8,128)S(1)}, f32[256,128]{1,0:T(8,128)S(1)}, u32[]{:S(2)}, u32[]{:S(2)}) collective-permute-start(f32[256,128]{1,0:T(8,128)S(1)} %add_add_fusion.rest_4_), channel_id=1, source_target_pairs={{0,32},{32,0},{1,33},{33,1},{2,34},{34,2},{3,35},{35,3},{4,36},{36... | collective-permute-start | bytes 393224 | tf_op jit(solution)/shard_map/ppermute | solution.py:21

commit v13 on v12

--- a/solution.py
+++ b/solution.py
@@ -13,8 +13,8 @@
 SWAP = [(0, 1), (1, 0)]
 CHUNK = 128
 OWN = (((0, 0), 0),)
-EARLY = (((0, 0), 1), ((2, 2), 0), ((2, 2), 1))
-LATE = (((1, 3), 0), ((1, 3), 1), ((3, 1), 0), ((3, 1), 1))
+EARLY = (((0, 0), 1), ((1, 3), 0), ((1, 3), 1))
+LATE = (((3, 1), 0), ((3, 1), 1), ((2, 2), 0), ((2, 2), 1))
 
 
 def swapped(value):
@@ -214,7 +214,7 @@
     )
     started, tail = lax.optimization_barrier((started, tail))
     twins = [swapped(c[:depth]) for c in tail]
-    first, third, second = (joined(c[depth:]) for c in (*tail, head))
+    first, third, second = (joined(c[depth:]) for c in (head, *tail))
     modal = (joined(modal) + second) + (first + third)
     updated_rhs, modal_forces, panel_solution = update(
         LATE,

time: 65.1 us -> 67.7 us (1.040)
  starting transfers between devices: 24.6 us -> 27.2 us
    ppermute x5, starting transfers between devices: 8.99 us -> 11.9 us  [swapped(): return lax.ppermute(value, 'core', SWAP)]
where the time goes in v13:
time: 67.7 us; the launch traced here: 67.4 us
  starting transfers between devices  27.2 us (40%)
  blocking collectives  16 us (24%)
  waiting for transfers between devices  15.1 us (22%)
  Pallas kernels  4.93 us (7%)
  local copies, waits for them, and re-layouts  2.26 us (3%)
  other arithmetic  0.86 us (1%)
  between operations  0.78 us (1%)
    all_to_all x1, blocking collectives, on_device(): gathered = lax.all_to_all(packed, COL, 0, 0, tiled=True)  16 us
    all_to_all x1, waiting for transfers between devices, on_device(): came = lax.all_to_all(outgoing, COL, 0, 0, tiled=True)  13.1 us
    all_to_all x1, starting transfers between devices, on_device(): came = lax.all_to_all(outgoing, COL, 0, 0, tiled=True)  11.9 us
    ppermute x5, starting transfers between devices, swapped(): return lax.ppermute(value, 'core', SWAP)  11.9 us
    ppermute x3, starting transfers between devices, flipped(): return lax.ppermute(value, ('y', 'core'), pairs)  3.49 us
    pallas_call x3, Pallas kernels, update(): pl.pallas_call(functools.partial(update_kernel, turns), out_shape=shapes,...  2.46 us
    pallas_call x1, Pallas kernels, first_partials(): pl.pallas_call(first_kernel, out_shape=jax.ShapeDtypeStruct((peers, 3 * o...  2.42 us
    unnamed x6, local copies, waits for them, and re-layouts  2.2 us
  transfers between devices with their start and end apart: 9, of which 5 were waited for; matrix products, arithmetic and copies ran while one was open for 1% of the time, Pallas kernels for 1%

profile of v13, /device:TPU:1, one launch (start us, length us, event | category | flops | bytes accessed | tf_op | source)
XLA Modules:
  0.0 67.4 jit_solution(7709400937702926404)
XLA Ops:
  0.6 0.0 copy-start.2
  0.6 2.4 %partials.1 = f32[32,24,128]{2,1,0:T(8,128)} custom-call(f32[2,64,256]{2,1,0:T(8,128)} %bitcast.26, f32[2,64,128]{2,1,0:T(8,128)} %rhs_hbm.1, bf16[256,128]{1,0:T(8,128)(2,1)} %modes_hbm.1, bf16[2,256,128]{2,1,0:T(8,128)(2,1)} %solved_hbm.1), custom_call_target="tpu_custom_call" | custom-call | tf_op jit(solution)/shard_map/partials/pallas_call | solution.py:81
  3.1 11.9 %all-to-all-start = ((f32[32,24,128]{2,1,0:T(8,128)}), f32[32,24,128]{2,1,0:T(8,128)S(1)}, u32[]{:S(2)}, u32[]{:S(2)}) async-start(f32[32,24,128]{2,1,0:T(8,128)} %partials.1), calls=%async_computation | async-start | bytes 786432 | tf_op jit(solution)/shard_map/all_to_all | solution.py:188
  15.0 0.7 %convert_element_type.39.modes_ref = f32[8,128]{1,0:T(8,128)S(1)} convert(bf16[8,128]{1,0:T(8,128)(2,1)} %param.13) | non-fusion elementwise | flops 1024 | bytes 6144 | tf_op jit(solution)/shard_map/convert_element_type | solution.py:189
  15.6 13.1 %all-to-all-done.came_ref = f32[32,24,128]{2,1,0:T(8,128)S(1)} async-done(((f32[32,24,128]{2,1,0:T(8,128)}), f32[32,24,128]{2,1,0:T(8,128)S(1)}, u32[]{:S(2)}, u32[]{:S(2)}) %all-to-all-start) | async-done | bytes 393248 | tf_op jit(solution)/shard_map/all_to_all | solution.py:188
  28.8 0.1 pack.1
  28.8 16.0 %all_to_all.10 = bf16[32,40,128]{2,1,0:T(8,128)(2,1)S(1)} all-to-all(bf16[32,40,128]{2,1,0:T(8,128)(2,1)S(1)} %get-tuple-element.13), channel_id=1, replica_groups=mesh['y'=4,'core'=2,'z'=8,'x'=4] {'z','x'}, dimensions={0} | all-to-all | bytes 655360 | tf_op jit(solution)/shard_map/all_to_all | solution.py:190
  44.9 0.2 fusion.1
  45.2 2.8 %collective-permute-start = (bf16[512,256]{1,0:T(8,128)(2,1)S(1)}, bf16[512,256]{1,0:T(8,128)(2,1)S(1)}, u32[]{:S(2)}, u32[]{:S(2)}) collective-permute-start(bf16[512,256]{1,0:T(8,128)(2,1)S(1)} %maximum_maximum_fusion), channel_id=1, source_target_pairs={{0,64},{32,224},{64,0},{96,160},{128,192},{160,96},{192,128},{224,... | collective-permute-start | bytes 786440 | tf_op jit(solution)/shard_map/ppermute | solution.py:26
  48.0 0.3 collective-permute-start.4
  48.4 0.3 collective-permute-start.3
  48.7 5.4 %collective-permute-start.1 = (bf16[256,256]{1,0:T(8,128)(2,1)S(1)}, bf16[256,256]{1,0:T(8,128)(2,1)S(1)}, u32[]{:S(2)}, u32[]{:S(2)}) collective-permute-start(bf16[256,256]{1,0:T(8,128)(2,1)S(1)} %pad_maximum_fusion.rest_0_), channel_id=1, source_target_pairs={{0,32},{32,0},{1,33},{33,1},{2,34},{34,2},{3,35},{35,3},{4,36},{36... | collective-permute-start | bytes 393224 | tf_op jit(solution)/shard_map/ppermute | solution.py:21
  54.1 0.0 copy-done.2
  54.1 0.0 copy-start
  54.1 2.2 %copy-done = bf16[2,512,2048]{2,1,0:T(8,128)(2,1)S(1)} copy-done((bf16[2,512,2048]{2,1,0:T(8,128)(2,1)S(1)}, bf16[2,512,2048]{2,1,0:T(8,128)(2,1)}, u32[]{:S(2)}) %copy-start) | copy-done | bytes 4194328
  56.3 0.3 update_own.1.rhs_ref
  56.6 0.0 copy-start.1
  56.6 0.0 collective-permute-done.rest_1_
  56.6 2.0 %collective-permute-start.2 = (bf16[256,256]{1,0:T(8,128)(2,1)S(1)}, bf16[256,256]{1,0:T(8,128)(2,1)S(1)}, u32[]{:S(2)}, u32[]{:S(2)}) collective-permute-start(bf16[256,256]{1,0:T(8,128)(2,1)S(1)} %slice.64), channel_id=1, source_target_pairs={{0,32},{32,0},{1,33},{33,1},{2,34},{34,2},{3,35},{35,3},{4,36},{36... | collective-permute-start | bytes 393224 | tf_op jit(solution)/shard_map/ppermute | solution.py:21
  58.6 0.0 collective-permute-done.1.rest_0_
  58.6 1.0 %collective-permute-done.2.rest_2_ = bf16[256,256]{1,0:T(8,128)(2,1)S(1)} collective-permute-done((bf16[256,256]{1,0:T(8,128)(2,1)S(1)}, bf16[256,256]{1,0:T(8,128)(2,1)S(1)}, u32[]{:S(2)}, u32[]{:S(2)}) %collective-permute-start.2) | collective-permute-done | bytes 131104 | tf_op jit(solution)/shard_map/ppermute | solution.py:21
  59.6 0.6 update_early.1.rhs_ref
  60.2 0.0 collective-permute-done.4.rest_2_
  60.3 0.0 collective-permute-done.3.rest_0_
  60.3 0.1 add_add_fusion.rest_4_
  60.4 4.0 %collective-permute-start.6 = (bf16[256,256]{1,0:T(8,128)(2,1)S(1)}, bf16[256,256]{1,0:T(8,128)(2,1)S(1)}, u32[]{:S(2)}, u32[]{:S(2)}) collective-permute-start(bf16[256,256]{1,0:T(8,128)(2,1)S(1)} %slice.66), channel_id=1, source_target_pairs={{0,32},{32,0},{1,33},{33,1},{2,34},{34,2},{3,35},{35,3},{4,36},{36... | collective-permute-start | bytes 393224 | tf_op jit(solution)/shard_map/ppermute | solution.py:21
  64.3 0.1 collective-permute-start.5
  64.5 0.4 collective-permute-start.7
  64.9 0.5 collective-permute-done.6.rest_3_
  65.3 0.4 collective-permute-done.5.rest_1_
  65.7 0.2 collective-permute-done.7.rest_5_
  65.9 0.0 copy-done.1
  65.9 1.5 %update_late.1 = (f32[2,512,128]{2,1,0:T(8,128)}, f32[256,128]{1,0:T(8,128)}, f32[16,128]{1,0:T(8,128)}) custom-call(bf16[2,512,2048]{2,1,0:T(8,128)(2,1)S(1)} %copy-done.1, f32[2,512,128]{2,1,0:T(8,128)S(1)} %update_early.1.rhs_ref, bf16[512,256]{1,0:T(8,128)(2,1)S(1)} %collective-permute-done.3.rest_0_, ...), custom_call_target="tpu_custom_call" | custom-call | flops 536870912 | bytes 2097152 | tf_op jit(solution)/shard_map/update_late/pallas_call | solution.py:166
  (9 shorter events, 0.2 us)
Async XLA Ops:
  0.6 53.5 %copy-start.2 = (f32[2,512,128]{2,1,0:T(8,128)S(1)}, f32[2,512,128]{2,1,0:T(8,128)}, u32[]{:S(2)}) copy-start(f32[2,512,128]{2,1,0:T(8,128)} %rhs_ref.1) | copy-start | bytes 1572868
  3.1 25.7 %all-to-all-start = ((f32[32,24,128]{2,1,0:T(8,128)}), f32[32,24,128]{2,1,0:T(8,128)S(1)}, u32[]{:S(2)}, u32[]{:S(2)}) async-start(f32[32,24,128]{2,1,0:T(8,128)} %partials.1), calls=%async_computation | async-start | bytes 786432 | tf_op jit(solution)/shard_map/all_to_all | solution.py:188
  45.2 11.4 %collective-permute-start = (bf16[512,256]{1,0:T(8,128)(2,1)S(1)}, bf16[512,256]{1,0:T(8,128)(2,1)S(1)}, u32[]{:S(2)}, u32[]{:S(2)}) collective-permute-start(bf16[512,256]{1,0:T(8,128)(2,1)S(1)} %maximum_maximum_fusion), channel_id=1, source_target_pairs={{0,64},{32,224},{64,0},{96,160},{128,192},{160,96},{192,128},{224,... | collective-permute-start | bytes 786440 | tf_op jit(solution)/shard_map/ppermute | solution.py:26
  48.0 12.2 %collective-permute-start.4 = (bf16[512,256]{1,0:T(8,128)(2,1)S(1)}, bf16[512,256]{1,0:T(8,128)(2,1)S(1)}, u32[]{:S(2)}, u32[]{:S(2)}) collective-permute-start(bf16[512,256]{1,0:T(8,128)(2,1)S(1)} %maximum_maximum_fusion), channel_id=1, source_target_pairs={{0,128},{32,160},{64,192},{96,224},{128,0},{160,32},{192,64},{224,... | collective-permute-start | bytes 786440 | tf_op jit(solution)/shard_map/ppermute | solution.py:26
  48.4 11.9 %collective-permute-start.3 = (bf16[512,256]{1,0:T(8,128)(2,1)S(1)}, bf16[512,256]{1,0:T(8,128)(2,1)S(1)}, u32[]{:S(2)}, u32[]{:S(2)}) collective-permute-start(bf16[512,256]{1,0:T(8,128)(2,1)S(1)} %maximum_maximum_fusion), channel_id=1, source_target_pairs={{0,192},{32,96},{64,128},{96,32},{128,64},{160,224},{192,0},{224,1... | collective-permute-start | bytes 786440 | tf_op jit(solution)/shard_map/ppermute | solution.py:26
  48.7 9.9 %collective-permute-start.1 = (bf16[256,256]{1,0:T(8,128)(2,1)S(1)}, bf16[256,256]{1,0:T(8,128)(2,1)S(1)}, u32[]{:S(2)}, u32[]{:S(2)}) collective-permute-start(bf16[256,256]{1,0:T(8,128)(2,1)S(1)} %pad_maximum_fusion.rest_0_), channel_id=1, source_target_pairs={{0,32},{32,0},{1,33},{33,1},{2,34},{34,2},{3,35},{35,3},{4,36},{36... | collective-permute-start | bytes 393224 | tf_op jit(solution)/shard_map/ppermute | solution.py:21
  54.1 2.2 %copy-start = (bf16[2,512,2048]{2,1,0:T(8,128)(2,1)S(1)}, bf16[2,512,2048]{2,1,0:T(8,128)(2,1)}, u32[]{:S(2)}) copy-start(bf16[2,512,2048]{2,1,0:T(8,128)(2,1)} %factor_ref.5) | copy-start | bytes 12582916
  56.6 9.3 %copy-start.1 = (bf16[2,512,2048]{2,1,0:T(8,128)(2,1)S(1)}, bf16[2,512,2048]{2,1,0:T(8,128)(2,1)}, u32[]{:S(2)}) copy-start(bf16[2,512,2048]{2,1,0:T(8,128)(2,1)} %factor_ref.5) | copy-start | bytes 12582916
  56.6 3.0 %collective-permute-start.2 = (bf16[256,256]{1,0:T(8,128)(2,1)S(1)}, bf16[256,256]{1,0:T(8,128)(2,1)S(1)}, u32[]{:S(2)}, u32[]{:S(2)}) collective-permute-start(bf16[256,256]{1,0:T(8,128)(2,1)S(1)} %slice.64), channel_id=1, source_target_pairs={{0,32},{32,0},{1,33},{33,1},{2,34},{34,2},{3,35},{35,3},{4,36},{36... | collective-permute-start | bytes 393224 | tf_op jit(solution)/shard_map/ppermute | solution.py:21
  60.4 5.0 %collective-permute-start.6 = (bf16[256,256]{1,0:T(8,128)(2,1)S(1)}, bf16[256,256]{1,0:T(8,128)(2,1)S(1)}, u32[]{:S(2)}, u32[]{:S(2)}) collective-permute-start(bf16[256,256]{1,0:T(8,128)(2,1)S(1)} %slice.66), channel_id=1, source_target_pairs={{0,32},{32,0},{1,33},{33,1},{2,34},{34,2},{3,35},{35,3},{4,36},{36... | collective-permute-start | bytes 393224 | tf_op jit(solution)/shard_map/ppermute | solution.py:21
  64.3 1.3 %collective-permute-start.5 = (bf16[256,256]{1,0:T(8,128)(2,1)S(1)}, bf16[256,256]{1,0:T(8,128)(2,1)S(1)}, u32[]{:S(2)}, u32[]{:S(2)}) collective-permute-start(bf16[256,256]{1,0:T(8,128)(2,1)S(1)} %slice.65), channel_id=1, source_target_pairs={{0,32},{32,0},{1,33},{33,1},{2,34},{34,2},{3,35},{35,3},{4,36},{36... | collective-permute-start | bytes 393224 | tf_op jit(solution)/shard_map/ppermute | solution.py:21
  64.5 1.4 %collective-permute-start.7 = (f32[256,128]{1,0:T(8,128)S(1)}, f32[256,128]{1,0:T(8,128)S(1)}, u32[]{:S(2)}, u32[]{:S(2)}) collective-permute-start(f32[256,128]{1,0:T(8,128)S(1)} %add_add_fusion.rest_4_), channel_id=1, source_target_pairs={{0,32},{32,0},{1,33},{33,1},{2,34},{34,2},{3,35},{35,3},{4,36},{36... | collective-permute-start | bytes 393224 | tf_op jit(solution)/shard_map/ppermute | solution.py:21

commit v14 on v12

--- a/solution.py
+++ b/solution.py
@@ -43,10 +43,10 @@
         pltpu.make_async_copy(source, target, sems.at[i])
         for i, (source, target) in enumerate(
             (
+                (diag_hbm, diag_ref),
+                (rhs_hbm, rhs_ref),
                 (modes_hbm, modes_ref),
                 (solved_hbm, solved_ref),
-                (rhs_hbm, rhs_ref),
-                (diag_hbm, diag_ref),
             )
         )
     ]
@@ -56,23 +56,23 @@
     half = peers // 2
     moves[0].wait()
     moves[1].wait()
+    left = jnp.concatenate([diag_ref[0], diag_ref[1]], axis=0)
+    real, imag = rhs_ref[0], rhs_ref[1]
+    right = jnp.concatenate(
+        [jnp.concatenate([real, imag], axis=1), jnp.concatenate([-imag, real], axis=1)], axis=0
+    )
+    partial = lax.dot_general(
+        left, right, over_first, precision=lax.Precision.HIGHEST, preferred_element_type=F32
+    )
+    out_ref[:, :own, :] = partial[:, :width].reshape(peers, own, width)
+    out_ref[:, own : 2 * own, :] = partial[:, width:].reshape(peers, own, width)
+    moves[2].wait()
+    moves[3].wait()
     for c in range(2):
         earlier = lax.dot_general(
             modes_ref[...], solved_ref[c], over_first, preferred_element_type=F32
         )
         out_ref[c * half : (c + 1) * half, 2 * own :, :] = earlier.reshape(half, own, width)
-    moves[2].wait()
-    moves[3].wait()
-    left = jnp.concatenate([diag_ref[0], diag_ref[1]], axis=0)
-    real, imag = rhs_ref[0], rhs_ref[1]
-    right = jnp.concatenate(
-        [jnp.concatenate([real, imag], axis=1), jnp.concatenate([-imag, real], axis=1)], axis=0
-    )
-    partial = lax.dot_general(
-        left, right, over_first, precision=lax.Precision.HIGHEST, preferred_element_type=F32
-    )
-    out_ref[:, :own, :] = partial[:, :width].reshape(peers, own, width)
-    out_ref[:, own : 2 * own, :] = partial[:, width:].reshape(peers, own, width)
 
 
 def first_partials(diag_inverse, panel_rhs, modes_prev, solved_prev, peers, own):

time: 65.1 us -> 65.1 us (level)
  no operation moved by 1% of the time
where the time goes in v14:
time: 65.1 us; the launch traced here: 64.8 us
  starting transfers between devices  24.6 us (38%)
  blocking collectives  16 us (25%)
  waiting for transfers between devices  15.1 us (23%)
  Pallas kernels  4.94 us (8%)
  local copies, waits for them, and re-layouts  2.26 us (3%)
  other arithmetic  0.86 us (1%)
  between operations  0.78 us (1%)
    all_to_all x1, blocking collectives, on_device(): gathered = lax.all_to_all(packed, COL, 0, 0, tiled=True)  16 us
    all_to_all x1, waiting for transfers between devices, on_device(): came = lax.all_to_all(outgoing, COL, 0, 0, tiled=True)  13.1 us
    all_to_all x1, starting transfers between devices, on_device(): came = lax.all_to_all(outgoing, COL, 0, 0, tiled=True)  11.9 us
    ppermute x5, starting transfers between devices, swapped(): return lax.ppermute(value, 'core', SWAP)  8.98 us
    ppermute x3, starting transfers between devices, flipped(): return lax.ppermute(value, ('y', 'core'), pairs)  3.78 us
    pallas_call x3, Pallas kernels, update(): pl.pallas_call(functools.partial(update_kernel, turns), out_shape=shapes,...  2.46 us
    pallas_call x1, Pallas kernels, first_partials(): pl.pallas_call(first_kernel, out_shape=jax.ShapeDtypeStruct((peers, 3 * o...  2.42 us
    unnamed x6, local copies, waits for them, and re-layouts  2.2 us
  transfers between devices with their start and end apart: 9, of which 5 were waited for; matrix products, arithmetic and copies ran while one was open for 1% of the time, Pallas kernels for 1%

profile of v14, /device:TPU:1, one launch (start us, length us, event | category | flops | bytes accessed | tf_op | source)
XLA Modules:
  0.0 64.8 jit_solution(3415907208716831542)
XLA Ops:
  0.6 0.0 copy-start.2
  0.6 2.4 %partials.1 = f32[32,24,128]{2,1,0:T(8,128)} custom-call(f32[2,64,256]{2,1,0:T(8,128)} %bitcast.26, f32[2,64,128]{2,1,0:T(8,128)} %rhs_hbm.1, bf16[256,128]{1,0:T(8,128)(2,1)} %modes_hbm.1, bf16[2,256,128]{2,1,0:T(8,128)(2,1)} %solved_hbm.1), custom_call_target="tpu_custom_call" | custom-call | tf_op jit(solution)/shard_map/partials/pallas_call | solution.py:81
  3.1 11.9 %all-to-all-start = ((f32[32,24,128]{2,1,0:T(8,128)}), f32[32,24,128]{2,1,0:T(8,128)S(1)}, u32[]{:S(2)}, u32[]{:S(2)}) async-start(f32[32,24,128]{2,1,0:T(8,128)} %partials.1), calls=%async_computation | async-start | bytes 786432 | tf_op jit(solution)/shard_map/all_to_all | solution.py:188
  15.0 0.7 %convert_element_type.39.modes_ref = f32[8,128]{1,0:T(8,128)S(1)} convert(bf16[8,128]{1,0:T(8,128)(2,1)} %param.13) | non-fusion elementwise | flops 1024 | bytes 6144 | tf_op jit(solution)/shard_map/convert_element_type | solution.py:189
  15.6 13.1 %all-to-all-done.came_ref = f32[32,24,128]{2,1,0:T(8,128)S(1)} async-done(((f32[32,24,128]{2,1,0:T(8,128)}), f32[32,24,128]{2,1,0:T(8,128)S(1)}, u32[]{:S(2)}, u32[]{:S(2)}) %all-to-all-start) | async-done | bytes 393248 | tf_op jit(solution)/shard_map/all_to_all | solution.py:188
  28.8 0.1 pack.1
  28.8 16.0 %all_to_all.10 = bf16[32,40,128]{2,1,0:T(8,128)(2,1)S(1)} all-to-all(bf16[32,40,128]{2,1,0:T(8,128)(2,1)S(1)} %get-tuple-element.13), channel_id=1, replica_groups=mesh['y'=4,'core'=2,'z'=8,'x'=4] {'z','x'}, dimensions={0} | all-to-all | bytes 655360 | tf_op jit(solution)/shard_map/all_to_all | solution.py:190
  44.9 0.2 fusion.1
  45.2 3.0 %collective-permute-start = (bf16[512,256]{1,0:T(8,128)(2,1)S(1)}, bf16[512,256]{1,0:T(8,128)(2,1)S(1)}, u32[]{:S(2)}, u32[]{:S(2)}) collective-permute-start(bf16[512,256]{1,0:T(8,128)(2,1)S(1)} %maximum_maximum_fusion), channel_id=1, source_target_pairs={{0,128},{32,160},{64,192},{96,224},{128,0},{160,32},{192,64},{224,... | collective-permute-start | bytes 786440 | tf_op jit(solution)/shard_map/ppermute | solution.py:26
  48.2 0.4 collective-permute-start.4
  48.6 0.4 collective-permute-start.3
  49.0 4.7 %collective-permute-start.1 = (bf16[256,256]{1,0:T(8,128)(2,1)S(1)}, bf16[256,256]{1,0:T(8,128)(2,1)S(1)}, u32[]{:S(2)}, u32[]{:S(2)}) collective-permute-start(bf16[256,256]{1,0:T(8,128)(2,1)S(1)} %pad_maximum_fusion.rest_0_), channel_id=1, source_target_pairs={{0,32},{32,0},{1,33},{33,1},{2,34},{34,2},{3,35},{35,3},{4,36},{36... | collective-permute-start | bytes 393224 | tf_op jit(solution)/shard_map/ppermute | solution.py:21
  53.7 0.0 copy-done.2
  53.7 0.0 copy-start
  53.7 2.2 %copy-done = bf16[2,512,2048]{2,1,0:T(8,128)(2,1)S(1)} copy-done((bf16[2,512,2048]{2,1,0:T(8,128)(2,1)S(1)}, bf16[2,512,2048]{2,1,0:T(8,128)(2,1)}, u32[]{:S(2)}) %copy-start) | copy-done | bytes 4194328
  55.8 0.3 update_own.1.rhs_ref
  56.2 0.0 copy-start.1
  56.2 0.0 collective-permute-done.rest_1_
  56.2 2.3 %collective-permute-start.2 = (bf16[256,256]{1,0:T(8,128)(2,1)S(1)}, bf16[256,256]{1,0:T(8,128)(2,1)S(1)}, u32[]{:S(2)}, u32[]{:S(2)}) collective-permute-start(bf16[256,256]{1,0:T(8,128)(2,1)S(1)} %slice.64), channel_id=1, source_target_pairs={{0,32},{32,0},{1,33},{33,1},{2,34},{34,2},{3,35},{35,3},{4,36},{36... | collective-permute-start | bytes 393224 | tf_op jit(solution)/shard_map/ppermute | solution.py:21
  58.5 0.0 collective-permute-done.1.rest_0_
  58.5 1.0 %collective-permute-done.2.rest_2_ = bf16[256,256]{1,0:T(8,128)(2,1)S(1)} collective-permute-done((bf16[256,256]{1,0:T(8,128)(2,1)S(1)}, bf16[256,256]{1,0:T(8,128)(2,1)S(1)}, u32[]{:S(2)}, u32[]{:S(2)}) %collective-permute-start.2) | collective-permute-done | bytes 131104 | tf_op jit(solution)/shard_map/ppermute | solution.py:21
  59.5 0.6 update_early.1.rhs_ref
  60.1 0.0 collective-permute-done.4.rest_2_
  60.1 0.0 collective-permute-done.3.rest_0_
  60.2 0.1 add_add_fusion.rest_4_
  60.3 1.5 %collective-permute-start.6 = (bf16[256,256]{1,0:T(8,128)(2,1)S(1)}, bf16[256,256]{1,0:T(8,128)(2,1)S(1)}, u32[]{:S(2)}, u32[]{:S(2)}) collective-permute-start(bf16[256,256]{1,0:T(8,128)(2,1)S(1)} %slice.66), channel_id=1, source_target_pairs={{0,32},{32,0},{1,33},{33,1},{2,34},{34,2},{3,35},{35,3},{4,36},{36... | collective-permute-start | bytes 393224 | tf_op jit(solution)/shard_map/ppermute | solution.py:21
  61.8 0.1 collective-permute-start.5
  61.9 0.4 collective-permute-start.7
  62.3 0.5 collective-permute-done.6.rest_3_
  62.7 0.4 collective-permute-done.5.rest_1_
  63.1 0.2 collective-permute-done.7.rest_5_
  63.3 0.0 copy-done.1
  63.3 1.5 %update_late.1 = (f32[2,512,128]{2,1,0:T(8,128)}, f32[256,128]{1,0:T(8,128)}, f32[16,128]{1,0:T(8,128)}) custom-call(bf16[2,512,2048]{2,1,0:T(8,128)(2,1)S(1)} %copy-done.1, f32[2,512,128]{2,1,0:T(8,128)S(1)} %update_early.1.rhs_ref, bf16[512,256]{1,0:T(8,128)(2,1)S(1)} %collective-permute-done.3.rest_0_, ...), custom_call_target="tpu_custom_call" | custom-call | flops 536870912 | bytes 2097152 | tf_op jit(solution)/shard_map/update_late/pallas_call | solution.py:166
  (9 shorter events, 0.2 us)
Async XLA Ops:
  0.6 53.0 %copy-start.2 = (f32[2,512,128]{2,1,0:T(8,128)S(1)}, f32[2,512,128]{2,1,0:T(8,128)}, u32[]{:S(2)}) copy-start(f32[2,512,128]{2,1,0:T(8,128)} %rhs_ref.1) | copy-start | bytes 1572868
  3.1 25.7 %all-to-all-start = ((f32[32,24,128]{2,1,0:T(8,128)}), f32[32,24,128]{2,1,0:T(8,128)S(1)}, u32[]{:S(2)}, u32[]{:S(2)}) async-start(f32[32,24,128]{2,1,0:T(8,128)} %partials.1), calls=%async_computation | async-start | bytes 786432 | tf_op jit(solution)/shard_map/all_to_all | solution.py:188
  45.2 11.0 %collective-permute-start = (bf16[512,256]{1,0:T(8,128)(2,1)S(1)}, bf16[512,256]{1,0:T(8,128)(2,1)S(1)}, u32[]{:S(2)}, u32[]{:S(2)}) collective-permute-start(bf16[512,256]{1,0:T(8,128)(2,1)S(1)} %maximum_maximum_fusion), channel_id=1, source_target_pairs={{0,128},{32,160},{64,192},{96,224},{128,0},{160,32},{192,64},{224,... | collective-permute-start | bytes 786440 | tf_op jit(solution)/shard_map/ppermute | solution.py:26
  48.2 11.9 %collective-permute-start.4 = (bf16[512,256]{1,0:T(8,128)(2,1)S(1)}, bf16[512,256]{1,0:T(8,128)(2,1)S(1)}, u32[]{:S(2)}, u32[]{:S(2)}) collective-permute-start(bf16[512,256]{1,0:T(8,128)(2,1)S(1)} %maximum_maximum_fusion), channel_id=1, source_target_pairs={{0,192},{32,96},{64,128},{96,32},{128,64},{160,224},{192,0},{224,1... | collective-permute-start | bytes 786440 | tf_op jit(solution)/shard_map/ppermute | solution.py:26
  48.6 11.5 %collective-permute-start.3 = (bf16[512,256]{1,0:T(8,128)(2,1)S(1)}, bf16[512,256]{1,0:T(8,128)(2,1)S(1)}, u32[]{:S(2)}, u32[]{:S(2)}) collective-permute-start(bf16[512,256]{1,0:T(8,128)(2,1)S(1)} %maximum_maximum_fusion), channel_id=1, source_target_pairs={{0,64},{32,224},{64,0},{96,160},{128,192},{160,96},{192,128},{224,... | collective-permute-start | bytes 786440 | tf_op jit(solution)/shard_map/ppermute | solution.py:26
  49.0 9.5 %collective-permute-start.1 = (bf16[256,256]{1,0:T(8,128)(2,1)S(1)}, bf16[256,256]{1,0:T(8,128)(2,1)S(1)}, u32[]{:S(2)}, u32[]{:S(2)}) collective-permute-start(bf16[256,256]{1,0:T(8,128)(2,1)S(1)} %pad_maximum_fusion.rest_0_), channel_id=1, source_target_pairs={{0,32},{32,0},{1,33},{33,1},{2,34},{34,2},{3,35},{35,3},{4,36},{36... | collective-permute-start | bytes 393224 | tf_op jit(solution)/shard_map/ppermute | solution.py:21
  53.7 2.2 %copy-start = (bf16[2,512,2048]{2,1,0:T(8,128)(2,1)S(1)}, bf16[2,512,2048]{2,1,0:T(8,128)(2,1)}, u32[]{:S(2)}) copy-start(bf16[2,512,2048]{2,1,0:T(8,128)(2,1)} %factor_ref.5) | copy-start | bytes 12582916
  56.2 7.1 %copy-start.1 = (bf16[2,512,2048]{2,1,0:T(8,128)(2,1)S(1)}, bf16[2,512,2048]{2,1,0:T(8,128)(2,1)}, u32[]{:S(2)}) copy-start(bf16[2,512,2048]{2,1,0:T(8,128)(2,1)} %factor_ref.5) | copy-start | bytes 12582916
  56.2 3.3 %collective-permute-start.2 = (bf16[256,256]{1,0:T(8,128)(2,1)S(1)}, bf16[256,256]{1,0:T(8,128)(2,1)S(1)}, u32[]{:S(2)}, u32[]{:S(2)}) collective-permute-start(bf16[256,256]{1,0:T(8,128)(2,1)S(1)} %slice.64), channel_id=1, source_target_pairs={{0,32},{32,0},{1,33},{33,1},{2,34},{34,2},{3,35},{35,3},{4,36},{36... | collective-permute-start | bytes 393224 | tf_op jit(solution)/shard_map/ppermute | solution.py:21
  60.3 2.5 %collective-permute-start.6 = (bf16[256,256]{1,0:T(8,128)(2,1)S(1)}, bf16[256,256]{1,0:T(8,128)(2,1)S(1)}, u32[]{:S(2)}, u32[]{:S(2)}) collective-permute-start(bf16[256,256]{1,0:T(8,128)(2,1)S(1)} %slice.66), channel_id=1, source_target_pairs={{0,32},{32,0},{1,33},{33,1},{2,34},{34,2},{3,35},{35,3},{4,36},{36... | collective-permute-start | bytes 393224 | tf_op jit(solution)/shard_map/ppermute | solution.py:21
  61.8 1.3 %collective-permute-start.5 = (bf16[256,256]{1,0:T(8,128)(2,1)S(1)}, bf16[256,256]{1,0:T(8,128)(2,1)S(1)}, u32[]{:S(2)}, u32[]{:S(2)}) collective-permute-start(bf16[256,256]{1,0:T(8,128)(2,1)S(1)} %slice.65), channel_id=1, source_target_pairs={{0,32},{32,0},{1,33},{33,1},{2,34},{34,2},{3,35},{35,3},{4,36},{36... | collective-permute-start | bytes 393224 | tf_op jit(solution)/shard_map/ppermute | solution.py:21
  61.9 1.4 %collective-permute-start.7 = (f32[256,128]{1,0:T(8,128)S(1)}, f32[256,128]{1,0:T(8,128)S(1)}, u32[]{:S(2)}, u32[]{:S(2)}) collective-permute-start(f32[256,128]{1,0:T(8,128)S(1)} %add_add_fusion.rest_4_), channel_id=1, source_target_pairs={{0,32},{32,0},{1,33},{33,1},{2,34},{34,2},{3,35},{35,3},{4,36},{36... | collective-permute-start | bytes 393224 | tf_op jit(solution)/shard_map/ppermute | solution.py:21
